TPU v7x, 256 devices: a whole 4x4x8 slice. The times are simulated.
256 devices in a mesh: ctx: 32 (over z_hi, y, core), head: 8 (over x, z_lo).
Axes of the slice: x: 4, y: 4, z: 8 (z_hi: 4, z_lo: 2; z = z_hi * 2 + z_lo), core: 2. Of those that a mesh axis runs over, the one named last changes fastest.
Arguments:
- query_set: bfloat16 [3, 8192, 2048], P(None, ('ctx', 'head')), may hold values from -80 to 80
- key_set: bfloat16 [3, 8192, 2048], P(None, ('ctx', 'head')), may hold values from -80 to 80
- value_set: bfloat16 [3, 8192, 2048], P(None, ('ctx', 'head')), may hold values from -6 to 6
- block_order: int32 [64], replicated, may hold values from 0 to 63, each once
- documents: int32 [8192], replicated, may hold values from 0 to 3, as said below
Outputs:
- attended: bfloat16 [3, 8192, 2048], P(None, ('ctx', 'head'))
Inputs may be any that keep to these rules, and one draw needn't show every extreme that they name: `block_order`: a permutation. Never falling along the sequence; four documents, each non-empty.
All inputs are finite; a program needn't handle non-finite values.
Results may differ from a plain program's by a relative error of at most 0.013.
Values may be sent and summed in bfloat16 or wider, within the bound.
No kernel may reach another device: no remote copies, remote signals or barrier semaphores. Data moves between devices by JAX's collectives and lax.ppermute only.
A program may use at most 192 MiB of HBM per device.

v0:
```python
import jax
import jax.numpy as jnp
from jax import lax
from jax.sharding import PartitionSpec as P

HD = 128


def shifted(block, axis, distance):
    devices = range(lax.axis_size(axis))
    route = [((i - distance) % len(devices), i) for i in devices]
    return lax.ppermute(block, axis, route)


def locate(order, docs, first, count, half):
    rows = first + jnp.arange(count, dtype=jnp.int32)
    where_pos = jnp.take(order, rows // half) * half + rows % half
    return (where_pos, jnp.take(docs, where_pos))


def shards(query_set, key_set, value_set, block_order, documents):
    queries, keys_here, values_here = (
        lax.all_to_all(query_set, "head", split_axis=2, concat_axis=1, tiled=True),
        lax.all_to_all(key_set, "head", split_axis=2, concat_axis=1, tiled=True),
        lax.all_to_all(value_set, "head", split_axis=2, concat_axis=1, tiled=True),
    )
    n_ctx = lax.axis_size("ctx")
    mine = lax.axis_index("ctx")
    rows = queries.shape[1]
    feats = queries.shape[2]
    heads = feats // HD
    half = rows // 2
    scale = 1.0 / HD**0.5
    local_kv = jnp.concatenate([keys_here, values_here], 0)
    q_pos, q_doc = locate(block_order, documents, mine * rows, rows, half)
    qsplit = queries.reshape(3, rows, heads, HD)
    start_state = (
        jnp.full((heads, rows), -1e30, jnp.float32),
        jnp.zeros((heads, rows), jnp.float32),
        jnp.zeros((2, heads, rows), jnp.float32),
        jnp.zeros((heads, rows, HD), jnp.float32),
        jnp.zeros((2, heads, rows, HD), jnp.float32),
    )

    def update(state, piece, first):
        count = piece.shape[1]
        k_pos, k_doc = locate(block_order, documents, first, count, half)
        visible = (k_pos[None, :] <= q_pos[:, None]) & (k_doc[None, :] == q_doc[:, None])
        top, total, cterms, numer, grads = state
        ksplit = piece.reshape(6, count, heads, HD)
        scores = (
            jnp.einsum("qhd,khd->hqk", qsplit[0], ksplit[0], preferred_element_type=jnp.float32)
            * scale
        )
        masked = jnp.where(visible[None], scores, -1e30)
        new_top = jnp.maximum(top, jnp.max(masked, axis=2))
        shrink = jnp.exp(top - new_top)
        expo = jnp.where(visible[None], jnp.exp(masked - new_top[:, :, None]), 0.0)
        total = total * shrink + jnp.sum(expo, axis=2)
        rounded = expo.astype(jnp.bfloat16)
        numer = numer * shrink[:, :, None] + jnp.einsum(
            "hqk,khd->hqd", rounded, ksplit[3], preferred_element_type=jnp.float32
        )
        new_c = []
        new_g = []
        for idx in (1, 2):
            dscore = (
                jnp.einsum(
                    "qhd,khd->hqk", qsplit[idx], ksplit[0], preferred_element_type=jnp.float32
                )
                + jnp.einsum(
                    "qhd,khd->hqk", qsplit[0], ksplit[idx], preferred_element_type=jnp.float32
                )
            ) * scale
            weighted = expo * dscore
            new_c.append(cterms[idx - 1] * shrink + jnp.sum(weighted, axis=2))
            grad = jnp.einsum(
                "hqk,khd->hqd",
                weighted.astype(jnp.bfloat16),
                ksplit[3],
                preferred_element_type=jnp.float32,
            )
            grad = grad + jnp.einsum(
                "hqk,khd->hqd", rounded, ksplit[3 + idx], preferred_element_type=jnp.float32
            )
            new_g.append(grads[idx - 1] * shrink[:, :, None] + grad)
        return (new_top, total, jnp.stack(new_c, 0), numer, jnp.stack(new_g, 0))

    state = update(start_state, local_kv, mine * rows)

    def turn(step, carried):
        buffer, inner = carried
        buffer = shifted(buffer, "ctx", 1)
        source = (mine - step) % n_ctx
        return (buffer, update(inner, buffer, source * rows))

    ignored, state = lax.fori_loop(1, n_ctx, turn, (local_kv, state))
    top, total, cterms, numer, grads = state
    primal = numer / total[:, :, None]
    pieces = [primal]
    for idx in (0, 1):
        pieces.append(grads[idx] / total[:, :, None] - (cterms[idx] / total)[:, :, None] * primal)
    stacked = jnp.stack(pieces, 0)
    stacked = jnp.transpose(stacked, (0, 2, 1, 3)).reshape(3, rows, feats).astype(jnp.bfloat16)
    return lax.all_to_all(stacked, "head", split_axis=1, concat_axis=2, tiled=True)


def solution(mesh):
    return jax.shard_map(
        shards,
        mesh=mesh,
        in_specs=(
            P(None, ("ctx", "head"), None),
            P(None, ("ctx", "head"), None),
            P(None, ("ctx", "head"), None),
            P(),
            P(),
        ),
        out_specs=P(None, ("ctx", "head"), None),
        check_vma=False,
    )
```

profile of v0, /device:TPU:128, one launch (start us, length us, event | category | flops | bytes accessed | tf_op | source)
XLA Modules:
  0.0 802.8 jit_solution(4630368966705246820)
XLA Ops:
  60.1 718.7 %while.26 = (s32[]{:T(128)}, bf16[6,256,256]{1,2,0:T(8,128)(2,1)S(1)}, f32[2,256]{1,0:T(2,128)S(1)}, f32[2,256]{1,0:T(2,128)S(1)}, f32[2,2,256]{2,1,0:T(2,128)S(...) while((s32[]{:T(128)}, ...), condition=%wide.region_9.12_spmd, body=%wide.region_4.11_spmd.sunk | while | flops 339168768 | bytes 18640216 | solution.py:97
  63.9 20.2 %collective-permute-done = bf16[6,256,256]{1,2,0:T(8,128)(2,1)S(1)} collective-permute-done((bf16[6,256,256]{1,2,0:T(8,128)(2,1)S(1)}, bf16[6,256,256]{1,2,0:T(8,128)(2,1)S(1)}, u32[]{:S(2)}, u32[]{:S(2)}) %collective-permute-start) | collective-permute-done | bytes 786464 | tf_op jit(solution)/shard_map/while/body/eval_jaxpr/ppermute | solution.py:12
  91.5 18.0 %collective-permute-done = bf16[6,256,256]{1,2,0:T(8,128)(2,1)S(1)} collective-permute-done((bf16[6,256,256]{1,2,0:T(8,128)(2,1)S(1)}, bf16[6,256,256]{1,2,0:T(8,128)(2,1)S(1)}, u32[]{:S(2)}, u32[]{:S(2)}) %collective-permute-start) | collective-permute-done | bytes 786464 | tf_op jit(solution)/shard_map/while/body/eval_jaxpr/ppermute | solution.py:12
  116.9 12.2 %collective-permute-done = bf16[6,256,256]{1,2,0:T(8,128)(2,1)S(1)} collective-permute-done((bf16[6,256,256]{1,2,0:T(8,128)(2,1)S(1)}, bf16[6,256,256]{1,2,0:T(8,128)(2,1)S(1)}, u32[]{:S(2)}, u32[]{:S(2)}) %collective-permute-start) | collective-permute-done | bytes 786464 | tf_op jit(solution)/shard_map/while/body/eval_jaxpr/ppermute | solution.py:12
  136.5 11.8 %collective-permute-done = bf16[6,256,256]{1,2,0:T(8,128)(2,1)S(1)} collective-permute-done((bf16[6,256,256]{1,2,0:T(8,128)(2,1)S(1)}, bf16[6,256,256]{1,2,0:T(8,128)(2,1)S(1)}, u32[]{:S(2)}, u32[]{:S(2)}) %collective-permute-start) | collective-permute-done | bytes 786464 | tf_op jit(solution)/shard_map/while/body/eval_jaxpr/ppermute | solution.py:12
  155.6 11.9 %collective-permute-done = bf16[6,256,256]{1,2,0:T(8,128)(2,1)S(1)} collective-permute-done((bf16[6,256,256]{1,2,0:T(8,128)(2,1)S(1)}, bf16[6,256,256]{1,2,0:T(8,128)(2,1)S(1)}, u32[]{:S(2)}, u32[]{:S(2)}) %collective-permute-start) | collective-permute-done | bytes 786464 | tf_op jit(solution)/shard_map/while/body/eval_jaxpr/ppermute | solution.py:12
  174.8 11.9 %collective-permute-done = bf16[6,256,256]{1,2,0:T(8,128)(2,1)S(1)} collective-permute-done((bf16[6,256,256]{1,2,0:T(8,128)(2,1)S(1)}, bf16[6,256,256]{1,2,0:T(8,128)(2,1)S(1)}, u32[]{:S(2)}, u32[]{:S(2)}) %collective-permute-start) | collective-permute-done | bytes 786464 | tf_op jit(solution)/shard_map/while/body/eval_jaxpr/ppermute | solution.py:12
  213.2 12.3 %collective-permute-done = bf16[6,256,256]{1,2,0:T(8,128)(2,1)S(1)} collective-permute-done((bf16[6,256,256]{1,2,0:T(8,128)(2,1)S(1)}, bf16[6,256,256]{1,2,0:T(8,128)(2,1)S(1)}, u32[]{:S(2)}, u32[]{:S(2)}) %collective-permute-start) | collective-permute-done | bytes 786464 | tf_op jit(solution)/shard_map/while/body/eval_jaxpr/ppermute | solution.py:12
  232.9 14.3 %collective-permute-done = bf16[6,256,256]{1,2,0:T(8,128)(2,1)S(1)} collective-permute-done((bf16[6,256,256]{1,2,0:T(8,128)(2,1)S(1)}, bf16[6,256,256]{1,2,0:T(8,128)(2,1)S(1)}, u32[]{:S(2)}, u32[]{:S(2)}) %collective-permute-start) | collective-permute-done | bytes 786464 | tf_op jit(solution)/shard_map/while/body/eval_jaxpr/ppermute | solution.py:12
  254.5 20.2 %collective-permute-done = bf16[6,256,256]{1,2,0:T(8,128)(2,1)S(1)} collective-permute-done((bf16[6,256,256]{1,2,0:T(8,128)(2,1)S(1)}, bf16[6,256,256]{1,2,0:T(8,128)(2,1)S(1)}, u32[]{:S(2)}, u32[]{:S(2)}) %collective-permute-start) | collective-permute-done | bytes 786464 | tf_op jit(solution)/shard_map/while/body/eval_jaxpr/ppermute | solution.py:12
  282.1 15.7 %collective-permute-done = bf16[6,256,256]{1,2,0:T(8,128)(2,1)S(1)} collective-permute-done((bf16[6,256,256]{1,2,0:T(8,128)(2,1)S(1)}, bf16[6,256,256]{1,2,0:T(8,128)(2,1)S(1)}, u32[]{:S(2)}, u32[]{:S(2)}) %collective-permute-start) | collective-permute-done | bytes 786464 | tf_op jit(solution)/shard_map/while/body/eval_jaxpr/ppermute | solution.py:12
  305.1 14.2 %collective-permute-done = bf16[6,256,256]{1,2,0:T(8,128)(2,1)S(1)} collective-permute-done((bf16[6,256,256]{1,2,0:T(8,128)(2,1)S(1)}, bf16[6,256,256]{1,2,0:T(8,128)(2,1)S(1)}, u32[]{:S(2)}, u32[]{:S(2)}) %collective-permute-start) | collective-permute-done | bytes 786464 | tf_op jit(solution)/shard_map/while/body/eval_jaxpr/ppermute | solution.py:12
  326.7 15.4 %collective-permute-done = bf16[6,256,256]{1,2,0:T(8,128)(2,1)S(1)} collective-permute-done((bf16[6,256,256]{1,2,0:T(8,128)(2,1)S(1)}, bf16[6,256,256]{1,2,0:T(8,128)(2,1)S(1)}, u32[]{:S(2)}, u32[]{:S(2)}) %collective-permute-start) | collective-permute-done | bytes 786464 | tf_op jit(solution)/shard_map/while/body/eval_jaxpr/ppermute | solution.py:12
  349.4 17.4 %collective-permute-done = bf16[6,256,256]{1,2,0:T(8,128)(2,1)S(1)} collective-permute-done((bf16[6,256,256]{1,2,0:T(8,128)(2,1)S(1)}, bf16[6,256,256]{1,2,0:T(8,128)(2,1)S(1)}, u32[]{:S(2)}, u32[]{:S(2)}) %collective-permute-start) | collective-permute-done | bytes 786464 | tf_op jit(solution)/shard_map/while/body/eval_jaxpr/ppermute | solution.py:12
  374.2 17.3 %collective-permute-done = bf16[6,256,256]{1,2,0:T(8,128)(2,1)S(1)} collective-permute-done((bf16[6,256,256]{1,2,0:T(8,128)(2,1)S(1)}, bf16[6,256,256]{1,2,0:T(8,128)(2,1)S(1)}, u32[]{:S(2)}, u32[]{:S(2)}) %collective-permute-start) | collective-permute-done | bytes 786464 | tf_op jit(solution)/shard_map/while/body/eval_jaxpr/ppermute | solution.py:12
  398.9 15.4 %collective-permute-done = bf16[6,256,256]{1,2,0:T(8,128)(2,1)S(1)} collective-permute-done((bf16[6,256,256]{1,2,0:T(8,128)(2,1)S(1)}, bf16[6,256,256]{1,2,0:T(8,128)(2,1)S(1)}, u32[]{:S(2)}, u32[]{:S(2)}) %collective-permute-start) | collective-permute-done | bytes 786464 | tf_op jit(solution)/shard_map/while/body/eval_jaxpr/ppermute | solution.py:12
  421.7 17.4 %collective-permute-done = bf16[6,256,256]{1,2,0:T(8,128)(2,1)S(1)} collective-permute-done((bf16[6,256,256]{1,2,0:T(8,128)(2,1)S(1)}, bf16[6,256,256]{1,2,0:T(8,128)(2,1)S(1)}, u32[]{:S(2)}, u32[]{:S(2)}) %collective-permute-start) | collective-permute-done | bytes 786464 | tf_op jit(solution)/shard_map/while/body/eval_jaxpr/ppermute | solution.py:12
  446.5 17.3 %collective-permute-done = bf16[6,256,256]{1,2,0:T(8,128)(2,1)S(1)} collective-permute-done((bf16[6,256,256]{1,2,0:T(8,128)(2,1)S(1)}, bf16[6,256,256]{1,2,0:T(8,128)(2,1)S(1)}, u32[]{:S(2)}, u32[]{:S(2)}) %collective-permute-start) | collective-permute-done | bytes 786464 | tf_op jit(solution)/shard_map/while/body/eval_jaxpr/ppermute | solution.py:12
  471.1 15.4 %collective-permute-done = bf16[6,256,256]{1,2,0:T(8,128)(2,1)S(1)} collective-permute-done((bf16[6,256,256]{1,2,0:T(8,128)(2,1)S(1)}, bf16[6,256,256]{1,2,0:T(8,128)(2,1)S(1)}, u32[]{:S(2)}, u32[]{:S(2)}) %collective-permute-start) | collective-permute-done | bytes 786464 | tf_op jit(solution)/shard_map/while/body/eval_jaxpr/ppermute | solution.py:12
  493.9 17.4 %collective-permute-done = bf16[6,256,256]{1,2,0:T(8,128)(2,1)S(1)} collective-permute-done((bf16[6,256,256]{1,2,0:T(8,128)(2,1)S(1)}, bf16[6,256,256]{1,2,0:T(8,128)(2,1)S(1)}, u32[]{:S(2)}, u32[]{:S(2)}) %collective-permute-start) | collective-permute-done | bytes 786464 | tf_op jit(solution)/shard_map/while/body/eval_jaxpr/ppermute | solution.py:12
  518.7 17.3 %collective-permute-done = bf16[6,256,256]{1,2,0:T(8,128)(2,1)S(1)} collective-permute-done((bf16[6,256,256]{1,2,0:T(8,128)(2,1)S(1)}, bf16[6,256,256]{1,2,0:T(8,128)(2,1)S(1)}, u32[]{:S(2)}, u32[]{:S(2)}) %collective-permute-start) | collective-permute-done | bytes 786464 | tf_op jit(solution)/shard_map/while/body/eval_jaxpr/ppermute | solution.py:12
  543.4 15.4 %collective-permute-done = bf16[6,256,256]{1,2,0:T(8,128)(2,1)S(1)} collective-permute-done((bf16[6,256,256]{1,2,0:T(8,128)(2,1)S(1)}, bf16[6,256,256]{1,2,0:T(8,128)(2,1)S(1)}, u32[]{:S(2)}, u32[]{:S(2)}) %collective-permute-start) | collective-permute-done | bytes 786464 | tf_op jit(solution)/shard_map/while/body/eval_jaxpr/ppermute | solution.py:12
  566.1 17.4 %collective-permute-done = bf16[6,256,256]{1,2,0:T(8,128)(2,1)S(1)} collective-permute-done((bf16[6,256,256]{1,2,0:T(8,128)(2,1)S(1)}, bf16[6,256,256]{1,2,0:T(8,128)(2,1)S(1)}, u32[]{:S(2)}, u32[]{:S(2)}) %collective-permute-start) | collective-permute-done | bytes 786464 | tf_op jit(solution)/shard_map/while/body/eval_jaxpr/ppermute | solution.py:12
  590.9 17.3 %collective-permute-done = bf16[6,256,256]{1,2,0:T(8,128)(2,1)S(1)} collective-permute-done((bf16[6,256,256]{1,2,0:T(8,128)(2,1)S(1)}, bf16[6,256,256]{1,2,0:T(8,128)(2,1)S(1)}, u32[]{:S(2)}, u32[]{:S(2)}) %collective-permute-start) | collective-permute-done | bytes 786464 | tf_op jit(solution)/shard_map/while/body/eval_jaxpr/ppermute | solution.py:12
  615.6 15.4 %collective-permute-done = bf16[6,256,256]{1,2,0:T(8,128)(2,1)S(1)} collective-permute-done((bf16[6,256,256]{1,2,0:T(8,128)(2,1)S(1)}, bf16[6,256,256]{1,2,0:T(8,128)(2,1)S(1)}, u32[]{:S(2)}, u32[]{:S(2)}) %collective-permute-start) | collective-permute-done | bytes 786464 | tf_op jit(solution)/shard_map/while/body/eval_jaxpr/ppermute | solution.py:12
  638.3 17.4 %collective-permute-done = bf16[6,256,256]{1,2,0:T(8,128)(2,1)S(1)} collective-permute-done((bf16[6,256,256]{1,2,0:T(8,128)(2,1)S(1)}, bf16[6,256,256]{1,2,0:T(8,128)(2,1)S(1)}, u32[]{:S(2)}, u32[]{:S(2)}) %collective-permute-start) | collective-permute-done | bytes 786464 | tf_op jit(solution)/shard_map/while/body/eval_jaxpr/ppermute | solution.py:12
  663.1 17.3 %collective-permute-done = bf16[6,256,256]{1,2,0:T(8,128)(2,1)S(1)} collective-permute-done((bf16[6,256,256]{1,2,0:T(8,128)(2,1)S(1)}, bf16[6,256,256]{1,2,0:T(8,128)(2,1)S(1)}, u32[]{:S(2)}, u32[]{:S(2)}) %collective-permute-start) | collective-permute-done | bytes 786464 | tf_op jit(solution)/shard_map/while/body/eval_jaxpr/ppermute | solution.py:12
  687.8 15.4 %collective-permute-done = bf16[6,256,256]{1,2,0:T(8,128)(2,1)S(1)} collective-permute-done((bf16[6,256,256]{1,2,0:T(8,128)(2,1)S(1)}, bf16[6,256,256]{1,2,0:T(8,128)(2,1)S(1)}, u32[]{:S(2)}, u32[]{:S(2)}) %collective-permute-start) | collective-permute-done | bytes 786464 | tf_op jit(solution)/shard_map/while/body/eval_jaxpr/ppermute | solution.py:12
  710.5 17.4 %collective-permute-done = bf16[6,256,256]{1,2,0:T(8,128)(2,1)S(1)} collective-permute-done((bf16[6,256,256]{1,2,0:T(8,128)(2,1)S(1)}, bf16[6,256,256]{1,2,0:T(8,128)(2,1)S(1)}, u32[]{:S(2)}, u32[]{:S(2)}) %collective-permute-start) | collective-permute-done | bytes 786464 | tf_op jit(solution)/shard_map/while/body/eval_jaxpr/ppermute | solution.py:12
  735.3 17.3 %collective-permute-done = bf16[6,256,256]{1,2,0:T(8,128)(2,1)S(1)} collective-permute-done((bf16[6,256,256]{1,2,0:T(8,128)(2,1)S(1)}, bf16[6,256,256]{1,2,0:T(8,128)(2,1)S(1)}, u32[]{:S(2)}, u32[]{:S(2)}) %collective-permute-start) | collective-permute-done | bytes 786464 | tf_op jit(solution)/shard_map/while/body/eval_jaxpr/ppermute | solution.py:12
  760.0 15.4 %collective-permute-done = bf16[6,256,256]{1,2,0:T(8,128)(2,1)S(1)} collective-permute-done((bf16[6,256,256]{1,2,0:T(8,128)(2,1)S(1)}, bf16[6,256,256]{1,2,0:T(8,128)(2,1)S(1)}, u32[]{:S(2)}, u32[]{:S(2)}) %collective-permute-start) | collective-permute-done | bytes 786464 | tf_op jit(solution)/shard_map/while/body/eval_jaxpr/ppermute | solution.py:12
  779.6 22.4 %all_to_all.69 = bf16[3,256,256]{2,0,1:T(4,128)(2,1)S(1)} all-to-all(bf16[3,256,256]{2,0,1:T(4,128)(2,1)S(1)} %copy.211), channel_id=1, replica_groups=mesh['ctx'=32,'head'=8] {'head'}, dimensions={1} | all-to-all | bytes 786432 | tf_op jit(solution)/shard_map/all_to_all | solution.py:105
  (962 shorter events, 295.2 us)
Async XLA Ops:
  30.1 13.6 %all-to-all-start.1 = ((bf16[8,2,12288]{2,1,0:T(2,128)(2,1)}), bf16[8,2,12288]{2,1,0:T(2,128)(2,1)S(1)}, u32[]{:S(2)}, u32[]{:S(2)}) async-start(bf16[8,2,12288]{2,1,0:T(2,128)(2,1)} %reshape.272), calls=%async_computation.1 | async-start | bytes 786432 | tf_op jit(solution)/shard_map/all_to_all | solution.py:25
  60.1 24.1 %collective-permute-start = (bf16[6,256,256]{1,2,0:T(8,128)(2,1)S(1)}, bf16[6,256,256]{1,2,0:T(8,128)(2,1)S(1)}, u32[]{:S(2)}, u32[]{:S(2)}) collective-permute-start(bf16[6,256,256]{1,2,0:T(8,128)(2,1)S(1)} %get-tuple-element.638), channel_id=1, source_target_pairs={{248,0},{0,8},{8,16},{16,24},{24,32},{32,40},{40,48},{48,56},{56,6... | collective-permute-start | bytes 2359304 | tf_op jit(solution)/shard_map/while/body/eval_jaxpr/ppermute | solution.py:12
  87.6 22.0 %collective-permute-start = (bf16[6,256,256]{1,2,0:T(8,128)(2,1)S(1)}, bf16[6,256,256]{1,2,0:T(8,128)(2,1)S(1)}, u32[]{:S(2)}, u32[]{:S(2)}) collective-permute-start(bf16[6,256,256]{1,2,0:T(8,128)(2,1)S(1)} %get-tuple-element.638), channel_id=1, source_target_pairs={{248,0},{0,8},{8,16},{16,24},{24,32},{32,40},{40,48},{48,56},{56,6... | collective-permute-start | bytes 2359304 | tf_op jit(solution)/shard_map/while/body/eval_jaxpr/ppermute | solution.py:12
  113.0 16.1 %collective-permute-start = (bf16[6,256,256]{1,2,0:T(8,128)(2,1)S(1)}, bf16[6,256,256]{1,2,0:T(8,128)(2,1)S(1)}, u32[]{:S(2)}, u32[]{:S(2)}) collective-permute-start(bf16[6,256,256]{1,2,0:T(8,128)(2,1)S(1)} %get-tuple-element.638), channel_id=1, source_target_pairs={{248,0},{0,8},{8,16},{16,24},{24,32},{32,40},{40,48},{48,56},{56,6... | collective-permute-start | bytes 2359304 | tf_op jit(solution)/shard_map/while/body/eval_jaxpr/ppermute | solution.py:12
  132.5 15.7 %collective-permute-start = (bf16[6,256,256]{1,2,0:T(8,128)(2,1)S(1)}, bf16[6,256,256]{1,2,0:T(8,128)(2,1)S(1)}, u32[]{:S(2)}, u32[]{:S(2)}) collective-permute-start(bf16[6,256,256]{1,2,0:T(8,128)(2,1)S(1)} %get-tuple-element.638), channel_id=1, source_target_pairs={{248,0},{0,8},{8,16},{16,24},{24,32},{32,40},{40,48},{48,56},{56,6... | collective-permute-start | bytes 2359304 | tf_op jit(solution)/shard_map/while/body/eval_jaxpr/ppermute | solution.py:12
  151.7 15.8 %collective-permute-start = (bf16[6,256,256]{1,2,0:T(8,128)(2,1)S(1)}, bf16[6,256,256]{1,2,0:T(8,128)(2,1)S(1)}, u32[]{:S(2)}, u32[]{:S(2)}) collective-permute-start(bf16[6,256,256]{1,2,0:T(8,128)(2,1)S(1)} %get-tuple-element.638), channel_id=1, source_target_pairs={{248,0},{0,8},{8,16},{16,24},{24,32},{32,40},{40,48},{48,56},{56,6... | collective-permute-start | bytes 2359304 | tf_op jit(solution)/shard_map/while/body/eval_jaxpr/ppermute | solution.py:12
  170.9 15.8 %collective-permute-start = (bf16[6,256,256]{1,2,0:T(8,128)(2,1)S(1)}, bf16[6,256,256]{1,2,0:T(8,128)(2,1)S(1)}, u32[]{:S(2)}, u32[]{:S(2)}) collective-permute-start(bf16[6,256,256]{1,2,0:T(8,128)(2,1)S(1)} %get-tuple-element.638), channel_id=1, source_target_pairs={{248,0},{0,8},{8,16},{16,24},{24,32},{32,40},{40,48},{48,56},{56,6... | collective-permute-start | bytes 2359304 | tf_op jit(solution)/shard_map/while/body/eval_jaxpr/ppermute | solution.py:12
  190.1 15.7 %collective-permute-start = (bf16[6,256,256]{1,2,0:T(8,128)(2,1)S(1)}, bf16[6,256,256]{1,2,0:T(8,128)(2,1)S(1)}, u32[]{:S(2)}, u32[]{:S(2)}) collective-permute-start(bf16[6,256,256]{1,2,0:T(8,128)(2,1)S(1)} %get-tuple-element.638), channel_id=1, source_target_pairs={{248,0},{0,8},{8,16},{16,24},{24,32},{32,40},{40,48},{48,56},{56,6... | collective-permute-start | bytes 2359304 | tf_op jit(solution)/shard_map/while/body/eval_jaxpr/ppermute | solution.py:12
  209.3 16.2 %collective-permute-start = (bf16[6,256,256]{1,2,0:T(8,128)(2,1)S(1)}, bf16[6,256,256]{1,2,0:T(8,128)(2,1)S(1)}, u32[]{:S(2)}, u32[]{:S(2)}) collective-permute-start(bf16[6,256,256]{1,2,0:T(8,128)(2,1)S(1)} %get-tuple-element.638), channel_id=1, source_target_pairs={{248,0},{0,8},{8,16},{16,24},{24,32},{32,40},{40,48},{48,56},{56,6... | collective-permute-start | bytes 2359304 | tf_op jit(solution)/shard_map/while/body/eval_jaxpr/ppermute | solution.py:12
  228.9 18.3 %collective-permute-start = (bf16[6,256,256]{1,2,0:T(8,128)(2,1)S(1)}, bf16[6,256,256]{1,2,0:T(8,128)(2,1)S(1)}, u32[]{:S(2)}, u32[]{:S(2)}) collective-permute-start(bf16[6,256,256]{1,2,0:T(8,128)(2,1)S(1)} %get-tuple-element.638), channel_id=1, source_target_pairs={{248,0},{0,8},{8,16},{16,24},{24,32},{32,40},{40,48},{48,56},{56,6... | collective-permute-start | bytes 2359304 | tf_op jit(solution)/shard_map/while/body/eval_jaxpr/ppermute | solution.py:12
  250.6 24.1 %collective-permute-start = (bf16[6,256,256]{1,2,0:T(8,128)(2,1)S(1)}, bf16[6,256,256]{1,2,0:T(8,128)(2,1)S(1)}, u32[]{:S(2)}, u32[]{:S(2)}) collective-permute-start(bf16[6,256,256]{1,2,0:T(8,128)(2,1)S(1)} %get-tuple-element.638), channel_id=1, source_target_pairs={{248,0},{0,8},{8,16},{16,24},{24,32},{32,40},{40,48},{48,56},{56,6... | collective-permute-start | bytes 2359304 | tf_op jit(solution)/shard_map/while/body/eval_jaxpr/ppermute | solution.py:12
  278.1 19.6 %collective-permute-start = (bf16[6,256,256]{1,2,0:T(8,128)(2,1)S(1)}, bf16[6,256,256]{1,2,0:T(8,128)(2,1)S(1)}, u32[]{:S(2)}, u32[]{:S(2)}) collective-permute-start(bf16[6,256,256]{1,2,0:T(8,128)(2,1)S(1)} %get-tuple-element.638), channel_id=1, source_target_pairs={{248,0},{0,8},{8,16},{16,24},{24,32},{32,40},{40,48},{48,56},{56,6... | collective-permute-start | bytes 2359304 | tf_op jit(solution)/shard_map/while/body/eval_jaxpr/ppermute | solution.py:12
  301.2 18.1 %collective-permute-start = (bf16[6,256,256]{1,2,0:T(8,128)(2,1)S(1)}, bf16[6,256,256]{1,2,0:T(8,128)(2,1)S(1)}, u32[]{:S(2)}, u32[]{:S(2)}) collective-permute-start(bf16[6,256,256]{1,2,0:T(8,128)(2,1)S(1)} %get-tuple-element.638), channel_id=1, source_target_pairs={{248,0},{0,8},{8,16},{16,24},{24,32},{32,40},{40,48},{48,56},{56,6... | collective-permute-start | bytes 2359304 | tf_op jit(solution)/shard_map/while/body/eval_jaxpr/ppermute | solution.py:12
  322.8 19.3 %collective-permute-start = (bf16[6,256,256]{1,2,0:T(8,128)(2,1)S(1)}, bf16[6,256,256]{1,2,0:T(8,128)(2,1)S(1)}, u32[]{:S(2)}, u32[]{:S(2)}) collective-permute-start(bf16[6,256,256]{1,2,0:T(8,128)(2,1)S(1)} %get-tuple-element.638), channel_id=1, source_target_pairs={{248,0},{0,8},{8,16},{16,24},{24,32},{32,40},{40,48},{48,56},{56,6... | collective-permute-start | bytes 2359304 | tf_op jit(solution)/shard_map/while/body/eval_jaxpr/ppermute | solution.py:12
  345.5 21.4 %collective-permute-start = (bf16[6,256,256]{1,2,0:T(8,128)(2,1)S(1)}, bf16[6,256,256]{1,2,0:T(8,128)(2,1)S(1)}, u32[]{:S(2)}, u32[]{:S(2)}) collective-permute-start(bf16[6,256,256]{1,2,0:T(8,128)(2,1)S(1)} %get-tuple-element.638), channel_id=1, source_target_pairs={{248,0},{0,8},{8,16},{16,24},{24,32},{32,40},{40,48},{48,56},{56,6... | collective-permute-start | bytes 2359304 | tf_op jit(solution)/shard_map/while/body/eval_jaxpr/ppermute | solution.py:12
  370.3 21.3 %collective-permute-start = (bf16[6,256,256]{1,2,0:T(8,128)(2,1)S(1)}, bf16[6,256,256]{1,2,0:T(8,128)(2,1)S(1)}, u32[]{:S(2)}, u32[]{:S(2)}) collective-permute-start(bf16[6,256,256]{1,2,0:T(8,128)(2,1)S(1)} %get-tuple-element.638), channel_id=1, source_target_pairs={{248,0},{0,8},{8,16},{16,24},{24,32},{32,40},{40,48},{48,56},{56,6... | collective-permute-start | bytes 2359304 | tf_op jit(solution)/shard_map/while/body/eval_jaxpr/ppermute | solution.py:12
  395.0 19.3 %collective-permute-start = (bf16[6,256,256]{1,2,0:T(8,128)(2,1)S(1)}, bf16[6,256,256]{1,2,0:T(8,128)(2,1)S(1)}, u32[]{:S(2)}, u32[]{:S(2)}) collective-permute-start(bf16[6,256,256]{1,2,0:T(8,128)(2,1)S(1)} %get-tuple-element.638), channel_id=1, source_target_pairs={{248,0},{0,8},{8,16},{16,24},{24,32},{32,40},{40,48},{48,56},{56,6... | collective-permute-start | bytes 2359304 | tf_op jit(solution)/shard_map/while/body/eval_jaxpr/ppermute | solution.py:12
  417.7 21.4 %collective-permute-start = (bf16[6,256,256]{1,2,0:T(8,128)(2,1)S(1)}, bf16[6,256,256]{1,2,0:T(8,128)(2,1)S(1)}, u32[]{:S(2)}, u32[]{:S(2)}) collective-permute-start(bf16[6,256,256]{1,2,0:T(8,128)(2,1)S(1)} %get-tuple-element.638), channel_id=1, source_target_pairs={{248,0},{0,8},{8,16},{16,24},{24,32},{32,40},{40,48},{48,56},{56,6... | collective-permute-start | bytes 2359304 | tf_op jit(solution)/shard_map/while/body/eval_jaxpr/ppermute | solution.py:12
  442.5 21.3 %collective-permute-start = (bf16[6,256,256]{1,2,0:T(8,128)(2,1)S(1)}, bf16[6,256,256]{1,2,0:T(8,128)(2,1)S(1)}, u32[]{:S(2)}, u32[]{:S(2)}) collective-permute-start(bf16[6,256,256]{1,2,0:T(8,128)(2,1)S(1)} %get-tuple-element.638), channel_id=1, source_target_pairs={{248,0},{0,8},{8,16},{16,24},{24,32},{32,40},{40,48},{48,56},{56,6... | collective-permute-start | bytes 2359304 | tf_op jit(solution)/shard_map/while/body/eval_jaxpr/ppermute | solution.py:12
  467.2 19.3 %collective-permute-start = (bf16[6,256,256]{1,2,0:T(8,128)(2,1)S(1)}, bf16[6,256,256]{1,2,0:T(8,128)(2,1)S(1)}, u32[]{:S(2)}, u32[]{:S(2)}) collective-permute-start(bf16[6,256,256]{1,2,0:T(8,128)(2,1)S(1)} %get-tuple-element.638), channel_id=1, source_target_pairs={{248,0},{0,8},{8,16},{16,24},{24,32},{32,40},{40,48},{48,56},{56,6... | collective-permute-start | bytes 2359304 | tf_op jit(solution)/shard_map/while/body/eval_jaxpr/ppermute | solution.py:12
  489.9 21.4 %collective-permute-start = (bf16[6,256,256]{1,2,0:T(8,128)(2,1)S(1)}, bf16[6,256,256]{1,2,0:T(8,128)(2,1)S(1)}, u32[]{:S(2)}, u32[]{:S(2)}) collective-permute-start(bf16[6,256,256]{1,2,0:T(8,128)(2,1)S(1)} %get-tuple-element.638), channel_id=1, source_target_pairs={{248,0},{0,8},{8,16},{16,24},{24,32},{32,40},{40,48},{48,56},{56,6... | collective-permute-start | bytes 2359304 | tf_op jit(solution)/shard_map/while/body/eval_jaxpr/ppermute | solution.py:12
  514.7 21.3 %collective-permute-start = (bf16[6,256,256]{1,2,0:T(8,128)(2,1)S(1)}, bf16[6,256,256]{1,2,0:T(8,128)(2,1)S(1)}, u32[]{:S(2)}, u32[]{:S(2)}) collective-permute-start(bf16[6,256,256]{1,2,0:T(8,128)(2,1)S(1)} %get-tuple-element.638), channel_id=1, source_target_pairs={{248,0},{0,8},{8,16},{16,24},{24,32},{32,40},{40,48},{48,56},{56,6... | collective-permute-start | bytes 2359304 | tf_op jit(solution)/shard_map/while/body/eval_jaxpr/ppermute | solution.py:12
  539.4 19.3 %collective-permute-start = (bf16[6,256,256]{1,2,0:T(8,128)(2,1)S(1)}, bf16[6,256,256]{1,2,0:T(8,128)(2,1)S(1)}, u32[]{:S(2)}, u32[]{:S(2)}) collective-permute-start(bf16[6,256,256]{1,2,0:T(8,128)(2,1)S(1)} %get-tuple-element.638), channel_id=1, source_target_pairs={{248,0},{0,8},{8,16},{16,24},{24,32},{32,40},{40,48},{48,56},{56,6... | collective-permute-start | bytes 2359304 | tf_op jit(solution)/shard_map/while/body/eval_jaxpr/ppermute | solution.py:12
  562.2 21.4 %collective-permute-start = (bf16[6,256,256]{1,2,0:T(8,128)(2,1)S(1)}, bf16[6,256,256]{1,2,0:T(8,128)(2,1)S(1)}, u32[]{:S(2)}, u32[]{:S(2)}) collective-permute-start(bf16[6,256,256]{1,2,0:T(8,128)(2,1)S(1)} %get-tuple-element.638), channel_id=1, source_target_pairs={{248,0},{0,8},{8,16},{16,24},{24,32},{32,40},{40,48},{48,56},{56,6... | collective-permute-start | bytes 2359304 | tf_op jit(solution)/shard_map/while/body/eval_jaxpr/ppermute | solution.py:12
  586.9 21.3 %collective-permute-start = (bf16[6,256,256]{1,2,0:T(8,128)(2,1)S(1)}, bf16[6,256,256]{1,2,0:T(8,128)(2,1)S(1)}, u32[]{:S(2)}, u32[]{:S(2)}) collective-permute-start(bf16[6,256,256]{1,2,0:T(8,128)(2,1)S(1)} %get-tuple-element.638), channel_id=1, source_target_pairs={{248,0},{0,8},{8,16},{16,24},{24,32},{32,40},{40,48},{48,56},{56,6... | collective-permute-start | bytes 2359304 | tf_op jit(solution)/shard_map/while/body/eval_jaxpr/ppermute | solution.py:12
  611.6 19.3 %collective-permute-start = (bf16[6,256,256]{1,2,0:T(8,128)(2,1)S(1)}, bf16[6,256,256]{1,2,0:T(8,128)(2,1)S(1)}, u32[]{:S(2)}, u32[]{:S(2)}) collective-permute-start(bf16[6,256,256]{1,2,0:T(8,128)(2,1)S(1)} %get-tuple-element.638), channel_id=1, source_target_pairs={{248,0},{0,8},{8,16},{16,24},{24,32},{32,40},{40,48},{48,56},{56,6... | collective-permute-start | bytes 2359304 | tf_op jit(solution)/shard_map/while/body/eval_jaxpr/ppermute | solution.py:12
  634.4 21.4 %collective-permute-start = (bf16[6,256,256]{1,2,0:T(8,128)(2,1)S(1)}, bf16[6,256,256]{1,2,0:T(8,128)(2,1)S(1)}, u32[]{:S(2)}, u32[]{:S(2)}) collective-permute-start(bf16[6,256,256]{1,2,0:T(8,128)(2,1)S(1)} %get-tuple-element.638), channel_id=1, source_target_pairs={{248,0},{0,8},{8,16},{16,24},{24,32},{32,40},{40,48},{48,56},{56,6... | collective-permute-start | bytes 2359304 | tf_op jit(solution)/shard_map/while/body/eval_jaxpr/ppermute | solution.py:12
  659.2 21.3 %collective-permute-start = (bf16[6,256,256]{1,2,0:T(8,128)(2,1)S(1)}, bf16[6,256,256]{1,2,0:T(8,128)(2,1)S(1)}, u32[]{:S(2)}, u32[]{:S(2)}) collective-permute-start(bf16[6,256,256]{1,2,0:T(8,128)(2,1)S(1)} %get-tuple-element.638), channel_id=1, source_target_pairs={{248,0},{0,8},{8,16},{16,24},{24,32},{32,40},{40,48},{48,56},{56,6... | collective-permute-start | bytes 2359304 | tf_op jit(solution)/shard_map/while/body/eval_jaxpr/ppermute | solution.py:12
  683.9 19.3 %collective-permute-start = (bf16[6,256,256]{1,2,0:T(8,128)(2,1)S(1)}, bf16[6,256,256]{1,2,0:T(8,128)(2,1)S(1)}, u32[]{:S(2)}, u32[]{:S(2)}) collective-permute-start(bf16[6,256,256]{1,2,0:T(8,128)(2,1)S(1)} %get-tuple-element.638), channel_id=1, source_target_pairs={{248,0},{0,8},{8,16},{16,24},{24,32},{32,40},{40,48},{48,56},{56,6... | collective-permute-start | bytes 2359304 | tf_op jit(solution)/shard_map/while/body/eval_jaxpr/ppermute | solution.py:12
  706.6 21.4 %collective-permute-start = (bf16[6,256,256]{1,2,0:T(8,128)(2,1)S(1)}, bf16[6,256,256]{1,2,0:T(8,128)(2,1)S(1)}, u32[]{:S(2)}, u32[]{:S(2)}) collective-permute-start(bf16[6,256,256]{1,2,0:T(8,128)(2,1)S(1)} %get-tuple-element.638), channel_id=1, source_target_pairs={{248,0},{0,8},{8,16},{16,24},{24,32},{32,40},{40,48},{48,56},{56,6... | collective-permute-start | bytes 2359304 | tf_op jit(solution)/shard_map/while/body/eval_jaxpr/ppermute | solution.py:12
  731.4 21.3 %collective-permute-start = (bf16[6,256,256]{1,2,0:T(8,128)(2,1)S(1)}, bf16[6,256,256]{1,2,0:T(8,128)(2,1)S(1)}, u32[]{:S(2)}, u32[]{:S(2)}) collective-permute-start(bf16[6,256,256]{1,2,0:T(8,128)(2,1)S(1)} %get-tuple-element.638), channel_id=1, source_target_pairs={{248,0},{0,8},{8,16},{16,24},{24,32},{32,40},{40,48},{48,56},{56,6... | collective-permute-start | bytes 2359304 | tf_op jit(solution)/shard_map/while/body/eval_jaxpr/ppermute | solution.py:12
  756.1 19.3 %collective-permute-start = (bf16[6,256,256]{1,2,0:T(8,128)(2,1)S(1)}, bf16[6,256,256]{1,2,0:T(8,128)(2,1)S(1)}, u32[]{:S(2)}, u32[]{:S(2)}) collective-permute-start(bf16[6,256,256]{1,2,0:T(8,128)(2,1)S(1)} %get-tuple-element.638), channel_id=1, source_target_pairs={{248,0},{0,8},{8,16},{16,24},{24,32},{32,40},{40,48},{48,56},{56,6... | collective-permute-start | bytes 2359304 | tf_op jit(solution)/shard_map/while/body/eval_jaxpr/ppermute | solution.py:12
  (12 other events, 70.5 us)
where the time goes:
time: 803 us
  waiting for transfers between devices  497 us (62%)
  local copies, waits for them, and re-layouts  153 us (19%)
  matrix products  95.5 us (12%)
  blocking collectives  22.4 us (3%)
  starting transfers between devices  14.4 us (2%)
  other arithmetic  13.8 us (2%)
    ppermute x31, waiting for transfers between devices, shifted(): return lax.ppermute(block, axis, route)  490 us
    gather x32, local copies, waits for them, and re-layouts, locate(): where_pos = jnp.take(order, rows // half) * half + rows % half  59.8 us
    gather x32, local copies, waits for them, and re-layouts, locate(): return (where_pos, jnp.take(docs, where_pos))  55.1 us
    all_to_all x1, blocking collectives, shards(): lax.all_to_all(stacked, 'head', split_axis=1, concat_axis=2, tiled=True)  22.4 us
    dot_general x64, matrix products, update(): jnp.einsum('qhd,khd->hqk', qsplit[idx], ksplit[0], preferred_element_type...  21.9 us
    dot_general x64, matrix products, update(): jnp.einsum('hqk,khd->hqd', weighted.astype(jnp.bfloat16), ksplit[3], pref...  18.8 us
    dot_general x64, matrix products, update(): jnp.einsum('hqk,khd->hqd', rounded, ksplit[3 + idx], preferred_element_ty...  17.5 us
    unnamed x29, local copies, waits for them, and re-layouts  17.1 us
  transfers between devices with their start and end apart: 34, of which 33 were waited for; matrix products, arithmetic and copies ran while one was open for 17% of the time, Pallas kernels for 0%

commit v1 on v0

v1 whole, which is shorter than its diff:
```python
import jax
import jax.numpy as jnp
from jax import lax
from jax.experimental import pallas as pl
from jax.experimental.pallas import tpu as pltpu
from jax.sharding import Mesh
from jax.sharding import PartitionSpec as P

HD = 128
HEADS = 16
BLOCK = 128
SLICE = 32
Z = ("zh", "zl")
XY = ("y", "xh", "xl")
NAMES = ("zh", "y", "c", "xh", "xl", "zl")
SIZES = (4, 4, 2, 2, 2, 2)
NZ = 8
SCALE = 1.0 / HD**0.5
LOG2E = 1.4426950408889634
HIDDEN = -1e30
VMEM = pl.BlockSpec(memory_space=pltpu.VMEM)
SMEM = pl.BlockSpec(memory_space=pltpu.SMEM)
ANY = pl.BlockSpec(memory_space=pl.ANY)

KRANK = 0
KPOS = 32
QRANK = 64
QPOS = 80
QINDEX = 96
KLO = 112
KHI = 120
STARTS = 128
ZPOS = 131
ZLOW = 132
N_SCALARS = 133

QT = 128
KT = 256


def split_heads(*arrays):
    def kernel(*refs):
        out = refs[-1]
        for h in range(HEADS):
            for a, ref in enumerate(refs[:-1]):
                out[h, 3 * a : 3 * a + 3] = ref[:, :, h * HD : (h + 1) * HD]

    return pl.pallas_call(
        kernel,
        out_shape=jax.ShapeDtypeStruct((HEADS, 3 * len(arrays), SLICE, HD), jnp.bfloat16),
        in_specs=[VMEM] * len(arrays),
        out_specs=VMEM,
    )(*arrays)


def join_heads(parts):
    def kernel(ref, out):
        for h in range(HEADS):
            out[:, :, h * HD : (h + 1) * HD] = ref[h]

    return pl.pallas_call(
        kernel,
        out_shape=jax.ShapeDtypeStruct((3, SLICE, HEADS * HD), jnp.bfloat16),
        in_specs=[VMEM],
        out_specs=VMEM,
    )(parts)


def ranks(values):
    n = values.shape[0]
    order = jnp.sum((values[None, :] < values[:, None]).astype(jnp.int32), axis=1)
    hits = order[None, :] == jnp.arange(n, dtype=jnp.int32)[:, None]
    index = jnp.sum(jnp.where(hits, jnp.arange(n, dtype=jnp.int32)[None, :], 0), axis=1)
    ordered = jnp.sum(jnp.where(hits, values[None, :], 0), axis=1)
    return order, index, ordered


def scalars(order, documents):
    zh, zl, c = lax.axis_index("zh"), lax.axis_index("zl"), lax.axis_index("c")
    blocks = order.reshape(4, 4, 2, 2)
    mine = lax.dynamic_index_in_dim(blocks, c, 2, keepdims=False)
    here = lax.dynamic_index_in_dim(blocks, zh, 0, keepdims=False)
    own = lax.dynamic_index_in_dim(here, c, 1, keepdims=False).reshape(-1)
    other = lax.dynamic_index_in_dim(here, 1 - c, 1, keepdims=False).reshape(-1)
    krank, _, kpos = ranks(mine.reshape(-1))
    qrank, qindex, qpos = ranks(jnp.concatenate([own, other]))
    starts = jnp.sum(
        (documents[None, :] < jnp.arange(1, 4, dtype=jnp.int32)[:, None]).astype(jnp.int32), axis=1
    )
    first = qpos[0::2] * BLOCK
    last = qpos[1::2] * BLOCK + BLOCK - 1
    begin = jnp.max(jnp.where(starts[None, :] <= first[:, None], starts[None, :], 0), axis=1)
    below = jnp.sum((kpos[None, :] * BLOCK + BLOCK - 1 < begin[:, None]).astype(jnp.int32), axis=1)
    upto = jnp.sum((kpos[None, :] * BLOCK <= last[:, None]).astype(jnp.int32), axis=1)
    return jnp.concatenate(
        [krank, kpos, qrank, qpos, qindex, below // 2, (upto + 1) // 2, starts,
         jnp.stack([zh * 2 + zl, zl]).astype(jnp.int32)]
    )


def attention(sc, queries, pieces):
    keys = sorted(pieces)

    def kernel(sc, q_own, q_other, *refs):
        n = len(keys)
        kv_refs, (out_own, out_other), (kv, q, s_all, sem) = refs[:n], refs[n : n + 2], refs[n + 2 :]
        copies = []
        for i, q_ref in enumerate((q_own, q_other)):
            for b in range(8):
                copies.append((q_ref.at[b], q.at[sc[QRANK + i * 8 + b]]))
        for (half, offset), ref in zip(keys, kv_refs, strict=True):
            z = lax.rem(sc[ZPOS] + offset + NZ, NZ)
            zh, zl = z // 2, lax.rem(z, 2)
            for b in range(4):
                copies.append((ref.at[b], kv.at[sc[KRANK + zh * 8 + half * 4 + b], zl]))
        started = [pltpu.make_async_copy(src, dst, sem) for src, dst in copies]
        for copy in started:
            copy.start()
        for copy in started:
            copy.wait()

        row = lax.broadcasted_iota(jnp.int32, (QT, 1), 0)
        in_row = lax.rem(row, 64)
        row_offset = (in_row // SLICE * 2 + sc[ZLOW]) * SLICE + lax.rem(row, SLICE)
        col = lax.broadcasted_iota(jnp.int32, (1, KT), 1)
        in_col = lax.rem(col, BLOCK)
        col_offset = (lax.rem(in_col, 64) // SLICE * 2 + in_col // 64) * SLICE + lax.rem(col, SLICE)
        lane = lax.broadcasted_iota(jnp.int32, (64, HD), 1)
        nt = (((1,), (1,)), ((), ()))

        def key_tile(kt, t):
            return kv[pl.ds(2 * kt, 2), :, :, t].reshape(KT, HD)

        def tile(qt, _):
            q0, q1, q2 = (q[pl.ds(2 * qt, 2), :, t].reshape(QT, HD) for t in range(3))
            q10 = jnp.concatenate([q1, q0], 1)
            q20 = jnp.concatenate([q2, q0], 1)
            qpos = jnp.where(row < 64, sc[QPOS + 2 * qt], sc[QPOS + 2 * qt + 1]) * BLOCK + row_offset
            qstart = jnp.zeros_like(qpos)
            for d in range(3):
                qstart = jnp.where(qpos >= sc[STARTS + d], sc[STARTS + d], qstart)
            lo, hi = sc[KLO + qt], sc[KHI + qt]

            def scores(kt, top):
                kpos = jnp.where(col < BLOCK, sc[KPOS + 2 * kt], sc[KPOS + 2 * kt + 1]) * BLOCK + col_offset
                s = lax.dot_general(q0, key_tile(kt, 0), nt, preferred_element_type=jnp.float32)
                s = jnp.where((kpos <= qpos) & (kpos >= qstart), s, HIDDEN)
                s_all[kt] = s
                return jnp.maximum(top, jnp.maximum(s[:, :HD], s[:, HD:]))

            top = lax.fori_loop(lo, hi, scores, jnp.full((QT, HD), HIDDEN, jnp.float32))
            top = jnp.max(top, axis=1, keepdims=True)
            shift = jnp.where(top < 0.5 * HIDDEN, 0.0, top)

            def weigh(kt, state):
                total, c1, c2, acc, acc_w = state
                e = jnp.exp2((s_all[kt] - shift) * (SCALE * LOG2E))
                es = e * SCALE
                k0, k1, k2 = (key_tile(kt, t) for t in range(3))
                d1 = lax.dot_general(q10, jnp.concatenate([k0, k1], 1), nt, preferred_element_type=jnp.float32)
                d2 = lax.dot_general(q20, jnp.concatenate([k0, k2], 1), nt, preferred_element_type=jnp.float32)
                w1, w2 = es * d1, es * d2
                v = jnp.concatenate([key_tile(kt, t) for t in (3, 4, 5)], 1)
                acc = acc + jnp.dot(e.astype(jnp.bfloat16), v, preferred_element_type=jnp.float32)
                w = jnp.concatenate([w1.astype(jnp.bfloat16), w2.astype(jnp.bfloat16)], 0)
                acc_w = acc_w + jnp.dot(w, v[:, :HD], preferred_element_type=jnp.float32)
                return (
                    total + (e[:, :HD] + e[:, HD:]),
                    c1 + (w1[:, :HD] + w1[:, HD:]),
                    c2 + (w2[:, :HD] + w2[:, HD:]),
                    acc,
                    acc_w,
                )

            zero = jnp.zeros((QT, HD), jnp.float32)
            total, c1, c2, acc, acc_w = lax.fori_loop(
                lo, hi, weigh,
                (zero, zero, zero, jnp.zeros((QT, 3 * HD), jnp.float32), jnp.zeros((2 * QT, HD), jnp.float32)),
            )
            total, c1, c2 = (jnp.sum(v, axis=1, keepdims=True) for v in (total, c1, c2))
            results = (acc[:, :HD], acc[:, HD : 2 * HD] + acc_w[:QT], acc[:, 2 * HD :] + acc_w[QT:])

            for half in range(2):
                rows = slice(64 * half, 64 * half + 64)
                stats = jnp.where(
                    lane == 0, top[rows],
                    jnp.where(lane == 1, total[rows], jnp.where(lane == 2, c1[rows], c2[rows])),
                )
                block = [r.reshape(2, SLICE, HD) for r in (*(r[rows] for r in results), stats)]
                index = sc[QINDEX + 2 * qt + half]

                @pl.when(index < 8)
                def _(block=block, index=index):
                    for t in range(4):
                        out_own[index, :, t] = block[t]

                @pl.when(index >= 8)
                def _(block=block, index=index):
                    for t in range(4):
                        out_other[index - 8, :, t] = block[t]

            return 0

        lax.fori_loop(0, 8, tile, 0)

    part = jax.ShapeDtypeStruct((8, 2, 4, SLICE, HD), jnp.float32)
    return pl.pallas_call(
        kernel,
        out_shape=(part, part),
        in_specs=[SMEM] + [ANY] * (2 + len(keys)),
        out_specs=(VMEM, VMEM),
        scratch_shapes=[
            pltpu.VMEM((32, 2, 2, 6, SLICE, HD), jnp.bfloat16),
            pltpu.VMEM((16, 2, 3, SLICE, HD), jnp.bfloat16),
            pltpu.VMEM((16, QT, KT), jnp.float32),
            pltpu.SemaphoreType.DMA,
        ],
        compiler_params=pltpu.CompilerParams(vmem_limit_bytes=32 * 2**20),
    )(sc, *queries, *(pieces[k] for k in keys))


def merge(mine, theirs):
    def kernel(a, b, out):
        for blk in range(8):
            for xl in range(2):
                sa, sb = a[blk, xl, 3], b[blk, xl, 3]
                ta, tb = sa[:, 0:1], sb[:, 0:1]
                top = jnp.maximum(ta, tb)
                fa = jnp.exp2((ta - top) * (SCALE * LOG2E))
                fb = jnp.exp2((tb - top) * (SCALE * LOG2E))
                total, c1, c2 = (sa[:, i : i + 1] * fa + sb[:, i : i + 1] * fb for i in (1, 2, 3))
                inv = 1.0 / total
                fa, fb = fa * inv, fb * inv
                primal = a[blk, xl, 0] * fa + b[blk, xl, 0] * fb
                out[blk * 2 + xl, 0] = primal.astype(jnp.bfloat16)
                for i, c in ((1, c1), (2, c2)):
                    grad = a[blk, xl, i] * fa + b[blk, xl, i] * fb
                    out[blk * 2 + xl, i] = (grad - (c * inv) * primal).astype(jnp.bfloat16)

    return pl.pallas_call(
        kernel,
        out_shape=jax.ShapeDtypeStruct((16, 3, SLICE, HD), jnp.bfloat16),
        in_specs=[VMEM, VMEM],
        out_specs=VMEM,
    )(mine, theirs)


def hop(block, direction):
    return lax.ppermute(block, Z, [(i, (i + direction) % NZ) for i in range(NZ)])


def swap_cores(block):
    return lax.ppermute(block, "c", [(0, 1), (1, 0)])


def shards(query_set, key_set, value_set, block_order, documents):
    kv = lax.all_to_all(split_heads(key_set, value_set), XY, 0, 0)
    kv = kv.reshape(8, 2, 6, SLICE, HD)
    q = lax.all_to_all(split_heads(query_set), XY, 0, 0).reshape(8, 2, 3, SLICE, HD)
    pieces = {(half, 0): kv[4 * half : 4 * half + 4] for half in range(2)}
    ups = [pieces[0, 0], pieces[1, 0]]
    downs = [pieces[0, 0], pieces[1, 0]]
    for step in range(1, 5):
        for half in range(2):
            if step < 4 or half == 0:
                ups[half] = pieces[half, -step] = hop(ups[half], 1)
            if step < 4 or half == 1:
                downs[half] = pieces[half, step] = hop(downs[half], -1)
    sc = scalars(block_order, documents)
    own, other = attention(sc, (q, swap_cores(q)), pieces)
    done = merge(own, swap_cores(other))
    return join_heads(lax.all_to_all(done, XY, 0, 0))


def solution(mesh):
    fine = Mesh(mesh.devices.reshape(SIZES), NAMES)
    rows = P(None, NAMES, None)
    return jax.shard_map(
        shards,
        mesh=fine,
        in_specs=(rows, rows, rows, P(), P()),
        out_specs=rows,
        check_vma=False,
    )
```

time: 803 us -> 154 us (0.19)
  the two profiles are of different devices: /device:TPU:128 before, /device:TPU:96 now
where the time goes in v1:
time: 154 us; the launch traced here: 155 us
  waiting for transfers between devices  46.3 us (30%)
  Pallas kernels  44.9 us (29%)
  starting transfers between devices  34.8 us (23%)
  blocking collectives  17.4 us (11%)
  local copies, waits for them, and re-layouts  5.68 us (4%)
  other arithmetic  5.37 us (3%)
    pallas_call x1, Pallas kernels, attention(): pl.pallas_call(kernel, out_shape=(part, part), in_specs=[SMEM] + [ANY] *...  32.6 us
    ppermute x14, waiting for transfers between devices, hop(): lax.ppermute(block, Z, [(i, (i + direction) % NZ) for i in range(NZ)])  32.2 us
    ppermute x14, starting transfers between devices, hop(): lax.ppermute(block, Z, [(i, (i + direction) % NZ) for i in range(NZ)])  24.1 us
    all_to_all x1, blocking collectives, shards(): return join_heads(lax.all_to_all(done, XY, 0, 0))  17.4 us
    all_to_all x1, waiting for transfers between devices, shards(): kv = lax.all_to_all(split_heads(key_set, value_set), XY, 0, 0)  11.4 us
    all_to_all x1, starting transfers between devices, shards(): kv = lax.all_to_all(split_heads(key_set, value_set), XY, 0, 0)  7.03 us
    pallas_call x1, Pallas kernels, merge(): pl.pallas_call(kernel, out_shape=jax.ShapeDtypeStruct((16, 3, SLICE, HD),...  6.48 us
    pallas_call x2, Pallas kernels, split_heads(): pl.pallas_call(kernel, out_shape=jax.ShapeDtypeStruct((HEADS, 3 * len(arr...  3.95 us
  transfers between devices with their start and end apart: 18, of which 10 were waited for; matrix products, arithmetic and copies ran while one was open for 5% of the time, Pallas kernels for 1%

profile of v1, /device:TPU:96, one launch (start us, length us, event | category | flops | bytes accessed | tf_op | source)
XLA Modules:
  0.0 154.6 jit_solution(18043127251753452846)
XLA Ops:
  0.0 2.1 %shard_map.56 = bf16[16,6,32,128]{3,2,1,0:T(8,128)(2,1)} custom-call(bf16[3,32,2048]{2,1,0:T(8,128)(2,1)} %refs_0_.3, bf16[3,32,2048]{2,1,0:T(8,128)(2,1)} %refs_1_.1), custom_call_target="tpu_custom_call" | custom-call | tf_op jit(solution)/shard_map/pallas_call | solution.py:48
  2.1 7.0 %all-to-all-start.1 = ((bf16[16,6,32,128]{3,2,1,0:T(8,128)(2,1)}), bf16[16,6,32,128]{3,2,1,0:T(8,128)(2,1)S(1)}, u32[]{:S(2)}, u32[]{:S(2)}) async-start(bf16[16,6,32,128]{3,2,1,0:T(8,128)(2,1)} %shard_map.56), calls=%async_computation.1 | async-start | bytes 1572864 | tf_op jit(solution)/shard_map/all_to_all | solution.py:257
  9.2 0.6 copy-done.3
  10.2 1.8 %shard_map.55 = bf16[16,3,32,128]{3,2,1,0:T(8,128)(2,1)} custom-call(bf16[3,32,2048]{2,1,0:T(8,128)(2,1)} %refs_0_.2), custom_call_target="tpu_custom_call" | custom-call | tf_op jit(solution)/shard_map/pallas_call | solution.py:48
  12.2 11.4 %all-to-all-done.1 = bf16[16,6,32,128]{3,2,1,0:T(8,128)(2,1)S(1)} async-done(((bf16[16,6,32,128]{3,2,1,0:T(8,128)(2,1)}), bf16[16,6,32,128]{3,2,1,0:T(8,128)(2,1)S(1)}, u32[]{:S(2)}, u32[]{:S(2)}) %all-to-all-start.1) | async-done | bytes 786464 | tf_op jit(solution)/shard_map/all_to_all | solution.py:257
  23.7 3.6 %all-to-all-start = ((bf16[16,3,32,128]{3,2,1,0:T(8,128)(2,1)}), bf16[16,3,32,128]{3,2,1,0:T(8,128)(2,1)S(1)}, u32[]{:S(2)}, u32[]{:S(2)}) async-start(bf16[16,3,32,128]{3,2,1,0:T(8,128)(2,1)} %shard_map.55), calls=%async_computation | async-start | bytes 786432 | tf_op jit(solution)/shard_map/all_to_all | solution.py:259
  27.3 3.2 %collective-permute-start.1 = (bf16[4,2,6,32,128]{4,3,2,1,0:T(8,128)(2,1)S(1)}, bf16[4,2,6,32,128]{4,3,2,1,0:T(8,128)(2,1)S(1)}, u32[]{:S(2)}, u32[]{:S(2)}) collective-permute-start(bf16[4,2,6,32,128]{4,3,2,1,0:T(8,128)(2,1)S(1)} %bitcast.10), channel_id=1, source_target_pairs={{0,1},{1,64},{64,65},{65,128},{128,129},{129,192},{192,193},{193,0... | collective-permute-start | bytes 1179656 | tf_op jit(solution)/shard_map/ppermute | solution.py:249
  31.3 0.8 convert_reduce_fusion.1
  32.5 3.2 %collective-permute-start.8 = (bf16[4,2,6,32,128]{4,3,2,1,0:T(8,128)(2,1)S(1)}, bf16[4,2,6,32,128]{4,3,2,1,0:T(8,128)(2,1)S(1)}, u32[]{:S(2)}, u32[]{:S(2)}) collective-permute-start(bf16[4,2,6,32,128]{4,3,2,1,0:T(8,128)(2,1)S(1)} %bitcast.8), channel_id=1, source_target_pairs={{0,1},{1,64},{64,65},{65,128},{128,129},{129,192},{192,193},{193,0... | collective-permute-start | bytes 1179656 | tf_op jit(solution)/shard_map/ppermute | solution.py:249
  35.8 4.3 %collective-permute-done.1.refs_3_ = bf16[4,2,6,32,128]{4,3,2,1,0:T(8,128)(2,1)S(1)} collective-permute-done((bf16[4,2,6,32,128]{4,3,2,1,0:T(8,128)(2,1)S(1)}, bf16[4,2,6,32,128]{4,3,2,1,0:T(8,128)(2,1)S(1)}, u32[]{:S(2)}, u32[]{:S(2)}) %collective-permute-start.1) | collective-permute-done | bytes 393248 | tf_op jit(solution)/shard_map/ppermute | solution.py:249
  40.1 3.7 %collective-permute-start.2 = (bf16[4,2,6,32,128]{4,3,2,1,0:T(8,128)(2,1)S(1)}, bf16[4,2,6,32,128]{4,3,2,1,0:T(8,128)(2,1)S(1)}, u32[]{:S(2)}, u32[]{:S(2)}) collective-permute-start(bf16[4,2,6,32,128]{4,3,2,1,0:T(8,128)(2,1)S(1)} %collective-permute-done.1.refs_3_), channel_id=1, source_target_pairs={{0,1},{1,64},{64,65},{65,128},{128,129},{129,192},{192,193},{193,0... | collective-permute-start | bytes 1179656 | tf_op jit(solution)/shard_map/ppermute | solution.py:249
  44.3 0.6 slice.18
  44.9 1.0 convert_reduce_fusion
  46.0 6.2 %collective-permute-done.5.refs_5_ = bf16[4,2,6,32,128]{4,3,2,1,0:T(8,128)(2,1)S(1)} collective-permute-done((bf16[4,2,6,32,128]{4,3,2,1,0:T(8,128)(2,1)S(1)}, bf16[4,2,6,32,128]{4,3,2,1,0:T(8,128)(2,1)S(1)}, u32[]{:S(2)}, u32[]{:S(2)}) %collective-permute-start.5) | collective-permute-done | bytes 393248 | tf_op jit(solution)/shard_map/ppermute | solution.py:249
  52.2 3.2 %collective-permute-start.9 = (bf16[4,2,6,32,128]{4,3,2,1,0:T(8,128)(2,1)S(1)}, bf16[4,2,6,32,128]{4,3,2,1,0:T(8,128)(2,1)}, u32[]{:S(2)}, u32[]{:S(2)}) collective-permute-start(bf16[4,2,6,32,128]{4,3,2,1,0:T(8,128)(2,1)S(1)} %collective-permute-done.8.refs_10_), channel_id=1, source_target_pairs={{0,1},{1,64},{64,65},{65,128},{128,129},{129,192},{192,193},{193,0... | collective-permute-start | bytes 1179656 | tf_op jit(solution)/shard_map/ppermute | solution.py:249
  55.4 1.5 collective-permute-done.2.refs_2_
  56.9 3.7 %collective-permute-start.3 = (bf16[4,2,6,32,128]{4,3,2,1,0:T(8,128)(2,1)S(1)}, bf16[4,2,6,32,128]{4,3,2,1,0:T(8,128)(2,1)}, u32[]{:S(2)}, u32[]{:S(2)}) collective-permute-start(bf16[4,2,6,32,128]{4,3,2,1,0:T(8,128)(2,1)S(1)} %collective-permute-done.2.refs_2_), channel_id=1, source_target_pairs={{0,1},{1,64},{64,65},{65,128},{128,129},{129,192},{192,193},{193,0... | collective-permute-start | bytes 1179656 | tf_op jit(solution)/shard_map/ppermute | solution.py:249
  62.1 7.1 %collective-permute-done.6.refs_6_ = bf16[4,2,6,32,128]{4,3,2,1,0:T(8,128)(2,1)} collective-permute-done((bf16[4,2,6,32,128]{4,3,2,1,0:T(8,128)(2,1)S(1)}, bf16[4,2,6,32,128]{4,3,2,1,0:T(8,128)(2,1)}, u32[]{:S(2)}, u32[]{:S(2)}) %collective-permute-start.6) | collective-permute-done | bytes 393248 | tf_op jit(solution)/shard_map/ppermute | solution.py:249
  69.2 3.2 %collective-permute-start.10 = (bf16[4,2,6,32,128]{4,3,2,1,0:T(8,128)(2,1)}, bf16[4,2,6,32,128]{4,3,2,1,0:T(8,128)(2,1)}, u32[]{:S(2)}, u32[]{:S(2)}) collective-permute-start(bf16[4,2,6,32,128]{4,3,2,1,0:T(8,128)(2,1)} %collective-permute-done.9.refs_9_), channel_id=1, source_target_pairs={{0,1},{1,64},{64,65},{65,128},{128,129},{129,192},{192,193},{193,0... | collective-permute-start | bytes 1179656 | tf_op jit(solution)/shard_map/ppermute | solution.py:249
  72.4 1.4 collective-permute-done.3.refs_1_
  73.8 3.8 %collective-permute-start.4 = (bf16[4,2,6,32,128]{4,3,2,1,0:T(8,128)(2,1)}, bf16[4,2,6,32,128]{4,3,2,1,0:T(8,128)(2,1)}, u32[]{:S(2)}, u32[]{:S(2)}) collective-permute-start(bf16[4,2,6,32,128]{4,3,2,1,0:T(8,128)(2,1)} %collective-permute-done.3.refs_1_), channel_id=1, source_target_pairs={{0,1},{1,64},{64,65},{65,128},{128,129},{129,192},{192,193},{193,0... | collective-permute-start | bytes 1179656 | tf_op jit(solution)/shard_map/ppermute | solution.py:249
  79.2 0.8 concatenate.7.sc
  80.0 6.1 %collective-permute-done.7.refs_7_ = bf16[4,2,6,32,128]{4,3,2,1,0:T(8,128)(2,1)} collective-permute-done((bf16[4,2,6,32,128]{4,3,2,1,0:T(8,128)(2,1)}, bf16[4,2,6,32,128]{4,3,2,1,0:T(8,128)(2,1)}, u32[]{:S(2)}, u32[]{:S(2)}) %collective-permute-start.7) | collective-permute-done | bytes 393248 | tf_op jit(solution)/shard_map/ppermute | solution.py:249
  86.0 2.2 %collective-permute-done.4.refs_0_ = bf16[4,2,6,32,128]{4,3,2,1,0:T(8,128)(2,1)} collective-permute-done((bf16[4,2,6,32,128]{4,3,2,1,0:T(8,128)(2,1)}, bf16[4,2,6,32,128]{4,3,2,1,0:T(8,128)(2,1)}, u32[]{:S(2)}, u32[]{:S(2)}) %collective-permute-start.4) | collective-permute-done | bytes 393248 | tf_op jit(solution)/shard_map/ppermute | solution.py:249
  88.2 3.4 %collective-permute-done.14.refs_15_ = bf16[4,2,6,32,128]{4,3,2,1,0:T(8,128)(2,1)} collective-permute-done((bf16[4,2,6,32,128]{4,3,2,1,0:T(8,128)(2,1)}, bf16[4,2,6,32,128]{4,3,2,1,0:T(8,128)(2,1)}, u32[]{:S(2)}, u32[]{:S(2)}) %collective-permute-start.14) | collective-permute-done | bytes 393248 | tf_op jit(solution)/shard_map/ppermute | solution.py:249
  91.6 32.6 %shard_map.57 = (f32[8,2,4,32,128]{4,3,2,1,0:T(8,128)S(1)}, f32[8,2,4,32,128]{4,3,2,1,0:T(8,128)S(1)}) custom-call(s32[133]{0:T(256)S(1)} %concatenate.7.sc, bf16[8,2,3,32,128]{4,3,2,1,0:T(8,128)(2,1)S(1)} %bitcast.6, bf16[8,2,3,32,128]{4,3,2,1,0:T(8,128)(2,1)} %collective-permute-done.q_other, bf16[4,2,6,32,128]{4,3,2,1,0:T(8,128)(2,1)} %collective-permute-done.4.refs_0_, ...), custom_call_target="tpu_custom_call" | custom-call | tf_op jit(solution)/shard_map/pallas_call | solution.py:207
  124.2 1.0 copy-done
  125.2 2.7 %collective-permute-done.15.b = f32[8,2,4,32,128]{4,3,2,1,0:T(8,128)S(1)} collective-permute-done((f32[8,2,4,32,128]{4,3,2,1,0:T(8,128)S(1)}, f32[8,2,4,32,128]{4,3,2,1,0:T(8,128)S(1)}, u32[]{:S(2)}, u32[]{:S(2)}) %collective-permute-start.15) | collective-permute-done | bytes 1048608 | tf_op jit(solution)/shard_map/ppermute | solution.py:253
  127.9 1.0 copy-done.1
  128.9 6.5 %shard_map.58 = bf16[16,3,32,128]{3,2,1,0:T(8,128)(2,1)} custom-call(f32[8,2,4,32,128]{4,3,2,1,0:T(8,128)} %copy-done, f32[8,2,4,32,128]{4,3,2,1,0:T(8,128)} %copy-done.1), custom_call_target="tpu_custom_call" | custom-call | tf_op jit(solution)/shard_map/pallas_call | solution.py:240
  135.4 17.4 %all_to_all.15.ref = bf16[16,3,32,128]{3,2,1,0:T(8,128)(2,1)} all-to-all(bf16[16,3,32,128]{3,2,1,0:T(8,128)(2,1)} %shard_map.58), channel_id=1, replica_groups=mesh['zh'=4,'y'=4,'c'=2,'xh'=2,'xl'=2,'zl'=2] {'y','xh','xl'}, dimensions={0} | all-to-all | bytes 786432 | tf_op jit(solution)/shard_map/all_to_all | solution.py:272
  152.8 1.8 %shard_map.59 = bf16[3,32,2048]{2,1,0:T(8,128)(2,1)} custom-call(bf16[16,3,32,128]{3,2,1,0:T(8,128)(2,1)} %all_to_all.15.ref), custom_call_target="tpu_custom_call" | custom-call | tf_op jit(solution)/shard_map/pallas_call | solution.py:61
  (60 shorter events, 5.4 us)
Async XLA Ops:
  2.1 21.5 %all-to-all-start.1 = ((bf16[16,6,32,128]{3,2,1,0:T(8,128)(2,1)}), bf16[16,6,32,128]{3,2,1,0:T(8,128)(2,1)S(1)}, u32[]{:S(2)}, u32[]{:S(2)}) async-start(bf16[16,6,32,128]{3,2,1,0:T(8,128)(2,1)} %shard_map.56), calls=%async_computation.1 | async-start | bytes 1572864 | tf_op jit(solution)/shard_map/all_to_all | solution.py:257
  9.2 0.7 copy-start.3
  23.7 38.3 %all-to-all-start = ((bf16[16,3,32,128]{3,2,1,0:T(8,128)(2,1)}), bf16[16,3,32,128]{3,2,1,0:T(8,128)(2,1)S(1)}, u32[]{:S(2)}, u32[]{:S(2)}) async-start(bf16[16,3,32,128]{3,2,1,0:T(8,128)(2,1)} %shard_map.55), calls=%async_computation | async-start | bytes 786432 | tf_op jit(solution)/shard_map/all_to_all | solution.py:259
  27.3 12.8 %collective-permute-start.1 = (bf16[4,2,6,32,128]{4,3,2,1,0:T(8,128)(2,1)S(1)}, bf16[4,2,6,32,128]{4,3,2,1,0:T(8,128)(2,1)S(1)}, u32[]{:S(2)}, u32[]{:S(2)}) collective-permute-start(bf16[4,2,6,32,128]{4,3,2,1,0:T(8,128)(2,1)S(1)} %bitcast.10), channel_id=1, source_target_pairs={{0,1},{1,64},{64,65},{65,128},{128,129},{129,192},{192,193},{193,0... | collective-permute-start | bytes 1179656 | tf_op jit(solution)/shard_map/ppermute | solution.py:249
  30.5 13.3 %collective-permute-start.11 = (bf16[4,2,6,32,128]{4,3,2,1,0:T(8,128)(2,1)S(1)}, bf16[4,2,6,32,128]{4,3,2,1,0:T(8,128)(2,1)S(1)}, u32[]{:S(2)}, u32[]{:S(2)}) collective-permute-start(bf16[4,2,6,32,128]{4,3,2,1,0:T(8,128)(2,1)S(1)} %bitcast.7), channel_id=1, source_target_pairs={{0,193},{1,0},{64,1},{65,64},{128,65},{129,128},{192,129},{193,192... | collective-permute-start | bytes 1179656 | tf_op jit(solution)/shard_map/ppermute | solution.py:249
  30.6 13.7 %copy-start.2 = (s32[16]{0:T(128)}, s32[16]{0:T(128)S(1)}, u32[]{:S(2)}) copy-start(s32[16]{0:T(128)S(1)} %get-tuple-element.12) | copy-start | bytes 196
  30.8 0.5 copy-start.6
  32.5 19.7 %collective-permute-start.5 = (bf16[4,2,6,32,128]{4,3,2,1,0:T(8,128)(2,1)S(1)}, bf16[4,2,6,32,128]{4,3,2,1,0:T(8,128)(2,1)S(1)}, u32[]{:S(2)}, u32[]{:S(2)}) collective-permute-start(bf16[4,2,6,32,128]{4,3,2,1,0:T(8,128)(2,1)S(1)} %bitcast.11), channel_id=1, source_target_pairs={{0,193},{1,0},{64,1},{65,64},{128,65},{129,128},{192,129},{193,192... | collective-permute-start | bytes 1179656 | tf_op jit(solution)/shard_map/ppermute | solution.py:249
  32.5 19.7 %collective-permute-start.8 = (bf16[4,2,6,32,128]{4,3,2,1,0:T(8,128)(2,1)S(1)}, bf16[4,2,6,32,128]{4,3,2,1,0:T(8,128)(2,1)S(1)}, u32[]{:S(2)}, u32[]{:S(2)}) collective-permute-start(bf16[4,2,6,32,128]{4,3,2,1,0:T(8,128)(2,1)S(1)} %bitcast.8), channel_id=1, source_target_pairs={{0,1},{1,64},{64,65},{65,128},{128,129},{129,192},{192,193},{193,0... | collective-permute-start | bytes 1179656 | tf_op jit(solution)/shard_map/ppermute | solution.py:249
  40.1 16.9 %collective-permute-start.2 = (bf16[4,2,6,32,128]{4,3,2,1,0:T(8,128)(2,1)S(1)}, bf16[4,2,6,32,128]{4,3,2,1,0:T(8,128)(2,1)S(1)}, u32[]{:S(2)}, u32[]{:S(2)}) collective-permute-start(bf16[4,2,6,32,128]{4,3,2,1,0:T(8,128)(2,1)S(1)} %collective-permute-done.1.refs_3_), channel_id=1, source_target_pairs={{0,1},{1,64},{64,65},{65,128},{128,129},{129,192},{192,193},{193,0... | collective-permute-start | bytes 1179656 | tf_op jit(solution)/shard_map/ppermute | solution.py:249
  43.8 16.9 %collective-permute-start.12 = (bf16[4,2,6,32,128]{4,3,2,1,0:T(8,128)(2,1)S(1)}, bf16[4,2,6,32,128]{4,3,2,1,0:T(8,128)(2,1)S(1)}, u32[]{:S(2)}, u32[]{:S(2)}) collective-permute-start(bf16[4,2,6,32,128]{4,3,2,1,0:T(8,128)(2,1)S(1)} %collective-permute-done.11.refs_12_), channel_id=1, source_target_pairs={{0,193},{1,0},{64,1},{65,64},{128,65},{129,128},{192,129},{193,192... | collective-permute-start | bytes 1179656 | tf_op jit(solution)/shard_map/ppermute | solution.py:249
  44.9 1.0 copy-start.12
  46.0 14.7 %copy-start.4 = (s32[32]{0:T(128)S(1)}, s32[32]{0:T(128)}, u32[]{:S(2)}) copy-start(s32[32]{0:T(128)} %convert_reduce_fusion.1) | copy-start | bytes 388
  46.0 14.7 %copy-start.7 = (s32[32]{0:T(128)S(1)}, s32[32]{0:T(128)}, u32[]{:S(2)}) copy-start(s32[32]{0:T(128)} %copy-done.6) | copy-start | bytes 388
  52.2 17.0 %collective-permute-start.6 = (bf16[4,2,6,32,128]{4,3,2,1,0:T(8,128)(2,1)S(1)}, bf16[4,2,6,32,128]{4,3,2,1,0:T(8,128)(2,1)}, u32[]{:S(2)}, u32[]{:S(2)}) collective-permute-start(bf16[4,2,6,32,128]{4,3,2,1,0:T(8,128)(2,1)S(1)} %collective-permute-done.5.refs_5_), channel_id=1, source_target_pairs={{0,193},{1,0},{64,1},{65,64},{128,65},{129,128},{192,129},{193,192... | collective-permute-start | bytes 1179656 | tf_op jit(solution)/shard_map/ppermute | solution.py:249
  52.2 17.0 %collective-permute-start.9 = (bf16[4,2,6,32,128]{4,3,2,1,0:T(8,128)(2,1)S(1)}, bf16[4,2,6,32,128]{4,3,2,1,0:T(8,128)(2,1)}, u32[]{:S(2)}, u32[]{:S(2)}) collective-permute-start(bf16[4,2,6,32,128]{4,3,2,1,0:T(8,128)(2,1)S(1)} %collective-permute-done.8.refs_10_), channel_id=1, source_target_pairs={{0,1},{1,64},{64,65},{65,128},{128,129},{129,192},{192,193},{193,0... | collective-permute-start | bytes 1179656 | tf_op jit(solution)/shard_map/ppermute | solution.py:249
  56.9 16.9 %collective-permute-start.3 = (bf16[4,2,6,32,128]{4,3,2,1,0:T(8,128)(2,1)S(1)}, bf16[4,2,6,32,128]{4,3,2,1,0:T(8,128)(2,1)}, u32[]{:S(2)}, u32[]{:S(2)}) collective-permute-start(bf16[4,2,6,32,128]{4,3,2,1,0:T(8,128)(2,1)S(1)} %collective-permute-done.2.refs_2_), channel_id=1, source_target_pairs={{0,1},{1,64},{64,65},{65,128},{128,129},{129,192},{192,193},{193,0... | collective-permute-start | bytes 1179656 | tf_op jit(solution)/shard_map/ppermute | solution.py:249
  60.6 17.0 %collective-permute-start.13 = (bf16[4,2,6,32,128]{4,3,2,1,0:T(8,128)(2,1)S(1)}, bf16[4,2,6,32,128]{4,3,2,1,0:T(8,128)(2,1)}, u32[]{:S(2)}, u32[]{:S(2)}) collective-permute-start(bf16[4,2,6,32,128]{4,3,2,1,0:T(8,128)(2,1)S(1)} %collective-permute-done.12.refs_13_), channel_id=1, source_target_pairs={{0,193},{1,0},{64,1},{65,64},{128,65},{129,128},{192,129},{193,192... | collective-permute-start | bytes 1179656 | tf_op jit(solution)/shard_map/ppermute | solution.py:249
  60.8 0.6 copy-start.5
  62.0 15.6 %copy-start.8 = (s32[8]{0:T(128)S(1)}, s32[8]{0:T(128)}, u32[]{:S(2)}) copy-start(s32[8]{0:T(128)} %multiply_add_fusion) | copy-start | bytes 100
  62.0 15.6 %copy-start.11 = (s32[32]{0:T(128)S(1)}, s32[32]{0:T(128)}, u32[]{:S(2)}) copy-start(s32[32]{0:T(128)} %get-tuple-element.15) | copy-start | bytes 388
  62.0 18.0 %collective-permute-start = (bf16[8,2,3,32,128]{4,3,2,1,0:T(8,128)(2,1)S(1)}, bf16[8,2,3,32,128]{4,3,2,1,0:T(8,128)(2,1)}, u32[]{:S(2)}, u32[]{:S(2)}) collective-permute-start(bf16[8,2,3,32,128]{4,3,2,1,0:T(8,128)(2,1)S(1)} %bitcast.5), channel_id=1, source_target_pairs={{0,8},{8,0},{1,9},{9,1},{2,10},{10,2},{3,11},{11,3},{4,12},{12,4},... | collective-permute-start | bytes 1179656 | tf_op jit(solution)/shard_map/ppermute | solution.py:253
  69.2 16.9 %collective-permute-start.7 = (bf16[4,2,6,32,128]{4,3,2,1,0:T(8,128)(2,1)}, bf16[4,2,6,32,128]{4,3,2,1,0:T(8,128)(2,1)}, u32[]{:S(2)}, u32[]{:S(2)}) collective-permute-start(bf16[4,2,6,32,128]{4,3,2,1,0:T(8,128)(2,1)} %collective-permute-done.6.refs_6_), channel_id=1, source_target_pairs={{0,193},{1,0},{64,1},{65,64},{128,65},{129,128},{192,129},{193,192... | collective-permute-start | bytes 1179656 | tf_op jit(solution)/shard_map/ppermute | solution.py:249
  69.2 16.8 %collective-permute-start.10 = (bf16[4,2,6,32,128]{4,3,2,1,0:T(8,128)(2,1)}, bf16[4,2,6,32,128]{4,3,2,1,0:T(8,128)(2,1)}, u32[]{:S(2)}, u32[]{:S(2)}) collective-permute-start(bf16[4,2,6,32,128]{4,3,2,1,0:T(8,128)(2,1)} %collective-permute-done.9.refs_9_), channel_id=1, source_target_pairs={{0,1},{1,64},{64,65},{65,128},{128,129},{129,192},{192,193},{193,0... | collective-permute-start | bytes 1179656 | tf_op jit(solution)/shard_map/ppermute | solution.py:249
  73.8 14.4 %collective-permute-start.4 = (bf16[4,2,6,32,128]{4,3,2,1,0:T(8,128)(2,1)}, bf16[4,2,6,32,128]{4,3,2,1,0:T(8,128)(2,1)}, u32[]{:S(2)}, u32[]{:S(2)}) collective-permute-start(bf16[4,2,6,32,128]{4,3,2,1,0:T(8,128)(2,1)} %collective-permute-done.3.refs_1_), channel_id=1, source_target_pairs={{0,1},{1,64},{64,65},{65,128},{128,129},{129,192},{192,193},{193,0... | collective-permute-start | bytes 1179656 | tf_op jit(solution)/shard_map/ppermute | solution.py:249
  77.6 14.0 %collective-permute-start.14 = (bf16[4,2,6,32,128]{4,3,2,1,0:T(8,128)(2,1)}, bf16[4,2,6,32,128]{4,3,2,1,0:T(8,128)(2,1)}, u32[]{:S(2)}, u32[]{:S(2)}) collective-permute-start(bf16[4,2,6,32,128]{4,3,2,1,0:T(8,128)(2,1)} %collective-permute-done.13.refs_14_), channel_id=1, source_target_pairs={{0,193},{1,0},{64,1},{65,64},{128,65},{129,128},{192,129},{193,192... | collective-permute-start | bytes 1179656 | tf_op jit(solution)/shard_map/ppermute | solution.py:249
  77.8 0.6 copy-start.9
  77.8 0.7 copy-start.10
  124.2 1.0 copy-start
  125.2 2.7 %collective-permute-start.15 = (f32[8,2,4,32,128]{4,3,2,1,0:T(8,128)S(1)}, f32[8,2,4,32,128]{4,3,2,1,0:T(8,128)S(1)}, u32[]{:S(2)}, u32[]{:S(2)}) collective-permute-start(f32[8,2,4,32,128]{4,3,2,1,0:T(8,128)S(1)} %get-tuple-element.8), channel_id=1, source_target_pairs={{0,8},{8,0},{1,9},{9,1},{2,10},{10,2},{3,11},{11,3},{4,12},{12,4},... | collective-permute-start | bytes 3145736 | tf_op jit(solution)/shard_map/ppermute | solution.py:253
  127.9 1.0 copy-start.1

commit v2 on v1

v2 whole, which is shorter than its diff:
```python
import jax
import jax.numpy as jnp
from jax import lax
from jax.experimental import pallas as pl
from jax.experimental.pallas import tpu as pltpu
from jax.sharding import Mesh
from jax.sharding import PartitionSpec as P

HD = 128
HEADS = 16
BLOCK = 128
SLICE = 32
HALF = 2 * SLICE
Z = ("zh", "zl")
XY = ("y", "xh", "xl")
NAMES = ("zh", "y", "c", "xh", "xl", "zl")
SIZES = (4, 4, 2, 2, 2, 2)
NZ = 8
SCALE = 1.0 / HD**0.5
EXPONENT = SCALE * 1.4426950408889634
HIDDEN = -1e30
VMEM = pl.BlockSpec(memory_space=pltpu.VMEM)
SMEM = pl.BlockSpec(memory_space=pltpu.SMEM)
ANY = pl.BlockSpec(memory_space=pl.ANY)
NT = (((1,), (1,)), ((), ()))

NEAR = (-2, -1, 0, 1, 2)
NEXT = (-3, 3)
FIRST = (0, 40, 56, 72, 88, 96)
N_SLOTS = 96
QB, KB = 4, 8
QT, KT = QB * HALF, KB * HALF
INDEX, BASE, LOW, HIGH, STARTS = 0, 96, 192, 210, 228


def split_heads(*arrays):
    def kernel(*refs):
        out = refs[-1]
        for h in range(HEADS):
            for a, ref in enumerate(refs[:-1]):
                out[h, 3 * a : 3 * a + 3] = ref[:, :, h * HD : (h + 1) * HD]

    return pl.pallas_call(
        kernel,
        out_shape=jax.ShapeDtypeStruct((HEADS, 3 * len(arrays), SLICE, HD), jnp.bfloat16),
        in_specs=[VMEM] * len(arrays),
        out_specs=VMEM,
    )(*arrays)


def join_heads(parts):
    def kernel(ref, out):
        for h in range(HEADS):
            out[:, :, h * HD : (h + 1) * HD] = ref[h]

    return pl.pallas_call(
        kernel,
        out_shape=jax.ShapeDtypeStruct((3, SLICE, HEADS * HD), jnp.bfloat16),
        in_specs=[VMEM],
        out_specs=VMEM,
    )(parts)


def scalars(order, documents, zh, zl, c):
    i32 = jnp.int32
    z = zh * 2 + zl
    offsets = jnp.array((*NEAR, *NEXT, 4, 4, 0, 0, 0), i32)
    cores = jnp.array((0, 0, 0, 0, 0, 0, 0, 0, 1, 0, 1, 0), i32)
    sets = jnp.array((0, 0, 0, 0, 0, 1, 1, 2, 2, 3, 3, 4), i32)
    begins = jnp.array((0, 0, 0, 0, 0, 5, 5, 7, 7, 9, 9, 11), i32)
    planes = lax.rem(z + offsets + NZ, NZ)
    table = order.reshape(4, 4, 2, 2).transpose(0, 2, 1, 3).reshape(8, 8)
    line = planes // 2 * 2 + lax.rem(cores + c, 2)
    hit = line[:, None] == jnp.arange(8, dtype=i32)[None, :]
    pos = jnp.sum(jnp.where(hit[:, :, None], table[None], 0), axis=1)
    code = (sets[:, None] * 4096 + pos * 2 + lax.rem(planes, 2)[:, None]).reshape(-1)
    payload = ((jnp.arange(12, dtype=i32) - begins)[:, None] * 8 + jnp.arange(8, dtype=i32)[None, :]).reshape(-1)
    rank = jnp.sum((code[None, :] < code[:, None]).astype(i32), axis=1)
    slot = jnp.arange(N_SLOTS, dtype=i32)
    hits = rank[None, :] == slot[:, None]
    index = jnp.sum(jnp.where(hits, payload[None, :], 0), axis=1)
    low_bits = code % 4096
    base_of = low_bits // 2 * BLOCK + low_bits % 2 * SLICE
    base = jnp.sum(jnp.where(hits, base_of[None, :], 0), axis=1)
    starts = jnp.sum((documents[None, :] < jnp.arange(1, 4, dtype=i32)[:, None]).astype(i32), axis=1)
    first = base[FIRST[3] :: QB]
    last = base[FIRST[3] + QB - 1 :: QB] + BLOCK - SLICE
    begin = jnp.max(jnp.where(starts[None, :] <= first[:, None], starts[None, :], 0), axis=1)
    set_of = code // 4096
    member = set_of[None, None, :] == jnp.arange(3, dtype=i32)[:, None, None]
    before = base_of[None, None, :] + BLOCK - SLICE <= begin[None, :, None]
    upto = base_of[None, None, :] < last[None, :, None]
    low = jnp.sum((member & before).astype(i32), axis=2) // KB
    high = (jnp.sum((member & upto).astype(i32), axis=2) + KB - 1) // KB
    return jnp.concatenate([index, base, low.reshape(-1), high.reshape(-1), starts])


def lookup(sc, at, count, position, size):
    out = sc[at]
    for i in range(1, count):
        out = jnp.where(position >= i * size, sc[at + i], out)
    return out


def within(position):
    return lax.rem(position, HALF) // SLICE * HALF + lax.rem(position, SLICE)


def gathered(sc, ref, at, count, t):
    return jnp.concatenate([ref[sc[at + i], :, t].reshape(HALF, HD) for i in range(count)], 0)


def query_tile(sc, q, first, tile):
    at = first + tile * QB
    q0, q1, q2 = (gathered(sc, q, INDEX + at, QB, t) for t in range(3))
    row = lax.broadcasted_iota(jnp.int32, (QT, 1), 0)
    qpos = lookup(sc, BASE + at, QB, row, HALF) + within(row)
    start = jnp.zeros_like(qpos)
    for d in range(3):
        start = jnp.where(qpos >= sc[STARTS + d], sc[STARTS + d], start)
    return q0, jnp.concatenate([q1, q0], 1), jnp.concatenate([q2, q0], 1), qpos, start


def see(sc, kv, first, queries, state, low, high):
    q0, q10, q20, qpos, start = queries
    col = lax.broadcasted_iota(jnp.int32, (1, KT), 1)
    ones = jnp.ones((KT, HD), jnp.bfloat16)

    def step(kt, state):
        top, acc, acc_w = state
        at = first + kt * KB
        k0, k1, k2, v0, v1, v2 = (gathered(sc, kv, INDEX + at, KB, t) for t in range(6))
        kpos = lookup(sc, BASE + at, KB, col, HALF) + within(col)
        s = lax.dot_general(q0, k0, NT, preferred_element_type=jnp.float32)
        d1 = lax.dot_general(q10, jnp.concatenate([k0, k1], 1), NT, preferred_element_type=jnp.float32)
        d2 = lax.dot_general(q20, jnp.concatenate([k0, k2], 1), NT, preferred_element_type=jnp.float32)
        s = jnp.where((kpos <= qpos) & (kpos >= start), s, HIDDEN)
        peak = jnp.maximum(jnp.maximum(s[:, :HD], s[:, HD : 2 * HD]), jnp.maximum(s[:, 2 * HD : 3 * HD], s[:, 3 * HD :]))
        new = jnp.maximum(top, jnp.max(peak, axis=1, keepdims=True))
        shrink = jnp.exp2((top - new) * EXPONENT)
        shift = jnp.where(new < 0.5 * HIDDEN, 0.0, new)[:, :1]
        e = jnp.exp2((s - shift) * EXPONENT)
        w = jnp.concatenate([(e * d1).astype(jnp.bfloat16), (e * d2).astype(jnp.bfloat16)], 0)
        shrink4 = jnp.concatenate([shrink] * 4, 1)
        shrink2 = shrink4[:, : 2 * HD]
        acc = acc * shrink4 + jnp.dot(
            e.astype(jnp.bfloat16), jnp.concatenate([v0, v1, v2, ones], 1), preferred_element_type=jnp.float32
        )
        acc_w = acc_w * jnp.concatenate([shrink2, shrink2], 0) + jnp.dot(
            w, jnp.concatenate([v0, ones], 1), preferred_element_type=jnp.float32
        )
        return new, acc, acc_w

    return lax.fori_loop(low, high, step, state)


def fresh():
    return (
        jnp.full((QT, HD), HIDDEN, jnp.float32),
        jnp.zeros((QT, 4 * HD), jnp.float32),
        jnp.zeros((2 * QT, 2 * HD), jnp.float32),
    )


def pack_state(state):
    top, acc, acc_w = state
    total, c1, c2 = acc[:, 3 * HD :], acc_w[:QT, HD:] * SCALE, acc_w[QT:, HD:] * SCALE
    lane = lax.broadcasted_iota(jnp.int32, (QT, HD), 1)
    stats = jnp.where(lane == 0, top, jnp.where(lane == 1, total, jnp.where(lane == 2, c1, c2)))
    return (
        acc[:, :HD],
        acc[:, HD : 2 * HD] + acc_w[:QT, :HD] * SCALE,
        acc[:, 2 * HD : 3 * HD] + acc_w[QT:, :HD] * SCALE,
        stats,
    )


def unpack_state(parts):
    a, g1, g2, stats = parts
    top, total, c1, c2 = (jnp.broadcast_to(stats[:, i : i + 1], (QT, HD)) for i in range(4))
    zero = jnp.zeros((QT, HD), jnp.float32)
    acc = jnp.concatenate([a, g1, g2, total], 1)
    c = jnp.concatenate([c1, c2], 0) * (1.0 / SCALE)
    return top, acc, jnp.concatenate([jnp.concatenate([zero, zero], 0), c], 1)


def join_states(one, two):
    top = jnp.maximum(one[0], two[0])
    f, g = (jnp.exp2((t - top) * EXPONENT) for t in (one[0], two[0]))
    f4, g4 = (jnp.concatenate([v] * 4, 1) for v in (f, g))
    f2, g2 = (jnp.concatenate([v[:, : 2 * HD]] * 2, 0) for v in (f4, g4))
    return top, one[1] * f4 + two[1] * g4, one[2] * f2 + two[2] * g2


def gather_state(sc, ref, at):
    return unpack_state([gathered(sc, ref, at, QB, t) for t in range(4)])


def copy_in(pairs, sem):
    copies = [pltpu.make_async_copy(src, dst, sem) for src, dst in pairs]
    for copy in copies:
        copy.start()
    for copy in copies:
        copy.wait()


def attend(sc, queries, pieces, key_set, held=None):
    n = len(pieces)
    planes = n // 2

    def kernel(sc, q_own, q_other, *refs):
        kv_refs, refs = refs[:n], refs[n:]
        if held is not None:
            held_refs, refs = refs[:2], refs[2:]
        out_refs, (kv, q, st, sem) = refs[:2], refs[2:]
        pairs = [(q_own, q.at[0:8]), (q_other, q.at[8:16])]
        for i, ref in enumerate(kv_refs):
            pairs.append((ref, kv.at[i * 4 : i * 4 + 4]))
        if held is not None:
            pairs += [(ref, st.at[8 * i : 8 * i + 8]) for i, ref in enumerate(held_refs)]
        copy_in(pairs, sem)

        def tile(qt, _):
            info = query_tile(sc, q, FIRST[3], qt)
            low, high = sc[LOW + key_set * 6 + qt], sc[HIGH + key_set * 6 + qt]
            at = INDEX + FIRST[3] + qt * QB

            def work():
                before = fresh() if held is None else gather_state(sc, st, at)
                parts = pack_state(see(sc, kv, FIRST[key_set], info, before, low, high))
                for i in range(QB):
                    for t in range(4):
                        st[sc[at + i], :, t] = parts[t][i * HALF : i * HALF + HALF].reshape(2, SLICE, HD)

            if held is None:
                work()
            else:
                pl.when(high > low)(work)
            return 0

        lax.fori_loop(0, 4, tile, 0)
        copy_in([(st.at[8 * i : 8 * i + 8], ref) for i, ref in enumerate(out_refs)], sem)

    part = jax.ShapeDtypeStruct((8, 2, 4, SLICE, HD), jnp.float32)
    tiles = 4 * planes * HALF * 8 * 16 * HALF // 10
    return pl.pallas_call(
        kernel,
        out_shape=(part, part),
        in_specs=[SMEM] + [ANY] * (2 + n + (0 if held is None else 2)),
        out_specs=(ANY, ANY),
        scratch_shapes=[
            pltpu.VMEM((planes * 8, 2, 6, SLICE, HD), jnp.bfloat16),
            pltpu.VMEM((16, 2, 3, SLICE, HD), jnp.bfloat16),
            pltpu.VMEM((16, 2, 4, SLICE, HD), jnp.float32),
            pltpu.SemaphoreType.DMA,
        ],
        compiler_params=pltpu.CompilerParams(vmem_limit_bytes=28 * 2**20),
        cost_estimate=pl.CostEstimate(flops=tiles * 2560, bytes_accessed=8 * 2**20, transcendentals=tiles),
    )(sc, *queries, *pieces, *(held or ()))


def finish(sc, query, pieces, held):
    def kernel(sc, q_ref, p0, p1, p2, p3, own, other, out, kv, q, st_a, st_b, sem):
        pairs = [(q_ref, q), (own, st_a), (other, st_b)]
        pairs += [(ref, kv.at[4 * i : 4 * i + 4]) for i, ref in enumerate((p0, p1, p2, p3))]
        copy_in(pairs, sem)

        def tile(qt, _):
            info = query_tile(sc, q, FIRST[4], qt)
            at = INDEX + FIRST[4] + qt * QB
            state = join_states(gather_state(sc, st_a, at), gather_state(sc, st_b, at))
            low, high = sc[LOW + 2 * 6 + 4 + qt], sc[HIGH + 2 * 6 + 4 + qt]
            _, acc, acc_w = see(sc, kv, FIRST[2], info, state, low, high)
            inv = 1.0 / acc[:, 3 * HD :]
            primal = acc[:, :HD] * inv
            parts = [primal]
            for i in (1, 2):
                mine = slice((i - 1) * QT, i * QT)
                grad = acc[:, i * HD : (i + 1) * HD] + acc_w[mine, :HD] * SCALE
                parts.append(grad * inv - (acc_w[mine, HD:] * SCALE * inv) * primal)
            for i in range(QB):
                for t in range(3):
                    block = parts[t][i * HALF : i * HALF + HALF].reshape(2, SLICE, HD)
                    out[sc[at + i], :, t] = block.astype(jnp.bfloat16)
            return 0

        lax.fori_loop(0, 2, tile, 0)

    return pl.pallas_call(
        kernel,
        out_shape=jax.ShapeDtypeStruct((8, 2, 3, SLICE, HD), jnp.bfloat16),
        in_specs=[SMEM] + [ANY] * 7,
        out_specs=VMEM,
        scratch_shapes=[
            pltpu.VMEM((16, 2, 6, SLICE, HD), jnp.bfloat16),
            pltpu.VMEM((8, 2, 3, SLICE, HD), jnp.bfloat16),
            pltpu.VMEM((8, 2, 4, SLICE, HD), jnp.float32),
            pltpu.VMEM((8, 2, 4, SLICE, HD), jnp.float32),
            pltpu.SemaphoreType.DMA,
        ],
        compiler_params=pltpu.CompilerParams(vmem_limit_bytes=28 * 2**20),
    )(sc, query, *pieces, *held)


def hop(block, direction):
    return lax.ppermute(block, Z, [(i, (i + direction) % NZ) for i in range(NZ)])


def swap_cores(block):
    return lax.ppermute(block, "c", [(0, 1), (1, 0)])


def shards(query_set, key_set, value_set, block_order, documents):
    kv = lax.all_to_all(split_heads(key_set, value_set), XY, 0, 0)
    kv = kv.reshape(8, 2, 6, SLICE, HD)
    q = lax.all_to_all(split_heads(query_set), XY, 0, 0).reshape(8, 2, 3, SLICE, HD)
    pieces = {(half, 0): kv[4 * half : 4 * half + 4] for half in range(2)}
    ups = [pieces[0, 0], pieces[1, 0]]
    downs = [pieces[0, 0], pieces[1, 0]]
    for step in range(1, 5):
        for half in range(2):
            if step < 4 or half == 0:
                ups[half] = pieces[half, -step] = hop(ups[half], 1)
            if step < 4 or half == 1:
                downs[half] = pieces[half, step] = hop(downs[half], -1)
    sc = scalars(block_order, documents, *(lax.axis_index(a) for a in ("zh", "zl", "c")))
    queries = (q, swap_cores(q))
    state = attend(sc, queries, [pieces[half, o] for o in NEAR for half in range(2)], 0)
    own, other = attend(sc, queries, [pieces[half, o] for o in NEXT for half in range(2)], 1, state)
    far = [pieces[0, -4], pieces[1, 4]]
    done = finish(sc, q, [*far, *(swap_cores(p) for p in far)], (own, swap_cores(other)))
    done = lax.all_to_all(done.reshape(HEADS, 3, SLICE, HD), XY, 0, 0)
    return join_heads(done)


def solution(mesh):
    fine = Mesh(mesh.devices.reshape(SIZES), NAMES)
    rows = P(None, NAMES, None)
    return jax.shard_map(
        shards,
        mesh=fine,
        in_specs=(rows, rows, rows, P(), P()),
        out_specs=rows,
        check_vma=False,
    )
```

time: 154 us -> 143 us (0.929)
  the two profiles are of different devices: /device:TPU:96 before, /device:TPU:1 now
where the time goes in v2:
time: 143 us; the launch traced here: 142 us
  starting transfers between devices  46.3 us (32%)
  Pallas kernels  34.2 us (24%)
  waiting for transfers between devices  32.7 us (23%)
  blocking collectives  16.3 us (11%)
  local copies, waits for them, and re-layouts  9.98 us (7%)
  other arithmetic  2.21 us (2%)
    ppermute x14, waiting for transfers between devices, hop(): lax.ppermute(block, Z, [(i, (i + direction) % NZ) for i in range(NZ)])  23.6 us
    pallas_call x2, Pallas kernels, attend(): pl.pallas_call(kernel, out_shape=(part, part), in_specs=[SMEM] + [ANY] *...  22.9 us
    ppermute x14, starting transfers between devices, hop(): lax.ppermute(block, Z, [(i, (i + direction) % NZ) for i in range(NZ)])  20.9 us
    all_to_all x1, blocking collectives, shards(): done = lax.all_to_all(done.reshape(HEADS, 3, SLICE, HD), XY, 0, 0)  16.3 us
    ppermute x4, starting transfers between devices, swap_cores(): return lax.ppermute(block, 'c', [(0, 1), (1, 0)])  14 us
    unnamed x26, local copies, waits for them, and re-layouts  7.83 us
    all_to_all x1, starting transfers between devices, shards(): kv = lax.all_to_all(split_heads(key_set, value_set), XY, 0, 0)  7.58 us
    all_to_all x1, waiting for transfers between devices, shards(): kv = lax.all_to_all(split_heads(key_set, value_set), XY, 0, 0)  7.19 us
  transfers between devices with their start and end apart: 20, of which 7 were waited for; matrix products, arithmetic and copies ran while one was open for 3% of the time, Pallas kernels for 11%

profile of v2, /device:TPU:1, one launch (start us, length us, event | category | flops | bytes accessed | tf_op | source)
XLA Modules:
  0.0 141.9 jit_solution(5355146296934492987)
XLA Ops:
  0.0 2.1 %shard_map.92 = bf16[16,6,32,128]{3,2,1,0:T(8,128)(2,1)} custom-call(bf16[3,32,2048]{2,1,0:T(8,128)(2,1)} %refs_0_.3, bf16[3,32,2048]{2,1,0:T(8,128)(2,1)} %refs_1_.1), custom_call_target="tpu_custom_call" | custom-call | tf_op jit(solution)/shard_map/pallas_call | solution.py:43
  2.1 7.6 %all-to-all-start.1 = ((bf16[16,6,32,128]{3,2,1,0:T(8,128)(2,1)}), bf16[16,6,32,128]{3,2,1,0:T(8,128)(2,1)S(1)}, u32[]{:S(2)}, u32[]{:S(2)}) async-start(bf16[16,6,32,128]{3,2,1,0:T(8,128)(2,1)} %shard_map.92), calls=%async_computation.1 | async-start | bytes 1572864 | tf_op jit(solution)/shard_map/all_to_all | solution.py:314
  13.5 1.8 %shard_map.91 = bf16[16,3,32,128]{3,2,1,0:T(8,128)(2,1)} custom-call(bf16[3,32,2048]{2,1,0:T(8,128)(2,1)} %refs_0_.2), custom_call_target="tpu_custom_call" | custom-call | tf_op jit(solution)/shard_map/pallas_call | solution.py:43
  15.7 7.2 %all-to-all-done.1 = bf16[16,6,32,128]{3,2,1,0:T(8,128)(2,1)S(1)} async-done(((bf16[16,6,32,128]{3,2,1,0:T(8,128)(2,1)}), bf16[16,6,32,128]{3,2,1,0:T(8,128)(2,1)S(1)}, u32[]{:S(2)}, u32[]{:S(2)}) %all-to-all-start.1) | async-done | bytes 786464 | tf_op jit(solution)/shard_map/all_to_all | solution.py:314
  22.9 3.8 %all-to-all-start = ((bf16[16,3,32,128]{3,2,1,0:T(8,128)(2,1)}), bf16[16,3,32,128]{3,2,1,0:T(8,128)(2,1)S(1)}, u32[]{:S(2)}, u32[]{:S(2)}) async-start(bf16[16,3,32,128]{3,2,1,0:T(8,128)(2,1)} %shard_map.91), calls=%async_computation | async-start | bytes 786432 | tf_op jit(solution)/shard_map/all_to_all | solution.py:316
  26.8 1.7 %collective-permute-start = (bf16[4,2,6,32,128]{4,3,2,1,0:T(8,128)(2,1)S(1)}, bf16[4,2,6,32,128]{4,3,2,1,0:T(8,128)(2,1)S(1)}, u32[]{:S(2)}, u32[]{:S(2)}) collective-permute-start(bf16[4,2,6,32,128]{4,3,2,1,0:T(8,128)(2,1)S(1)} %bitcast.13), channel_id=1, source_target_pairs={{0,1},{1,64},{64,65},{65,128},{128,129},{129,192},{192,193},{193,0... | collective-permute-start | bytes 1179656 | tf_op jit(solution)/shard_map/ppermute | solution.py:306
  28.5 4.0 %collective-permute-start.14 = (bf16[4,2,6,32,128]{4,3,2,1,0:T(8,128)(2,1)S(1)}, bf16[4,2,6,32,128]{4,3,2,1,0:T(8,128)(2,1)S(1)}, u32[]{:S(2)}, u32[]{:S(2)}) collective-permute-start(bf16[4,2,6,32,128]{4,3,2,1,0:T(8,128)(2,1)S(1)} %bitcast.14), channel_id=1, source_target_pairs={{0,193},{1,0},{64,1},{65,64},{128,65},{129,128},{192,129},{193,192... | collective-permute-start | bytes 1179656 | tf_op jit(solution)/shard_map/ppermute | solution.py:306
  32.5 2.7 %collective-permute-start.4 = (bf16[4,2,6,32,128]{4,3,2,1,0:T(8,128)(2,1)S(1)}, bf16[4,2,6,32,128]{4,3,2,1,0:T(8,128)(2,1)S(1)}, u32[]{:S(2)}, u32[]{:S(2)}) collective-permute-start(bf16[4,2,6,32,128]{4,3,2,1,0:T(8,128)(2,1)S(1)} %bitcast.11), channel_id=1, source_target_pairs={{0,193},{1,0},{64,1},{65,64},{128,65},{129,128},{192,129},{193,192... | collective-permute-start | bytes 1179656 | tf_op jit(solution)/shard_map/ppermute | solution.py:306
  35.5 4.4 %collective-permute-done.refs_2_ = bf16[4,2,6,32,128]{4,3,2,1,0:T(8,128)(2,1)S(1)} collective-permute-done((bf16[4,2,6,32,128]{4,3,2,1,0:T(8,128)(2,1)S(1)}, bf16[4,2,6,32,128]{4,3,2,1,0:T(8,128)(2,1)S(1)}, u32[]{:S(2)}, u32[]{:S(2)}) %collective-permute-start) | collective-permute-done | bytes 393248 | tf_op jit(solution)/shard_map/ppermute | solution.py:306
  39.8 8.4 %collective-permute-done.11.refs_3_ = bf16[4,2,6,32,128]{4,3,2,1,0:T(8,128)(2,1)S(1)} collective-permute-done((bf16[4,2,6,32,128]{4,3,2,1,0:T(8,128)(2,1)S(1)}, bf16[4,2,6,32,128]{4,3,2,1,0:T(8,128)(2,1)S(1)}, u32[]{:S(2)}, u32[]{:S(2)}) %collective-permute-start.11) | collective-permute-done | bytes 393248 | tf_op jit(solution)/shard_map/ppermute | solution.py:306
  48.3 0.8 copy-done.2
  49.0 2.7 %collective-permute-start.15 = (bf16[4,2,6,32,128]{4,3,2,1,0:T(8,128)(2,1)S(1)}, bf16[4,2,6,32,128]{4,3,2,1,0:T(8,128)(2,1)}, u32[]{:S(2)}, u32[]{:S(2)}) collective-permute-start(bf16[4,2,6,32,128]{4,3,2,1,0:T(8,128)(2,1)S(1)} %collective-permute-done.14.refs_6_), channel_id=1, source_target_pairs={{0,193},{1,0},{64,1},{65,64},{128,65},{129,128},{192,129},{193,192... | collective-permute-start | bytes 1179656 | tf_op jit(solution)/shard_map/ppermute | solution.py:306
  52.5 0.8 copy-done.4
  53.9 6.3 %collective-permute-start.10 = (bf16[8,2,3,32,128]{4,3,2,1,0:T(8,128)(2,1)S(1)}, bf16[8,2,3,32,128]{4,3,2,1,0:T(8,128)(2,1)S(1)}, u32[]{:S(2)}, u32[]{:S(2)}) collective-permute-start(bf16[8,2,3,32,128]{4,3,2,1,0:T(8,128)(2,1)S(1)} %bitcast.5), channel_id=1, source_target_pairs={{0,8},{8,0},{1,9},{9,1},{2,10},{10,2},{3,11},{11,3},{4,12},{12,4},... | collective-permute-start | bytes 1179656 | tf_op jit(solution)/shard_map/ppermute | solution.py:310
  60.8 0.9 collective-permute-start.2
  61.8 1.6 %collective-permute-done.5.refs_9_ = bf16[4,2,6,32,128]{4,3,2,1,0:T(8,128)(2,1)} collective-permute-done((bf16[4,2,6,32,128]{4,3,2,1,0:T(8,128)(2,1)S(1)}, bf16[4,2,6,32,128]{4,3,2,1,0:T(8,128)(2,1)}, u32[]{:S(2)}, u32[]{:S(2)}) %collective-permute-start.5) | collective-permute-done | bytes 393248 | tf_op jit(solution)/shard_map/ppermute | solution.py:306
  63.3 3.5 %collective-permute-start.6 = (bf16[4,2,6,32,128]{4,3,2,1,0:T(8,128)(2,1)}, bf16[4,2,6,32,128]{4,3,2,1,0:T(8,128)(2,1)S(1)}, u32[]{:S(2)}, u32[]{:S(2)}) collective-permute-start(bf16[4,2,6,32,128]{4,3,2,1,0:T(8,128)(2,1)} %collective-permute-done.5.refs_9_), channel_id=1, source_target_pairs={{0,193},{1,0},{64,1},{65,64},{128,65},{129,128},{192,129},{193,192... | collective-permute-start | bytes 1179656 | tf_op jit(solution)/shard_map/ppermute | solution.py:306
  66.9 2.7 %collective-permute-start.16 = (bf16[4,2,6,32,128]{4,3,2,1,0:T(8,128)(2,1)}, bf16[4,2,6,32,128]{4,3,2,1,0:T(8,128)(2,1)S(1)}, u32[]{:S(2)}, u32[]{:S(2)}) collective-permute-start(bf16[4,2,6,32,128]{4,3,2,1,0:T(8,128)(2,1)} %collective-permute-done.15.refs_8_), channel_id=1, source_target_pairs={{0,193},{1,0},{64,1},{65,64},{128,65},{129,128},{192,129},{193,192... | collective-permute-start | bytes 1179656 | tf_op jit(solution)/shard_map/ppermute | solution.py:306
  70.1 0.8 concatenate.3.sc
  70.8 1.0 copy-done.1
  71.8 1.0 copy-done.3
  72.8 1.0 copy-done.5
  73.8 14.3 %shard_map.93 = (f32[8,2,4,32,128]{4,3,2,1,0:T(8,128)S(1)}, f32[8,2,4,32,128]{4,3,2,1,0:T(8,128)S(1)}) custom-call(s32[231]{0:T(256)S(1)} %concatenate.3.sc, bf16[8,2,3,32,128]{4,3,2,1,0:T(8,128)(2,1)S(1)} %bitcast.6, bf16[8,2,3,32,128]{4,3,2,1,0:T(8,128)(2,1)S(1)} %collective-permute-done.10.q_other, ...), custom_call_target="tpu_custom_call" | custom-call | flops 2684354560 | bytes 8388608 | tf_op jit(solution)/shard_map/pallas_call | solution.py:246
  88.1 8.6 %shard_map.94 = (f32[8,2,4,32,128]{4,3,2,1,0:T(8,128)S(1)}, f32[8,2,4,32,128]{4,3,2,1,0:T(8,128)S(1)}) custom-call(s32[231]{0:T(256)S(1)} %concatenate.3.sc, bf16[8,2,3,32,128]{4,3,2,1,0:T(8,128)(2,1)S(1)} %bitcast.7, bf16[8,2,3,32,128]{4,3,2,1,0:T(8,128)(2,1)S(1)} %collective-permute-done.10.q_other, ...), custom_call_target="tpu_custom_call" | custom-call | flops 1073740800 | bytes 8388608 | tf_op jit(solution)/shard_map/pallas_call | solution.py:246
  96.7 6.8 %collective-permute-start.17 = (f32[8,2,4,32,128]{4,3,2,1,0:T(8,128)S(1)}, f32[8,2,4,32,128]{4,3,2,1,0:T(8,128)S(1)}, u32[]{:S(2)}, u32[]{:S(2)}) collective-permute-start(f32[8,2,4,32,128]{4,3,2,1,0:T(8,128)S(1)} %get-tuple-element.12), channel_id=1, source_target_pairs={{0,8},{8,0},{1,9},{9,1},{2,10},{10,2},{3,11},{11,3},{4,12},{12,4},... | collective-permute-start | bytes 3145736 | tf_op jit(solution)/shard_map/ppermute | solution.py:310
  103.5 2.7 %collective-permute-start.7 = (bf16[4,2,6,32,128]{4,3,2,1,0:T(8,128)(2,1)S(1)}, bf16[4,2,6,32,128]{4,3,2,1,0:T(8,128)(2,1)S(1)}, u32[]{:S(2)}, u32[]{:S(2)}) collective-permute-start(bf16[4,2,6,32,128]{4,3,2,1,0:T(8,128)(2,1)S(1)} %collective-permute-done.6.refs_3_), channel_id=1, source_target_pairs={{0,193},{1,0},{64,1},{65,64},{128,65},{129,128},{192,129},{193,192... | collective-permute-start | bytes 1179656 | tf_op jit(solution)/shard_map/ppermute | solution.py:306
  106.2 9.2 %collective-permute-done.3.p0 = bf16[4,2,6,32,128]{4,3,2,1,0:T(8,128)(2,1)S(1)} collective-permute-done((bf16[4,2,6,32,128]{4,3,2,1,0:T(8,128)(2,1)S(1)}, bf16[4,2,6,32,128]{4,3,2,1,0:T(8,128)(2,1)S(1)}, u32[]{:S(2)}, u32[]{:S(2)}) %collective-permute-start.3) | collective-permute-done | bytes 393248 | tf_op jit(solution)/shard_map/ppermute | solution.py:306
  115.4 0.9 collective-permute-start.8
  116.3 1.3 collective-permute-done.8.p2
  118.2 5.6 %shard_map.95 = bf16[8,2,3,32,128]{4,3,2,1,0:T(8,128)(2,1)S(1)} custom-call(s32[231]{0:T(256)S(1)} %concatenate.3.sc, bf16[8,2,3,32,128]{4,3,2,1,0:T(8,128)(2,1)S(1)} %bitcast.8, bf16[4,2,6,32,128]{4,3,2,1,0:T(8,128)(2,1)S(1)} %collective-permute-done.3.p0, bf16[4,2,6,32,128]{4,3,2,1,0:T(8,128)(2,1)S(1)} %collective-permute-done.7.p1, ...), custom_call_target="tpu_custom_call" | custom-call | tf_op jit(solution)/shard_map/pallas_call | solution.py:289
  123.8 16.3 %all_to_all.15.ref = bf16[16,3,32,128]{3,2,1,0:T(8,128)(2,1)} all-to-all(bf16[16,3,32,128]{3,2,1,0:T(8,128)(2,1)S(1)} %bitcast.9), channel_id=1, replica_groups=mesh['zh'=4,'y'=4,'c'=2,'xh'=2,'xl'=2,'zl'=2] {'y','xh','xl'}, dimensions={0} | all-to-all | bytes 786432 | tf_op jit(solution)/shard_map/all_to_all | solution.py:332
  140.0 1.8 %shard_map.96 = bf16[3,32,2048]{2,1,0:T(8,128)(2,1)} custom-call(bf16[16,3,32,128]{3,2,1,0:T(8,128)(2,1)} %all_to_all.15.ref), custom_call_target="tpu_custom_call" | custom-call | tf_op jit(solution)/shard_map/pallas_call | solution.py:56
  (71 shorter events, 7.5 us)
Async XLA Ops:
  2.1 20.8 %all-to-all-start.1 = ((bf16[16,6,32,128]{3,2,1,0:T(8,128)(2,1)}), bf16[16,6,32,128]{3,2,1,0:T(8,128)(2,1)S(1)}, u32[]{:S(2)}, u32[]{:S(2)}) async-start(bf16[16,6,32,128]{3,2,1,0:T(8,128)(2,1)} %shard_map.92), calls=%async_computation.1 | async-start | bytes 1572864 | tf_op jit(solution)/shard_map/all_to_all | solution.py:314
  9.7 0.7 copy-start.11
  9.8 0.7 copy-start.12
  11.4 0.7 copy-start.9
  12.2 0.7 copy-start.8
  13.5 1.8 %copy-start.6 = (s32[8192]{0:T(1024)S(1)}, s32[8192]{0:T(1024)}, u32[]{:S(2)}) copy-start(s32[8192]{0:T(1024)} %param.13) | copy-start | bytes 98308
  22.9 31.0 %all-to-all-start = ((bf16[16,3,32,128]{3,2,1,0:T(8,128)(2,1)}), bf16[16,3,32,128]{3,2,1,0:T(8,128)(2,1)S(1)}, u32[]{:S(2)}, u32[]{:S(2)}) async-start(bf16[16,3,32,128]{3,2,1,0:T(8,128)(2,1)} %shard_map.91), calls=%async_computation | async-start | bytes 786432 | tf_op jit(solution)/shard_map/all_to_all | solution.py:316
  26.8 13.1 %collective-permute-start = (bf16[4,2,6,32,128]{4,3,2,1,0:T(8,128)(2,1)S(1)}, bf16[4,2,6,32,128]{4,3,2,1,0:T(8,128)(2,1)S(1)}, u32[]{:S(2)}, u32[]{:S(2)}) collective-permute-start(bf16[4,2,6,32,128]{4,3,2,1,0:T(8,128)(2,1)S(1)} %bitcast.13), channel_id=1, source_target_pairs={{0,1},{1,64},{64,65},{65,128},{128,129},{129,192},{192,193},{193,0... | collective-permute-start | bytes 1179656 | tf_op jit(solution)/shard_map/ppermute | solution.py:306
  28.5 20.5 %collective-permute-start.14 = (bf16[4,2,6,32,128]{4,3,2,1,0:T(8,128)(2,1)S(1)}, bf16[4,2,6,32,128]{4,3,2,1,0:T(8,128)(2,1)S(1)}, u32[]{:S(2)}, u32[]{:S(2)}) collective-permute-start(bf16[4,2,6,32,128]{4,3,2,1,0:T(8,128)(2,1)S(1)} %bitcast.14), channel_id=1, source_target_pairs={{0,193},{1,0},{64,1},{65,64},{128,65},{129,128},{192,129},{193,192... | collective-permute-start | bytes 1179656 | tf_op jit(solution)/shard_map/ppermute | solution.py:306
  32.5 15.7 %collective-permute-start.11 = (bf16[4,2,6,32,128]{4,3,2,1,0:T(8,128)(2,1)S(1)}, bf16[4,2,6,32,128]{4,3,2,1,0:T(8,128)(2,1)S(1)}, u32[]{:S(2)}, u32[]{:S(2)}) collective-permute-start(bf16[4,2,6,32,128]{4,3,2,1,0:T(8,128)(2,1)S(1)} %bitcast.10), channel_id=1, source_target_pairs={{0,1},{1,64},{64,65},{65,128},{128,129},{129,192},{192,193},{193,0... | collective-permute-start | bytes 1179656 | tf_op jit(solution)/shard_map/ppermute | solution.py:306
  32.5 19.9 %collective-permute-start.4 = (bf16[4,2,6,32,128]{4,3,2,1,0:T(8,128)(2,1)S(1)}, bf16[4,2,6,32,128]{4,3,2,1,0:T(8,128)(2,1)S(1)}, u32[]{:S(2)}, u32[]{:S(2)}) collective-permute-start(bf16[4,2,6,32,128]{4,3,2,1,0:T(8,128)(2,1)S(1)} %bitcast.11), channel_id=1, source_target_pairs={{0,193},{1,0},{64,1},{65,64},{128,65},{129,128},{192,129},{193,192... | collective-permute-start | bytes 1179656 | tf_op jit(solution)/shard_map/ppermute | solution.py:306
  39.8 21.0 %collective-permute-start.1 = (bf16[4,2,6,32,128]{4,3,2,1,0:T(8,128)(2,1)S(1)}, bf16[4,2,6,32,128]{4,3,2,1,0:T(8,128)(2,1)}, u32[]{:S(2)}, u32[]{:S(2)}) collective-permute-start(bf16[4,2,6,32,128]{4,3,2,1,0:T(8,128)(2,1)S(1)} %collective-permute-done.refs_2_), channel_id=1, source_target_pairs={{0,1},{1,64},{64,65},{65,128},{128,129},{129,192},{192,193},{193,0... | collective-permute-start | bytes 1179656 | tf_op jit(solution)/shard_map/ppermute | solution.py:306
  48.3 18.6 %collective-permute-start.12 = (bf16[4,2,6,32,128]{4,3,2,1,0:T(8,128)(2,1)S(1)}, bf16[4,2,6,32,128]{4,3,2,1,0:T(8,128)(2,1)}, u32[]{:S(2)}, u32[]{:S(2)}) collective-permute-start(bf16[4,2,6,32,128]{4,3,2,1,0:T(8,128)(2,1)S(1)} %collective-permute-done.11.refs_3_), channel_id=1, source_target_pairs={{0,1},{1,64},{64,65},{65,128},{128,129},{129,192},{192,193},{193,0... | collective-permute-start | bytes 1179656 | tf_op jit(solution)/shard_map/ppermute | solution.py:306
  48.3 0.8 copy-start.2
  49.0 17.8 %collective-permute-start.15 = (bf16[4,2,6,32,128]{4,3,2,1,0:T(8,128)(2,1)S(1)}, bf16[4,2,6,32,128]{4,3,2,1,0:T(8,128)(2,1)}, u32[]{:S(2)}, u32[]{:S(2)}) collective-permute-start(bf16[4,2,6,32,128]{4,3,2,1,0:T(8,128)(2,1)S(1)} %collective-permute-done.14.refs_6_), channel_id=1, source_target_pairs={{0,193},{1,0},{64,1},{65,64},{128,65},{129,128},{192,129},{193,192... | collective-permute-start | bytes 1179656 | tf_op jit(solution)/shard_map/ppermute | solution.py:306
  51.7 0.8 copy-start
  52.5 10.9 %collective-permute-start.5 = (bf16[4,2,6,32,128]{4,3,2,1,0:T(8,128)(2,1)S(1)}, bf16[4,2,6,32,128]{4,3,2,1,0:T(8,128)(2,1)}, u32[]{:S(2)}, u32[]{:S(2)}) collective-permute-start(bf16[4,2,6,32,128]{4,3,2,1,0:T(8,128)(2,1)S(1)} %collective-permute-done.4.refs_7_), channel_id=1, source_target_pairs={{0,193},{1,0},{64,1},{65,64},{128,65},{129,128},{192,129},{193,192... | collective-permute-start | bytes 1179656 | tf_op jit(solution)/shard_map/ppermute | solution.py:306
  52.5 0.8 copy-start.4
  53.9 15.6 %copy-start.10 = (s32[18]{0:T(128)S(1)}, s32[18]{0:T(128)}, u32[]{:S(2)}) copy-start(s32[18]{0:T(128)} %reduce_sum.71) | copy-start | bytes 220
  53.9 16.9 %collective-permute-start.10 = (bf16[8,2,3,32,128]{4,3,2,1,0:T(8,128)(2,1)S(1)}, bf16[8,2,3,32,128]{4,3,2,1,0:T(8,128)(2,1)S(1)}, u32[]{:S(2)}, u32[]{:S(2)}) collective-permute-start(bf16[8,2,3,32,128]{4,3,2,1,0:T(8,128)(2,1)S(1)} %bitcast.5), channel_id=1, source_target_pairs={{0,8},{8,0},{1,9},{9,1},{2,10},{10,2},{3,11},{11,3},{4,12},{12,4},... | collective-permute-start | bytes 1179656 | tf_op jit(solution)/shard_map/ppermute | solution.py:310
  60.8 27.3 %collective-permute-start.2 = (bf16[4,2,6,32,128]{4,3,2,1,0:T(8,128)(2,1)}, bf16[4,2,6,32,128]{4,3,2,1,0:T(8,128)(2,1)S(1)}, u32[]{:S(2)}, u32[]{:S(2)}) collective-permute-start(bf16[4,2,6,32,128]{4,3,2,1,0:T(8,128)(2,1)} %collective-permute-done.1.refs_0_), channel_id=1, source_target_pairs={{0,1},{1,64},{64,65},{65,128},{128,129},{129,192},{192,193},{193,0... | collective-permute-start | bytes 1179656 | tf_op jit(solution)/shard_map/ppermute | solution.py:306
  63.3 24.8 %collective-permute-start.6 = (bf16[4,2,6,32,128]{4,3,2,1,0:T(8,128)(2,1)}, bf16[4,2,6,32,128]{4,3,2,1,0:T(8,128)(2,1)S(1)}, u32[]{:S(2)}, u32[]{:S(2)}) collective-permute-start(bf16[4,2,6,32,128]{4,3,2,1,0:T(8,128)(2,1)} %collective-permute-done.5.refs_9_), channel_id=1, source_target_pairs={{0,193},{1,0},{64,1},{65,64},{128,65},{129,128},{192,129},{193,192... | collective-permute-start | bytes 1179656 | tf_op jit(solution)/shard_map/ppermute | solution.py:306
  66.9 21.2 %collective-permute-start.13 = (bf16[4,2,6,32,128]{4,3,2,1,0:T(8,128)(2,1)}, bf16[4,2,6,32,128]{4,3,2,1,0:T(8,128)(2,1)S(1)}, u32[]{:S(2)}, u32[]{:S(2)}) collective-permute-start(bf16[4,2,6,32,128]{4,3,2,1,0:T(8,128)(2,1)} %collective-permute-done.12.refs_1_), channel_id=1, source_target_pairs={{0,1},{1,64},{64,65},{65,128},{128,129},{129,192},{192,193},{193,0... | collective-permute-start | bytes 1179656 | tf_op jit(solution)/shard_map/ppermute | solution.py:306
  66.9 21.3 %collective-permute-start.16 = (bf16[4,2,6,32,128]{4,3,2,1,0:T(8,128)(2,1)}, bf16[4,2,6,32,128]{4,3,2,1,0:T(8,128)(2,1)S(1)}, u32[]{:S(2)}, u32[]{:S(2)}) collective-permute-start(bf16[4,2,6,32,128]{4,3,2,1,0:T(8,128)(2,1)} %collective-permute-done.15.refs_8_), channel_id=1, source_target_pairs={{0,193},{1,0},{64,1},{65,64},{128,65},{129,128},{192,129},{193,192... | collective-permute-start | bytes 1179656 | tf_op jit(solution)/shard_map/ppermute | solution.py:306
  70.8 1.0 copy-start.1
  71.8 1.0 copy-start.3
  72.8 1.0 copy-start.5
  96.7 21.5 %collective-permute-start.17 = (f32[8,2,4,32,128]{4,3,2,1,0:T(8,128)S(1)}, f32[8,2,4,32,128]{4,3,2,1,0:T(8,128)S(1)}, u32[]{:S(2)}, u32[]{:S(2)}) collective-permute-start(f32[8,2,4,32,128]{4,3,2,1,0:T(8,128)S(1)} %get-tuple-element.12), channel_id=1, source_target_pairs={{0,8},{8,0},{1,9},{9,1},{2,10},{10,2},{3,11},{11,3},{4,12},{12,4},... | collective-permute-start | bytes 3145736 | tf_op jit(solution)/shard_map/ppermute | solution.py:310
  103.5 11.9 %collective-permute-start.3 = (bf16[4,2,6,32,128]{4,3,2,1,0:T(8,128)(2,1)S(1)}, bf16[4,2,6,32,128]{4,3,2,1,0:T(8,128)(2,1)S(1)}, u32[]{:S(2)}, u32[]{:S(2)}) collective-permute-start(bf16[4,2,6,32,128]{4,3,2,1,0:T(8,128)(2,1)S(1)} %collective-permute-done.2.refs_0_), channel_id=1, source_target_pairs={{0,1},{1,64},{64,65},{65,128},{128,129},{129,192},{192,193},{193,0... | collective-permute-start | bytes 1179656 | tf_op jit(solution)/shard_map/ppermute | solution.py:306
  103.5 12.8 %collective-permute-start.7 = (bf16[4,2,6,32,128]{4,3,2,1,0:T(8,128)(2,1)S(1)}, bf16[4,2,6,32,128]{4,3,2,1,0:T(8,128)(2,1)S(1)}, u32[]{:S(2)}, u32[]{:S(2)}) collective-permute-start(bf16[4,2,6,32,128]{4,3,2,1,0:T(8,128)(2,1)S(1)} %collective-permute-done.6.refs_3_), channel_id=1, source_target_pairs={{0,193},{1,0},{64,1},{65,64},{128,65},{129,128},{192,129},{193,192... | collective-permute-start | bytes 1179656 | tf_op jit(solution)/shard_map/ppermute | solution.py:306
  115.4 2.2 %collective-permute-start.8 = (bf16[4,2,6,32,128]{4,3,2,1,0:T(8,128)(2,1)S(1)}, bf16[4,2,6,32,128]{4,3,2,1,0:T(8,128)(2,1)S(1)}, u32[]{:S(2)}, u32[]{:S(2)}) collective-permute-start(bf16[4,2,6,32,128]{4,3,2,1,0:T(8,128)(2,1)S(1)} %collective-permute-done.3.p0), channel_id=1, source_target_pairs={{0,8},{8,0},{1,9},{9,1},{2,10},{10,2},{3,11},{11,3},{4,12},{12,4},... | collective-permute-start | bytes 1179656 | tf_op jit(solution)/shard_map/ppermute | solution.py:310
  116.3 1.9 %collective-permute-start.9 = (bf16[4,2,6,32,128]{4,3,2,1,0:T(8,128)(2,1)S(1)}, bf16[4,2,6,32,128]{4,3,2,1,0:T(8,128)(2,1)S(1)}, u32[]{:S(2)}, u32[]{:S(2)}) collective-permute-start(bf16[4,2,6,32,128]{4,3,2,1,0:T(8,128)(2,1)S(1)} %collective-permute-done.7.p1), channel_id=1, source_target_pairs={{0,8},{8,0},{1,9},{9,1},{2,10},{10,2},{3,11},{11,3},{4,12},{12,4},... | collective-permute-start | bytes 1179656 | tf_op jit(solution)/shard_map/ppermute | solution.py:310
  (1 other events, 0.7 us)

commit v3 on v2

--- a/solution.py
+++ b/solution.py
@@ -19,6 +19,7 @@
 SCALE = 1.0 / HD**0.5
 EXPONENT = SCALE * 1.4426950408889634
 HIDDEN = -1e30
+GRANT = 16 * 2**20
 VMEM = pl.BlockSpec(memory_space=pltpu.VMEM)
 SMEM = pl.BlockSpec(memory_space=pltpu.SMEM)
 ANY = pl.BlockSpec(memory_space=pl.ANY)
@@ -26,7 +27,8 @@
 
 NEAR = (-2, -1, 0, 1, 2)
 NEXT = (-3, 3)
-FIRST = (0, 40, 56, 72, 88, 96)
+FAR = (4,)
+FIRST = (0, 40, 56, 72, 88)
 N_SLOTS = 96
 QB, KB = 4, 8
 QT, KT = QB * HALF, KB * HALF
@@ -64,17 +66,19 @@
 def scalars(order, documents, zh, zl, c):
     i32 = jnp.int32
     z = zh * 2 + zl
-    offsets = jnp.array((*NEAR, *NEXT, 4, 4, 0, 0, 0), i32)
-    cores = jnp.array((0, 0, 0, 0, 0, 0, 0, 0, 1, 0, 1, 0), i32)
-    sets = jnp.array((0, 0, 0, 0, 0, 1, 1, 2, 2, 3, 3, 4), i32)
-    begins = jnp.array((0, 0, 0, 0, 0, 5, 5, 7, 7, 9, 9, 11), i32)
+    rows = [(o, 0, 0) for o in NEAR]
+    rows += [(o, 0, 1) for o in NEXT]
+    rows += [(o, other, 2) for other in range(2) for o in FAR]
+    rows += [(0, 0, 3), (0, 1, 3), (0, 0, 4)]
+    offsets, cores, sets = (jnp.array(v, i32) for v in zip(*rows, strict=True))
+    begins = jnp.array([FIRST[r[2]] // 8 for r in rows], i32)
     planes = lax.rem(z + offsets + NZ, NZ)
     table = order.reshape(4, 4, 2, 2).transpose(0, 2, 1, 3).reshape(8, 8)
     line = planes // 2 * 2 + lax.rem(cores + c, 2)
     hit = line[:, None] == jnp.arange(8, dtype=i32)[None, :]
     pos = jnp.sum(jnp.where(hit[:, :, None], table[None], 0), axis=1)
     code = (sets[:, None] * 4096 + pos * 2 + lax.rem(planes, 2)[:, None]).reshape(-1)
-    payload = ((jnp.arange(12, dtype=i32) - begins)[:, None] * 8 + jnp.arange(8, dtype=i32)[None, :]).reshape(-1)
+    payload = ((jnp.arange(len(rows), dtype=i32) - begins)[:, None] * 8 + jnp.arange(8, dtype=i32)[None, :]).reshape(-1)
     rank = jnp.sum((code[None, :] < code[:, None]).astype(i32), axis=1)
     slot = jnp.arange(N_SLOTS, dtype=i32)
     hits = rank[None, :] == slot[:, None]
@@ -121,7 +125,7 @@
     return q0, jnp.concatenate([q1, q0], 1), jnp.concatenate([q2, q0], 1), qpos, start
 
 
-def see(sc, kv, first, queries, state, low, high):
+def see(sc, k, v, first, queries, state, low, high):
     q0, q10, q20, qpos, start = queries
     col = lax.broadcasted_iota(jnp.int32, (1, KT), 1)
     ones = jnp.ones((KT, HD), jnp.bfloat16)
@@ -129,7 +133,8 @@
     def step(kt, state):
         top, acc, acc_w = state
         at = first + kt * KB
-        k0, k1, k2, v0, v1, v2 = (gathered(sc, kv, INDEX + at, KB, t) for t in range(6))
+        k0, k1, k2 = (gathered(sc, k, INDEX + at, KB, t) for t in range(3))
+        v0, v1, v2 = (gathered(sc, v, INDEX + at, KB, t) for t in range(3))
         kpos = lookup(sc, BASE + at, KB, col, HALF) + within(col)
         s = lax.dot_general(q0, k0, NT, preferred_element_type=jnp.float32)
         d1 = lax.dot_general(q10, jnp.concatenate([k0, k1], 1), NT, preferred_element_type=jnp.float32)
@@ -204,83 +209,89 @@
         copy.wait()
 
 
-def attend(sc, queries, pieces, key_set, held=None):
-    n = len(pieces)
-    planes = n // 2
+def kernel_state(rows):
+    return pltpu.VMEM((rows, 2, 4, SLICE, HD), jnp.float32)
+
+
+def key_scratch(planes):
+    return [pltpu.VMEM((planes * 8, 2, 3, SLICE, HD), jnp.bfloat16) for _ in range(2)]
+
+
+def plane_copies(refs, k, v):
+    n = len(refs) // 2
+    return [(ref, (k, v)[i // n].at[pl.ds(i % n * 8, 8)]) for i, ref in enumerate(refs)]
+
+
+def estimate(queries, keys):
+    pairs = queries * keys // 4
+    return pl.CostEstimate(flops=pairs * 2560, bytes_accessed=8 * 2**20, transcendentals=pairs)
+
+
+def attend(sc, queries, planes, key_set, held=()):
+    n = len(planes)
 
     def kernel(sc, q_own, q_other, *refs):
         kv_refs, refs = refs[:n], refs[n:]
-        if held is not None:
-            held_refs, refs = refs[:2], refs[2:]
-        out_refs, (kv, q, st, sem) = refs[:2], refs[2:]
-        pairs = [(q_own, q.at[0:8]), (q_other, q.at[8:16])]
-        for i, ref in enumerate(kv_refs):
-            pairs.append((ref, kv.at[i * 4 : i * 4 + 4]))
-        if held is not None:
-            pairs += [(ref, st.at[8 * i : 8 * i + 8]) for i, ref in enumerate(held_refs)]
-        copy_in(pairs, sem)
+        held_refs, refs = refs[: len(held)], refs[len(held) :]
+        out_refs, (k, v, q, st, sem) = refs[:2], refs[2:]
+        before = [(ref, st.at[8 * i : 8 * i + 8]) for i, ref in enumerate(held_refs)]
+        copy_in([(q_own, q.at[0:8]), (q_other, q.at[8:16]), *before, *plane_copies(kv_refs, k, v)], sem)
 
         def tile(qt, _):
-            info = query_tile(sc, q, FIRST[3], qt)
+            at = INDEX + FIRST[3] + qt * QB
             low, high = sc[LOW + key_set * 6 + qt], sc[HIGH + key_set * 6 + qt]
-            at = INDEX + FIRST[3] + qt * QB
 
             def work():
-                before = fresh() if held is None else gather_state(sc, st, at)
-                parts = pack_state(see(sc, kv, FIRST[key_set], info, before, low, high))
+                info = query_tile(sc, q, FIRST[3], qt)
+                state = gather_state(sc, st, at) if held else fresh()
+                parts = pack_state(see(sc, k, v, FIRST[key_set], info, state, low, high))
                 for i in range(QB):
                     for t in range(4):
                         st[sc[at + i], :, t] = parts[t][i * HALF : i * HALF + HALF].reshape(2, SLICE, HD)
 
-            if held is None:
+            if held:
+                pl.when(high > low)(work)
+            else:
                 work()
-            else:
-                pl.when(high > low)(work)
             return 0
 
         lax.fori_loop(0, 4, tile, 0)
         copy_in([(st.at[8 * i : 8 * i + 8], ref) for i, ref in enumerate(out_refs)], sem)
 
     part = jax.ShapeDtypeStruct((8, 2, 4, SLICE, HD), jnp.float32)
-    tiles = 4 * planes * HALF * 8 * 16 * HALF // 10
     return pl.pallas_call(
         kernel,
         out_shape=(part, part),
-        in_specs=[SMEM] + [ANY] * (2 + n + (0 if held is None else 2)),
+        in_specs=[SMEM] + [ANY] * (2 + n + len(held)),
         out_specs=(ANY, ANY),
         scratch_shapes=[
-            pltpu.VMEM((planes * 8, 2, 6, SLICE, HD), jnp.bfloat16),
+            *key_scratch(n // 2),
             pltpu.VMEM((16, 2, 3, SLICE, HD), jnp.bfloat16),
-            pltpu.VMEM((16, 2, 4, SLICE, HD), jnp.float32),
+            kernel_state(16),
             pltpu.SemaphoreType.DMA,
         ],
-        compiler_params=pltpu.CompilerParams(vmem_limit_bytes=28 * 2**20),
-        cost_estimate=pl.CostEstimate(flops=tiles * 2560, bytes_accessed=8 * 2**20, transcendentals=tiles),
-    )(sc, *queries, *pieces, *(held or ()))
-
-
-def finish(sc, query, pieces, held):
-    def kernel(sc, q_ref, p0, p1, p2, p3, own, other, out, kv, q, st_a, st_b, sem):
-        pairs = [(q_ref, q), (own, st_a), (other, st_b)]
-        pairs += [(ref, kv.at[4 * i : 4 * i + 4]) for i, ref in enumerate((p0, p1, p2, p3))]
-        copy_in(pairs, sem)
+        compiler_params=pltpu.CompilerParams(vmem_limit_bytes=GRANT),
+        cost_estimate=estimate(1024, n // 2 * 512),
+    )(sc, *queries, *planes, *held)
+
+
+def finish(sc, query, planes, held):
+    n = len(planes)
+
+    def kernel(sc, q_ref, *refs):
+        kv_refs, held_refs = refs[:n], refs[n : n + 2]
+        out, k, v, q, one, two, sem = refs[n + 2 :]
+        copy_in([(q_ref, q), (held_refs[0], one), (held_refs[1], two), *plane_copies(kv_refs, k, v)], sem)
 
         def tile(qt, _):
+            at = INDEX + FIRST[4] + qt * QB
             info = query_tile(sc, q, FIRST[4], qt)
-            at = INDEX + FIRST[4] + qt * QB
-            state = join_states(gather_state(sc, st_a, at), gather_state(sc, st_b, at))
+            state = join_states(gather_state(sc, one, at), gather_state(sc, two, at))
             low, high = sc[LOW + 2 * 6 + 4 + qt], sc[HIGH + 2 * 6 + 4 + qt]
-            _, acc, acc_w = see(sc, kv, FIRST[2], info, state, low, high)
-            inv = 1.0 / acc[:, 3 * HD :]
-            primal = acc[:, :HD] * inv
-            parts = [primal]
-            for i in (1, 2):
-                mine = slice((i - 1) * QT, i * QT)
-                grad = acc[:, i * HD : (i + 1) * HD] + acc_w[mine, :HD] * SCALE
-                parts.append(grad * inv - (acc_w[mine, HD:] * SCALE * inv) * primal)
+            parts = results(see(sc, k, v, FIRST[2], info, state, low, high))
             for i in range(QB):
-                for t in range(3):
-                    block = parts[t][i * HALF : i * HALF + HALF].reshape(2, SLICE, HD)
+                for t, part in enumerate(parts):
+                    block = part[i * HALF : i * HALF + HALF].reshape(2, SLICE, HD)
                     out[sc[at + i], :, t] = block.astype(jnp.bfloat16)
             return 0
 
@@ -289,17 +300,30 @@
     return pl.pallas_call(
         kernel,
         out_shape=jax.ShapeDtypeStruct((8, 2, 3, SLICE, HD), jnp.bfloat16),
-        in_specs=[SMEM] + [ANY] * 7,
+        in_specs=[SMEM] + [ANY] * (3 + n),
         out_specs=VMEM,
         scratch_shapes=[
-            pltpu.VMEM((16, 2, 6, SLICE, HD), jnp.bfloat16),
+            *key_scratch(n // 2),
             pltpu.VMEM((8, 2, 3, SLICE, HD), jnp.bfloat16),
-            pltpu.VMEM((8, 2, 4, SLICE, HD), jnp.float32),
-            pltpu.VMEM((8, 2, 4, SLICE, HD), jnp.float32),
+            kernel_state(8),
+            kernel_state(8),
             pltpu.SemaphoreType.DMA,
         ],
-        compiler_params=pltpu.CompilerParams(vmem_limit_bytes=28 * 2**20),
-    )(sc, query, *pieces, *held)
+        compiler_params=pltpu.CompilerParams(vmem_limit_bytes=GRANT),
+        cost_estimate=estimate(512, n // 2 * 512),
+    )(sc, query, *planes, *held)
+
+
+def results(state):
+    _, acc, acc_w = state
+    inv = 1.0 / acc[:, 3 * HD :]
+    primal = acc[:, :HD] * inv
+    parts = [primal]
+    for i in (1, 2):
+        mine = slice((i - 1) * QT, i * QT)
+        grad = acc[:, i * HD : (i + 1) * HD] + acc_w[mine, :HD] * SCALE
+        parts.append(grad * inv - (acc_w[mine, HD:] * SCALE * inv) * primal)
+    return parts
 
 
 def hop(block, direction):
@@ -310,25 +334,26 @@
     return lax.ppermute(block, "c", [(0, 1), (1, 0)])
 
 
+def to_heads(array):
+    return lax.all_to_all(split_heads(array), XY, 0, 0).reshape(8, 2, 3, SLICE, HD)
+
+
 def shards(query_set, key_set, value_set, block_order, documents):
-    kv = lax.all_to_all(split_heads(key_set, value_set), XY, 0, 0)
-    kv = kv.reshape(8, 2, 6, SLICE, HD)
-    q = lax.all_to_all(split_heads(query_set), XY, 0, 0).reshape(8, 2, 3, SLICE, HD)
-    pieces = {(half, 0): kv[4 * half : 4 * half + 4] for half in range(2)}
-    ups = [pieces[0, 0], pieces[1, 0]]
-    downs = [pieces[0, 0], pieces[1, 0]]
-    for step in range(1, 5):
-        for half in range(2):
-            if step < 4 or half == 0:
-                ups[half] = pieces[half, -step] = hop(ups[half], 1)
-            if step < 4 or half == 1:
-                downs[half] = pieces[half, step] = hop(downs[half], -1)
+    planes = {0: [to_heads(key_set), to_heads(value_set)]}
+    for step in range(1, 4):
+        planes[-step] = [hop(p, 1) for p in planes[1 - step]]
+        planes[step] = [hop(p, -1) for p in planes[step - 1]]
+    query_set, _ = lax.optimization_barrier((query_set, planes[1][0]))
+    q = to_heads(query_set)
     sc = scalars(block_order, documents, *(lax.axis_index(a) for a in ("zh", "zl", "c")))
     queries = (q, swap_cores(q))
-    state = attend(sc, queries, [pieces[half, o] for o in NEAR for half in range(2)], 0)
-    own, other = attend(sc, queries, [pieces[half, o] for o in NEXT for half in range(2)], 1, state)
-    far = [pieces[0, -4], pieces[1, 4]]
-    done = finish(sc, q, [*far, *(swap_cores(p) for p in far)], (own, swap_cores(other)))
+    state = attend(sc, queries, [planes[o][t] for t in range(2) for o in NEAR], 0)
+    state, planes[-3][0], planes[3][1] = lax.optimization_barrier((state, planes[-3][0], planes[3][1]))
+    far = [hop(planes[-3][0], 1), hop(planes[3][1], -1)]
+    own, other = attend(sc, queries, [planes[o][t] for t in range(2) for o in NEXT], 1, state)
+    own, other, far = lax.optimization_barrier((own, other, far))
+    far = [p for f in far for p in (f, swap_cores(f))]
+    done = finish(sc, q, far, (own, swap_cores(other)))
     done = lax.all_to_all(done.reshape(HEADS, 3, SLICE, HD), XY, 0, 0)
     return join_heads(done)
 

time: 143 us -> 126 us (0.88)
  waiting for transfers between devices: 32.7 us -> 11.5 us
  starting transfers between devices: 46.3 us -> 53.5 us
  local copies, waits for them, and re-layouts: 9.98 us -> 5.24 us
  blocking collectives: 16.3 us -> 18.2 us
    ppermute x14, waiting for transfers between devices: 23.6 us -> 0.04 us  [hop(): lax.ppermute(block, Z, [(i, (i + direction) % NZ) for i in range(NZ)])]
    unnamed x26 -> x14, local copies, waits for them, and re-layouts: 7.83 us -> 2.6 us
    ppermute x14, starting transfers between devices: 20.9 us -> 26.1 us  [hop(): lax.ppermute(block, Z, [(i, (i + direction) % NZ) for i in range(NZ)])]
    all_to_all x2 -> x3, starting transfers between devices: 11.4 us -> 15.6 us  [to_heads(): lax.all_to_all(split_heads(array), XY, 0, 0).reshape(8, 2, 3, SLICE, HD)]
    ppermute x4, starting transfers between devices: 14 us -> 11.8 us  [swap_cores(): return lax.ppermute(block, 'c', [(0, 1), (1, 0)])]
    all_to_all x1, blocking collectives: 16.3 us -> 18.2 us  [shards(): done = lax.all_to_all(done.reshape(HEADS, 3, SLICE, HD), XY, 0, 0)]
    pallas_call x2, Pallas kernels: 22.9 us -> 21 us  [attend(): pl.pallas_call(kernel, out_shape=(part, part), in_specs=[SMEM] + [ANY] *...]
    pallas_call x2 -> x3, Pallas kernels: 3.97 us -> 5.43 us  [split_heads(): pl.pallas_call(kernel, out_shape=jax.ShapeDtypeStruct((HEADS, 3 * len(arr...]
  transfers between devices with their start and end apart: 20 -> 21, of which waited for: 7 -> 5; matrix products, arithmetic and copies ran while one was open for 3% -> 4% of each run, Pallas kernels for 11% -> 20%
where the time goes in v3:
time: 126 us; the launch traced here: 125 us
  starting transfers between devices  53.5 us (42%)
  Pallas kernels  33.9 us (27%)
  blocking collectives  18.2 us (14%)
  waiting for transfers between devices  11.5 us (9%)
  local copies, waits for them, and re-layouts  5.24 us (4%)
  other arithmetic  2.85 us (2%)
    ppermute x14, starting transfers between devices, hop(): lax.ppermute(block, Z, [(i, (i + direction) % NZ) for i in range(NZ)])  26.1 us
    pallas_call x2, Pallas kernels, attend(): pl.pallas_call(kernel, out_shape=(part, part), in_specs=[SMEM] + [ANY] *...  21 us
    all_to_all x1, blocking collectives, shards(): done = lax.all_to_all(done.reshape(HEADS, 3, SLICE, HD), XY, 0, 0)  18.2 us
    all_to_all x3, starting transfers between devices, to_heads(): lax.all_to_all(split_heads(array), XY, 0, 0).reshape(8, 2, 3, SLICE, HD)  15.6 us
    ppermute x4, starting transfers between devices, swap_cores(): return lax.ppermute(block, 'c', [(0, 1), (1, 0)])  11.8 us
    all_to_all x3, waiting for transfers between devices, to_heads(): lax.all_to_all(split_heads(array), XY, 0, 0).reshape(8, 2, 3, SLICE, HD)  8.52 us
    pallas_call x1, Pallas kernels, finish(): pl.pallas_call(kernel, out_shape=jax.ShapeDtypeStruct((8, 2, 3, SLICE, HD...  5.63 us
    pallas_call x3, Pallas kernels, split_heads(): pl.pallas_call(kernel, out_shape=jax.ShapeDtypeStruct((HEADS, 3 * len(arr...  5.43 us
  transfers between devices with their start and end apart: 21, of which 5 were waited for; matrix products, arithmetic and copies ran while one was open for 4% of the time, Pallas kernels for 20%

profile of v3, /device:TPU:1, one launch (start us, length us, event | category | flops | bytes accessed | tf_op | source)
XLA Modules:
  0.0 125.4 jit_solution(17773607703823492059)
XLA Ops:
  0.0 1.8 %shard_map.91 = bf16[16,3,32,128]{3,2,1,0:T(8,128)(2,1)} custom-call(bf16[3,32,2048]{2,1,0:T(8,128)(2,1)} %refs_0_.2), custom_call_target="tpu_custom_call" | custom-call | tf_op jit(solution)/shard_map/pallas_call | solution.py:45
  1.8 7.6 %all-to-all-start = ((bf16[16,3,32,128]{3,2,1,0:T(8,128)(2,1)}), bf16[16,3,32,128]{3,2,1,0:T(8,128)(2,1)S(1)}, u32[]{:S(2)}, u32[]{:S(2)}) async-start(bf16[16,3,32,128]{3,2,1,0:T(8,128)(2,1)} %shard_map.91), calls=%async_computation | async-start | bytes 786432 | tf_op jit(solution)/shard_map/all_to_all | solution.py:338
  9.4 0.6 copy-done.5
  10.1 0.6 copy-done.1
  11.1 0.6 copy-done.3
  11.7 0.6 copy-done.2
  12.7 1.8 %shard_map.93 = bf16[16,3,32,128]{3,2,1,0:T(8,128)(2,1)} custom-call(bf16[3,32,2048]{2,1,0:T(8,128)(2,1)} %refs_0_.4), custom_call_target="tpu_custom_call" | custom-call | tf_op jit(solution)/shard_map/pallas_call | solution.py:45
  14.7 3.9 %all-to-all-done = bf16[16,3,32,128]{3,2,1,0:T(8,128)(2,1)S(1)} async-done(((bf16[16,3,32,128]{3,2,1,0:T(8,128)(2,1)}), bf16[16,3,32,128]{3,2,1,0:T(8,128)(2,1)S(1)}, u32[]{:S(2)}, u32[]{:S(2)}) %all-to-all-start) | async-done | bytes 393248 | tf_op jit(solution)/shard_map/all_to_all | solution.py:338
  18.6 3.7 %all-to-all-start.2 = ((bf16[16,3,32,128]{3,2,1,0:T(8,128)(2,1)}), bf16[16,3,32,128]{3,2,1,0:T(8,128)(2,1)S(1)}, u32[]{:S(2)}, u32[]{:S(2)}) async-start(bf16[16,3,32,128]{3,2,1,0:T(8,128)(2,1)} %shard_map.93), calls=%async_computation.2 | async-start | bytes 786432 | tf_op jit(solution)/shard_map/all_to_all | solution.py:338
  22.5 5.7 %collective-permute-start = (bf16[8,2,3,32,128]{4,3,2,1,0:T(8,128)(2,1)S(1)}, bf16[8,2,3,32,128]{4,3,2,1,0:T(8,128)(2,1)S(1)}, u32[]{:S(2)}, u32[]{:S(2)}) collective-permute-start(bf16[8,2,3,32,128]{4,3,2,1,0:T(8,128)(2,1)S(1)} %bitcast.10), channel_id=1, source_target_pairs={{0,193},{1,0},{64,1},{65,64},{128,65},{129,128},{192,129},{193,192... | collective-permute-start | bytes 1179656 | tf_op jit(solution)/shard_map/ppermute | solution.py:330
  28.1 2.4 %all-to-all-done.2 = bf16[16,3,32,128]{3,2,1,0:T(8,128)(2,1)S(1)} async-done(((bf16[16,3,32,128]{3,2,1,0:T(8,128)(2,1)}), bf16[16,3,32,128]{3,2,1,0:T(8,128)(2,1)S(1)}, u32[]{:S(2)}, u32[]{:S(2)}) %all-to-all-start.2) | async-done | bytes 393248 | tf_op jit(solution)/shard_map/all_to_all | solution.py:338
  30.5 5.6 %collective-permute-start.7 = (bf16[8,2,3,32,128]{4,3,2,1,0:T(8,128)(2,1)S(1)}, bf16[8,2,3,32,128]{4,3,2,1,0:T(8,128)(2,1)S(1)}, u32[]{:S(2)}, u32[]{:S(2)}) collective-permute-start(bf16[8,2,3,32,128]{4,3,2,1,0:T(8,128)(2,1)S(1)} %bitcast.13), channel_id=1, source_target_pairs={{0,193},{1,0},{64,1},{65,64},{128,65},{129,128},{192,129},{193,192... | collective-permute-start | bytes 1179656 | tf_op jit(solution)/shard_map/ppermute | solution.py:330
  36.6 1.8 %shard_map.92 = bf16[16,3,32,128]{3,2,1,0:T(8,128)(2,1)} custom-call(bf16[3,32,2048]{2,1,0:T(8,128)(2,1)} %refs_0_.3), custom_call_target="tpu_custom_call" | custom-call | tf_op jit(solution)/shard_map/pallas_call | solution.py:45
  38.5 4.4 %all-to-all-start.1 = ((bf16[16,3,32,128]{3,2,1,0:T(8,128)(2,1)}), bf16[16,3,32,128]{3,2,1,0:T(8,128)(2,1)S(1)}, u32[]{:S(2)}, u32[]{:S(2)}) async-start(bf16[16,3,32,128]{3,2,1,0:T(8,128)(2,1)} %shard_map.92), calls=%async_computation.1 | async-start | bytes 786432 | tf_op jit(solution)/shard_map/all_to_all | solution.py:338
  42.9 3.5 %collective-permute-start.8 = (bf16[8,2,3,32,128]{4,3,2,1,0:T(8,128)(2,1)S(1)}, bf16[8,2,3,32,128]{4,3,2,1,0:T(8,128)(2,1)}, u32[]{:S(2)}, u32[]{:S(2)}) collective-permute-start(bf16[8,2,3,32,128]{4,3,2,1,0:T(8,128)(2,1)S(1)} %collective-permute-done.7.refs_8_), channel_id=1, source_target_pairs={{0,193},{1,0},{64,1},{65,64},{128,65},{129,128},{192,129},{193,192... | collective-permute-start | bytes 1179656 | tf_op jit(solution)/shard_map/ppermute | solution.py:330
  46.6 0.7 sub.50
  47.3 1.4 %collective-permute-start.4 = (bf16[8,2,3,32,128]{4,3,2,1,0:T(8,128)(2,1)S(1)}, bf16[8,2,3,32,128]{4,3,2,1,0:T(8,128)(2,1)}, u32[]{:S(2)}, u32[]{:S(2)}) collective-permute-start(bf16[8,2,3,32,128]{4,3,2,1,0:T(8,128)(2,1)S(1)} %collective-permute-done.refs_3_), channel_id=1, source_target_pairs={{0,193},{1,0},{64,1},{65,64},{128,65},{129,128},{192,129},{193,192... | collective-permute-start | bytes 1179656 | tf_op jit(solution)/shard_map/ppermute | solution.py:330
  48.8 2.3 %all-to-all-done.1 = bf16[16,3,32,128]{3,2,1,0:T(8,128)(2,1)S(1)} async-done(((bf16[16,3,32,128]{3,2,1,0:T(8,128)(2,1)}), bf16[16,3,32,128]{3,2,1,0:T(8,128)(2,1)S(1)}, u32[]{:S(2)}, u32[]{:S(2)}) %all-to-all-start.1) | async-done | bytes 393248 | tf_op jit(solution)/shard_map/all_to_all | solution.py:338
  51.1 7.2 %collective-permute-start.1 = (bf16[8,2,3,32,128]{4,3,2,1,0:T(8,128)(2,1)S(1)}, bf16[8,2,3,32,128]{4,3,2,1,0:T(8,128)(2,1)S(1)}, u32[]{:S(2)}, u32[]{:S(2)}) collective-permute-start(bf16[8,2,3,32,128]{4,3,2,1,0:T(8,128)(2,1)S(1)} %bitcast.5), channel_id=1, source_target_pairs={{0,8},{8,0},{1,9},{9,1},{2,10},{10,2},{3,11},{11,3},{4,12},{12,4},... | collective-permute-start | bytes 1179656 | tf_op jit(solution)/shard_map/ppermute | solution.py:334
  58.2 3.4 %collective-permute-start.10 = (bf16[8,2,3,32,128]{4,3,2,1,0:T(8,128)(2,1)}, bf16[8,2,3,32,128]{4,3,2,1,0:T(8,128)(2,1)S(1)}, u32[]{:S(2)}, u32[]{:S(2)}) collective-permute-start(bf16[8,2,3,32,128]{4,3,2,1,0:T(8,128)(2,1)} %collective-permute-done.8.refs_9_), channel_id=1, source_target_pairs={{0,193},{1,0},{64,1},{65,64},{128,65},{129,128},{192,129},{193,192... | collective-permute-start | bytes 1179656 | tf_op jit(solution)/shard_map/ppermute | solution.py:330
  62.2 0.6 reduce_sum.71
  62.8 1.2 and_select_fusion.1
  64.0 0.8 concatenate.3.sc
  64.8 2.7 %collective-permute-start.11 = (bf16[8,2,3,32,128]{4,3,2,1,0:T(8,128)(2,1)}, bf16[8,2,3,32,128]{4,3,2,1,0:T(8,128)(2,1)S(1)}, u32[]{:S(2)}, u32[]{:S(2)}) collective-permute-start(bf16[8,2,3,32,128]{4,3,2,1,0:T(8,128)(2,1)} %collective-permute-done.4.refs_4_), channel_id=1, source_target_pairs={{0,193},{1,0},{64,1},{65,64},{128,65},{129,128},{192,129},{193,192... | collective-permute-start | bytes 1179656 | tf_op jit(solution)/shard_map/ppermute | solution.py:330
  67.5 11.6 %shard_map.94 = (f32[8,2,4,32,128]{4,3,2,1,0:T(8,128)S(1)}, f32[8,2,4,32,128]{4,3,2,1,0:T(8,128)S(1)}) custom-call(s32[231]{0:T(256)S(1)} %concatenate.3.sc, bf16[8,2,3,32,128]{4,3,2,1,0:T(8,128)(2,1)S(1)} %bitcast.6, bf16[8,2,3,32,128]{4,3,2,1,0:T(8,128)(2,1)S(1)} %collective-permute-done.1.q_other, ...), custom_call_target="tpu_custom_call" | custom-call | flops 1677721600 | bytes 8388608 | tf_op jit(solution)/shard_map/pallas_call | solution.py:262
  79.2 3.6 %collective-permute-start.14 = (bf16[8,2,3,32,128]{4,3,2,1,0:T(8,128)(2,1)S(1)}, bf16[8,2,3,32,128]{4,3,2,1,0:T(8,128)(2,1)S(1)}, u32[]{:S(2)}, u32[]{:S(2)}) collective-permute-start(bf16[8,2,3,32,128]{4,3,2,1,0:T(8,128)(2,1)S(1)} %collective-permute-done.10.refs_3_), channel_id=1, source_target_pairs={{0,193},{1,0},{64,1},{65,64},{128,65},{129,128},{192,129},{193,192... | collective-permute-start | bytes 1179656 | tf_op jit(solution)/shard_map/ppermute | solution.py:330
  82.8 9.4 %shard_map.95 = (f32[8,2,4,32,128]{4,3,2,1,0:T(8,128)S(1)}, f32[8,2,4,32,128]{4,3,2,1,0:T(8,128)S(1)}) custom-call(s32[231]{0:T(256)S(1)} %concatenate.3.sc, bf16[8,2,3,32,128]{4,3,2,1,0:T(8,128)(2,1)S(1)} %bitcast.7, bf16[8,2,3,32,128]{4,3,2,1,0:T(8,128)(2,1)S(1)} %collective-permute-done.1.q_other, ...), custom_call_target="tpu_custom_call" | custom-call | flops 671088640 | bytes 8388608 | tf_op jit(solution)/shard_map/pallas_call | solution.py:262
  92.3 4.1 %collective-permute-start.17 = (f32[8,2,4,32,128]{4,3,2,1,0:T(8,128)S(1)}, f32[8,2,4,32,128]{4,3,2,1,0:T(8,128)S(1)}, u32[]{:S(2)}, u32[]{:S(2)}) collective-permute-start(f32[8,2,4,32,128]{4,3,2,1,0:T(8,128)S(1)} %get-tuple-element.30), channel_id=1, source_target_pairs={{0,8},{8,0},{1,9},{9,1},{2,10},{10,2},{3,11},{11,3},{4,12},{12,4},... | collective-permute-start | bytes 3145736 | tf_op jit(solution)/shard_map/ppermute | solution.py:334
  96.9 2.3 %collective-permute-done.15.refs_1_ = bf16[8,2,3,32,128]{4,3,2,1,0:T(8,128)(2,1)S(1)} collective-permute-done((bf16[8,2,3,32,128]{4,3,2,1,0:T(8,128)(2,1)S(1)}, bf16[8,2,3,32,128]{4,3,2,1,0:T(8,128)(2,1)S(1)}, u32[]{:S(2)}, u32[]{:S(2)}) %collective-permute-start.15) | collective-permute-done | bytes 393248 | tf_op jit(solution)/shard_map/ppermute | solution.py:334
  99.8 5.6 %shard_map.96 = bf16[8,2,3,32,128]{4,3,2,1,0:T(8,128)(2,1)S(1)} custom-call(s32[231]{0:T(256)S(1)} %concatenate.3.sc, bf16[8,2,3,32,128]{4,3,2,1,0:T(8,128)(2,1)S(1)} %bitcast.8, bf16[8,2,3,32,128]{4,3,2,1,0:T(8,128)(2,1)S(1)} %collective-permute-done.13.refs_0_, bf16[8,2,3,32,128]{4,3,2,1,0:T(8,128)(2,1)S(1)} %collective-permute-done.15.refs_1_, ...), custom_call_target="tpu_custom_call" | custom-call | flops 335544320 | bytes 8388608 | tf_op jit(solution)/shard_map/pallas_call | solution.py:300
  105.4 18.2 %all_to_all.20.ref = bf16[16,3,32,128]{3,2,1,0:T(8,128)(2,1)} all-to-all(bf16[16,3,32,128]{3,2,1,0:T(8,128)(2,1)S(1)} %bitcast.9), channel_id=1, replica_groups=mesh['zh'=4,'y'=4,'c'=2,'xh'=2,'xl'=2,'zl'=2] {'y','xh','xl'}, dimensions={0} | all-to-all | bytes 786432 | tf_op jit(solution)/shard_map/all_to_all | solution.py:357
  123.6 1.8 %shard_map.97 = bf16[3,32,2048]{2,1,0:T(8,128)(2,1)} custom-call(bf16[16,3,32,128]{3,2,1,0:T(8,128)(2,1)} %all_to_all.20.ref), custom_call_target="tpu_custom_call" | custom-call | tf_op jit(solution)/shard_map/pallas_call | solution.py:58
  (61 shorter events, 3.8 us)
Async XLA Ops:
  1.8 16.8 %all-to-all-start = ((bf16[16,3,32,128]{3,2,1,0:T(8,128)(2,1)}), bf16[16,3,32,128]{3,2,1,0:T(8,128)(2,1)S(1)}, u32[]{:S(2)}, u32[]{:S(2)}) async-start(bf16[16,3,32,128]{3,2,1,0:T(8,128)(2,1)} %shard_map.91), calls=%async_computation | async-start | bytes 786432 | tf_op jit(solution)/shard_map/all_to_all | solution.py:338
  9.4 0.7 copy-start.5
  9.4 0.7 copy-start.6
  10.1 0.7 copy-start.1
  11.1 0.7 copy-start.3
  11.7 0.7 copy-start.2
  18.6 17.5 %copy-start = (s32[8192]{0:T(1024)S(1)}, s32[8192]{0:T(1024)}, u32[]{:S(2)}) copy-start(s32[8192]{0:T(1024)} %param.13) | copy-start | bytes 98308
  18.6 11.9 %all-to-all-start.2 = ((bf16[16,3,32,128]{3,2,1,0:T(8,128)(2,1)}), bf16[16,3,32,128]{3,2,1,0:T(8,128)(2,1)S(1)}, u32[]{:S(2)}, u32[]{:S(2)}) async-start(bf16[16,3,32,128]{3,2,1,0:T(8,128)(2,1)} %shard_map.93), calls=%async_computation.2 | async-start | bytes 786432 | tf_op jit(solution)/shard_map/all_to_all | solution.py:338
  22.5 14.1 %collective-permute-start = (bf16[8,2,3,32,128]{4,3,2,1,0:T(8,128)(2,1)S(1)}, bf16[8,2,3,32,128]{4,3,2,1,0:T(8,128)(2,1)S(1)}, u32[]{:S(2)}, u32[]{:S(2)}) collective-permute-start(bf16[8,2,3,32,128]{4,3,2,1,0:T(8,128)(2,1)S(1)} %bitcast.10), channel_id=1, source_target_pairs={{0,193},{1,0},{64,1},{65,64},{128,65},{129,128},{192,129},{193,192... | collective-permute-start | bytes 1179656 | tf_op jit(solution)/shard_map/ppermute | solution.py:330
  28.1 14.7 %collective-permute-start.2 = (bf16[8,2,3,32,128]{4,3,2,1,0:T(8,128)(2,1)S(1)}, bf16[8,2,3,32,128]{4,3,2,1,0:T(8,128)(2,1)S(1)}, u32[]{:S(2)}, u32[]{:S(2)}) collective-permute-start(bf16[8,2,3,32,128]{4,3,2,1,0:T(8,128)(2,1)S(1)} %bitcast.11), channel_id=1, source_target_pairs={{0,1},{1,64},{64,65},{65,128},{128,129},{129,192},{192,193},{193,0... | collective-permute-start | bytes 1179656 | tf_op jit(solution)/shard_map/ppermute | solution.py:330
  30.5 12.4 %collective-permute-start.7 = (bf16[8,2,3,32,128]{4,3,2,1,0:T(8,128)(2,1)S(1)}, bf16[8,2,3,32,128]{4,3,2,1,0:T(8,128)(2,1)S(1)}, u32[]{:S(2)}, u32[]{:S(2)}) collective-permute-start(bf16[8,2,3,32,128]{4,3,2,1,0:T(8,128)(2,1)S(1)} %bitcast.13), channel_id=1, source_target_pairs={{0,193},{1,0},{64,1},{65,64},{128,65},{129,128},{192,129},{193,192... | collective-permute-start | bytes 1179656 | tf_op jit(solution)/shard_map/ppermute | solution.py:330
  36.6 12.1 %collective-permute-start.5 = (bf16[8,2,3,32,128]{4,3,2,1,0:T(8,128)(2,1)S(1)}, bf16[8,2,3,32,128]{4,3,2,1,0:T(8,128)(2,1)}, u32[]{:S(2)}, u32[]{:S(2)}) collective-permute-start(bf16[8,2,3,32,128]{4,3,2,1,0:T(8,128)(2,1)S(1)} %bitcast.14), channel_id=1, source_target_pairs={{0,1},{1,64},{64,65},{65,128},{128,129},{129,192},{192,193},{193,0... | collective-permute-start | bytes 1179656 | tf_op jit(solution)/shard_map/ppermute | solution.py:330
  38.5 12.6 %all-to-all-start.1 = ((bf16[16,3,32,128]{3,2,1,0:T(8,128)(2,1)}), bf16[16,3,32,128]{3,2,1,0:T(8,128)(2,1)S(1)}, u32[]{:S(2)}, u32[]{:S(2)}) async-start(bf16[16,3,32,128]{3,2,1,0:T(8,128)(2,1)} %shard_map.92), calls=%async_computation.1 | async-start | bytes 786432 | tf_op jit(solution)/shard_map/all_to_all | solution.py:338
  42.8 18.8 %collective-permute-start.3 = (bf16[8,2,3,32,128]{4,3,2,1,0:T(8,128)(2,1)S(1)}, bf16[8,2,3,32,128]{4,3,2,1,0:T(8,128)(2,1)}, u32[]{:S(2)}, u32[]{:S(2)}) collective-permute-start(bf16[8,2,3,32,128]{4,3,2,1,0:T(8,128)(2,1)S(1)} %collective-permute-done.2.refs_1_), channel_id=1, source_target_pairs={{0,1},{1,64},{64,65},{65,128},{128,129},{129,192},{192,193},{193,0... | collective-permute-start | bytes 1179656 | tf_op jit(solution)/shard_map/ppermute | solution.py:330
  42.9 15.3 %collective-permute-start.8 = (bf16[8,2,3,32,128]{4,3,2,1,0:T(8,128)(2,1)S(1)}, bf16[8,2,3,32,128]{4,3,2,1,0:T(8,128)(2,1)}, u32[]{:S(2)}, u32[]{:S(2)}) collective-permute-start(bf16[8,2,3,32,128]{4,3,2,1,0:T(8,128)(2,1)S(1)} %collective-permute-done.7.refs_8_), channel_id=1, source_target_pairs={{0,193},{1,0},{64,1},{65,64},{128,65},{129,128},{192,129},{193,192... | collective-permute-start | bytes 1179656 | tf_op jit(solution)/shard_map/ppermute | solution.py:330
  47.3 17.5 %collective-permute-start.4 = (bf16[8,2,3,32,128]{4,3,2,1,0:T(8,128)(2,1)S(1)}, bf16[8,2,3,32,128]{4,3,2,1,0:T(8,128)(2,1)}, u32[]{:S(2)}, u32[]{:S(2)}) collective-permute-start(bf16[8,2,3,32,128]{4,3,2,1,0:T(8,128)(2,1)S(1)} %collective-permute-done.refs_3_), channel_id=1, source_target_pairs={{0,193},{1,0},{64,1},{65,64},{128,65},{129,128},{192,129},{193,192... | collective-permute-start | bytes 1179656 | tf_op jit(solution)/shard_map/ppermute | solution.py:330
  48.7 18.8 %collective-permute-start.6 = (bf16[8,2,3,32,128]{4,3,2,1,0:T(8,128)(2,1)}, bf16[8,2,3,32,128]{4,3,2,1,0:T(8,128)(2,1)}, u32[]{:S(2)}, u32[]{:S(2)}) collective-permute-start(bf16[8,2,3,32,128]{4,3,2,1,0:T(8,128)(2,1)} %collective-permute-done.5.refs_6_), channel_id=1, source_target_pairs={{0,1},{1,64},{64,65},{65,128},{128,129},{129,192},{192,193},{193,0... | collective-permute-start | bytes 1179656 | tf_op jit(solution)/shard_map/ppermute | solution.py:330
  51.1 10.6 %copy-start.4 = (s32[18]{0:T(128)S(1)}, s32[18]{0:T(128)}, u32[]{:S(2)}) copy-start(s32[18]{0:T(128)} %sub.50) | copy-start | bytes 220
  51.1 16.4 %collective-permute-start.1 = (bf16[8,2,3,32,128]{4,3,2,1,0:T(8,128)(2,1)S(1)}, bf16[8,2,3,32,128]{4,3,2,1,0:T(8,128)(2,1)S(1)}, u32[]{:S(2)}, u32[]{:S(2)}) collective-permute-start(bf16[8,2,3,32,128]{4,3,2,1,0:T(8,128)(2,1)S(1)} %bitcast.5), channel_id=1, source_target_pairs={{0,8},{8,0},{1,9},{9,1},{2,10},{10,2},{3,11},{11,3},{4,12},{12,4},... | collective-permute-start | bytes 1179656 | tf_op jit(solution)/shard_map/ppermute | solution.py:334
  58.2 20.9 %collective-permute-start.10 = (bf16[8,2,3,32,128]{4,3,2,1,0:T(8,128)(2,1)}, bf16[8,2,3,32,128]{4,3,2,1,0:T(8,128)(2,1)S(1)}, u32[]{:S(2)}, u32[]{:S(2)}) collective-permute-start(bf16[8,2,3,32,128]{4,3,2,1,0:T(8,128)(2,1)} %collective-permute-done.8.refs_9_), channel_id=1, source_target_pairs={{0,193},{1,0},{64,1},{65,64},{128,65},{129,128},{192,129},{193,192... | collective-permute-start | bytes 1179656 | tf_op jit(solution)/shard_map/ppermute | solution.py:330
  61.6 17.5 %collective-permute-start.9 = (bf16[8,2,3,32,128]{4,3,2,1,0:T(8,128)(2,1)}, bf16[8,2,3,32,128]{4,3,2,1,0:T(8,128)(2,1)S(1)}, u32[]{:S(2)}, u32[]{:S(2)}) collective-permute-start(bf16[8,2,3,32,128]{4,3,2,1,0:T(8,128)(2,1)} %collective-permute-done.3.refs_0_), channel_id=1, source_target_pairs={{0,1},{1,64},{64,65},{65,128},{128,129},{129,192},{192,193},{193,0... | collective-permute-start | bytes 1179656 | tf_op jit(solution)/shard_map/ppermute | solution.py:330
  64.8 18.1 %collective-permute-start.11 = (bf16[8,2,3,32,128]{4,3,2,1,0:T(8,128)(2,1)}, bf16[8,2,3,32,128]{4,3,2,1,0:T(8,128)(2,1)S(1)}, u32[]{:S(2)}, u32[]{:S(2)}) collective-permute-start(bf16[8,2,3,32,128]{4,3,2,1,0:T(8,128)(2,1)} %collective-permute-done.4.refs_4_), channel_id=1, source_target_pairs={{0,193},{1,0},{64,1},{65,64},{128,65},{129,128},{192,129},{193,192... | collective-permute-start | bytes 1179656 | tf_op jit(solution)/shard_map/ppermute | solution.py:330
  67.5 15.4 %collective-permute-start.12 = (bf16[8,2,3,32,128]{4,3,2,1,0:T(8,128)(2,1)}, bf16[8,2,3,32,128]{4,3,2,1,0:T(8,128)(2,1)S(1)}, u32[]{:S(2)}, u32[]{:S(2)}) collective-permute-start(bf16[8,2,3,32,128]{4,3,2,1,0:T(8,128)(2,1)} %collective-permute-done.6.refs_5_), channel_id=1, source_target_pairs={{0,1},{1,64},{64,65},{65,128},{128,129},{129,192},{192,193},{193,0... | collective-permute-start | bytes 1179656 | tf_op jit(solution)/shard_map/ppermute | solution.py:330
  79.1 13.1 %collective-permute-start.13 = (bf16[8,2,3,32,128]{4,3,2,1,0:T(8,128)(2,1)S(1)}, bf16[8,2,3,32,128]{4,3,2,1,0:T(8,128)(2,1)S(1)}, u32[]{:S(2)}, u32[]{:S(2)}) collective-permute-start(bf16[8,2,3,32,128]{4,3,2,1,0:T(8,128)(2,1)S(1)} %collective-permute-done.9.refs_0_), channel_id=1, source_target_pairs={{0,1},{1,64},{64,65},{65,128},{128,129},{129,192},{192,193},{193,0... | collective-permute-start | bytes 1179656 | tf_op jit(solution)/shard_map/ppermute | solution.py:330
  79.2 13.0 %collective-permute-start.14 = (bf16[8,2,3,32,128]{4,3,2,1,0:T(8,128)(2,1)S(1)}, bf16[8,2,3,32,128]{4,3,2,1,0:T(8,128)(2,1)S(1)}, u32[]{:S(2)}, u32[]{:S(2)}) collective-permute-start(bf16[8,2,3,32,128]{4,3,2,1,0:T(8,128)(2,1)S(1)} %collective-permute-done.10.refs_3_), channel_id=1, source_target_pairs={{0,193},{1,0},{64,1},{65,64},{128,65},{129,128},{192,129},{193,192... | collective-permute-start | bytes 1179656 | tf_op jit(solution)/shard_map/ppermute | solution.py:330
  92.3 7.5 %collective-permute-start.17 = (f32[8,2,4,32,128]{4,3,2,1,0:T(8,128)S(1)}, f32[8,2,4,32,128]{4,3,2,1,0:T(8,128)S(1)}, u32[]{:S(2)}, u32[]{:S(2)}) collective-permute-start(f32[8,2,4,32,128]{4,3,2,1,0:T(8,128)S(1)} %get-tuple-element.30), channel_id=1, source_target_pairs={{0,8},{8,0},{1,9},{9,1},{2,10},{10,2},{3,11},{11,3},{4,12},{12,4},... | collective-permute-start | bytes 3145736 | tf_op jit(solution)/shard_map/ppermute | solution.py:334
  96.4 2.8 %collective-permute-start.15 = (bf16[8,2,3,32,128]{4,3,2,1,0:T(8,128)(2,1)S(1)}, bf16[8,2,3,32,128]{4,3,2,1,0:T(8,128)(2,1)S(1)}, u32[]{:S(2)}, u32[]{:S(2)}) collective-permute-start(bf16[8,2,3,32,128]{4,3,2,1,0:T(8,128)(2,1)S(1)} %collective-permute-done.13.refs_0_), channel_id=1, source_target_pairs={{0,8},{8,0},{1,9},{9,1},{2,10},{10,2},{3,11},{11,3},{4,12},{12,4},... | collective-permute-start | bytes 1179656 | tf_op jit(solution)/shard_map/ppermute | solution.py:334
  96.5 3.3 %collective-permute-start.16 = (bf16[8,2,3,32,128]{4,3,2,1,0:T(8,128)(2,1)S(1)}, bf16[8,2,3,32,128]{4,3,2,1,0:T(8,128)(2,1)S(1)}, u32[]{:S(2)}, u32[]{:S(2)}) collective-permute-start(bf16[8,2,3,32,128]{4,3,2,1,0:T(8,128)(2,1)S(1)} %collective-permute-done.14.refs_2_), channel_id=1, source_target_pairs={{0,8},{8,0},{1,9},{9,1},{2,10},{10,2},{3,11},{11,3},{4,12},{12,4},... | collective-permute-start | bytes 1179656 | tf_op jit(solution)/shard_map/ppermute | solution.py:334

commit v4 on v3

--- a/solution.py
+++ b/solution.py
@@ -125,7 +125,7 @@
     return q0, jnp.concatenate([q1, q0], 1), jnp.concatenate([q2, q0], 1), qpos, start
 
 
-def see(sc, k, v, first, queries, state, low, high):
+def see(sc, kv, first, queries, state, low, high):
     q0, q10, q20, qpos, start = queries
     col = lax.broadcasted_iota(jnp.int32, (1, KT), 1)
     ones = jnp.ones((KT, HD), jnp.bfloat16)
@@ -133,8 +133,7 @@
     def step(kt, state):
         top, acc, acc_w = state
         at = first + kt * KB
-        k0, k1, k2 = (gathered(sc, k, INDEX + at, KB, t) for t in range(3))
-        v0, v1, v2 = (gathered(sc, v, INDEX + at, KB, t) for t in range(3))
+        k0, k1, k2, v0, v1, v2 = (gathered(sc, kv, INDEX + at, KB, t) for t in range(6))
         kpos = lookup(sc, BASE + at, KB, col, HALF) + within(col)
         s = lax.dot_general(q0, k0, NT, preferred_element_type=jnp.float32)
         d1 = lax.dot_general(q10, jnp.concatenate([k0, k1], 1), NT, preferred_element_type=jnp.float32)
@@ -214,12 +213,11 @@
 
 
 def key_scratch(planes):
-    return [pltpu.VMEM((planes * 8, 2, 3, SLICE, HD), jnp.bfloat16) for _ in range(2)]
-
-
-def plane_copies(refs, k, v):
-    n = len(refs) // 2
-    return [(ref, (k, v)[i // n].at[pl.ds(i % n * 8, 8)]) for i, ref in enumerate(refs)]
+    return pltpu.VMEM((planes * 8, 2, 6, SLICE, HD), jnp.bfloat16)
+
+
+def plane_copies(refs, kv):
+    return [(ref, kv.at[4 * i : 4 * i + 4]) for i, ref in enumerate(refs)]
 
 
 def estimate(queries, keys):
@@ -233,9 +231,9 @@
     def kernel(sc, q_own, q_other, *refs):
         kv_refs, refs = refs[:n], refs[n:]
         held_refs, refs = refs[: len(held)], refs[len(held) :]
-        out_refs, (k, v, q, st, sem) = refs[:2], refs[2:]
+        out_refs, (kv, q, st, sem) = refs[:2], refs[2:]
         before = [(ref, st.at[8 * i : 8 * i + 8]) for i, ref in enumerate(held_refs)]
-        copy_in([(q_own, q.at[0:8]), (q_other, q.at[8:16]), *before, *plane_copies(kv_refs, k, v)], sem)
+        copy_in([(q_own, q.at[0:8]), (q_other, q.at[8:16]), *before, *plane_copies(kv_refs, kv)], sem)
 
         def tile(qt, _):
             at = INDEX + FIRST[3] + qt * QB
@@ -244,7 +242,7 @@
             def work():
                 info = query_tile(sc, q, FIRST[3], qt)
                 state = gather_state(sc, st, at) if held else fresh()
-                parts = pack_state(see(sc, k, v, FIRST[key_set], info, state, low, high))
+                parts = pack_state(see(sc, kv, FIRST[key_set], info, state, low, high))
                 for i in range(QB):
                     for t in range(4):
                         st[sc[at + i], :, t] = parts[t][i * HALF : i * HALF + HALF].reshape(2, SLICE, HD)
@@ -265,7 +263,7 @@
         in_specs=[SMEM] + [ANY] * (2 + n + len(held)),
         out_specs=(ANY, ANY),
         scratch_shapes=[
-            *key_scratch(n // 2),
+            key_scratch(n // 2),
             pltpu.VMEM((16, 2, 3, SLICE, HD), jnp.bfloat16),
             kernel_state(16),
             pltpu.SemaphoreType.DMA,
@@ -280,15 +278,15 @@
 
     def kernel(sc, q_ref, *refs):
         kv_refs, held_refs = refs[:n], refs[n : n + 2]
-        out, k, v, q, one, two, sem = refs[n + 2 :]
-        copy_in([(q_ref, q), (held_refs[0], one), (held_refs[1], two), *plane_copies(kv_refs, k, v)], sem)
+        out, kv, q, one, two, sem = refs[n + 2 :]
+        copy_in([(q_ref, q), (held_refs[0], one), (held_refs[1], two), *plane_copies(kv_refs, kv)], sem)
 
         def tile(qt, _):
             at = INDEX + FIRST[4] + qt * QB
             info = query_tile(sc, q, FIRST[4], qt)
             state = join_states(gather_state(sc, one, at), gather_state(sc, two, at))
             low, high = sc[LOW + 2 * 6 + 4 + qt], sc[HIGH + 2 * 6 + 4 + qt]
-            parts = results(see(sc, k, v, FIRST[2], info, state, low, high))
+            parts = results(see(sc, kv, FIRST[2], info, state, low, high))
             for i in range(QB):
                 for t, part in enumerate(parts):
                     block = part[i * HALF : i * HALF + HALF].reshape(2, SLICE, HD)
@@ -303,7 +301,7 @@
         in_specs=[SMEM] + [ANY] * (3 + n),
         out_specs=VMEM,
         scratch_shapes=[
-            *key_scratch(n // 2),
+            key_scratch(n // 2),
             pltpu.VMEM((8, 2, 3, SLICE, HD), jnp.bfloat16),
             kernel_state(8),
             kernel_state(8),
@@ -334,26 +332,22 @@
     return lax.ppermute(block, "c", [(0, 1), (1, 0)])
 
 
-def to_heads(array):
-    return lax.all_to_all(split_heads(array), XY, 0, 0).reshape(8, 2, 3, SLICE, HD)
-
-
 def shards(query_set, key_set, value_set, block_order, documents):
-    planes = {0: [to_heads(key_set), to_heads(value_set)]}
+    kv = lax.all_to_all(split_heads(key_set, value_set), XY, 0, 0).reshape(8, 2, 6, SLICE, HD)
+    sc = scalars(block_order, documents, *(lax.axis_index(a) for a in ("zh", "zl", "c")))
+    kv, q, sc = lax.optimization_barrier((kv, split_heads(query_set), sc))
+    q = lax.all_to_all(q, XY, 0, 0).reshape(8, 2, 3, SLICE, HD)
+    planes = {0: [kv[:4], kv[4:]]}
     for step in range(1, 4):
         planes[-step] = [hop(p, 1) for p in planes[1 - step]]
         planes[step] = [hop(p, -1) for p in planes[step - 1]]
-    query_set, _ = lax.optimization_barrier((query_set, planes[1][0]))
-    q = to_heads(query_set)
-    sc = scalars(block_order, documents, *(lax.axis_index(a) for a in ("zh", "zl", "c")))
     queries = (q, swap_cores(q))
-    state = attend(sc, queries, [planes[o][t] for t in range(2) for o in NEAR], 0)
+    state = attend(sc, queries, [p for o in NEAR for p in planes[o]], 0)
     state, planes[-3][0], planes[3][1] = lax.optimization_barrier((state, planes[-3][0], planes[3][1]))
     far = [hop(planes[-3][0], 1), hop(planes[3][1], -1)]
-    own, other = attend(sc, queries, [planes[o][t] for t in range(2) for o in NEXT], 1, state)
+    own, other = attend(sc, queries, [p for o in NEXT for p in planes[o]], 1, state)
     own, other, far = lax.optimization_barrier((own, other, far))
-    far = [p for f in far for p in (f, swap_cores(f))]
-    done = finish(sc, q, far, (own, swap_cores(other)))
+    done = finish(sc, q, [*far, *map(swap_cores, far)], (own, swap_cores(other)))
     done = lax.all_to_all(done.reshape(HEADS, 3, SLICE, HD), XY, 0, 0)
     return join_heads(done)
 

time: 126 us -> 122 us (0.968)
  waiting for transfers between devices: 11.5 us -> 23.3 us
  starting transfers between devices: 53.5 us -> 46.9 us
  blocking collectives: 18.2 us -> 14 us
  other arithmetic: 2.85 us -> 1.13 us
  local copies, waits for them, and re-layouts: 5.24 us -> 3.53 us
    ppermute x14, waiting for transfers between devices: 0.04 us -> 13.7 us  [hop(): lax.ppermute(block, Z, [(i, (i + direction) % NZ) for i in range(NZ)])]
    ppermute x14, starting transfers between devices: 26.1 us -> 20.9 us  [hop(): lax.ppermute(block, Z, [(i, (i + direction) % NZ) for i in range(NZ)])]
    all_to_all x3 -> x2, starting transfers between devices: 15.6 us -> 11.4 us  [the longest x1 7.58 us: shards(): lax.all_to_all(split_heads(key_set, value_set), XY, 0, 0)]
    all_to_all x1, blocking collectives: 18.2 us -> 14 us  [shards(): done = lax.all_to_all(done.reshape(HEADS, 3, SLICE, HD), XY, 0, 0)]
    ppermute x4, starting transfers between devices: 11.8 us -> 14.6 us  [swap_cores(): return lax.ppermute(block, 'c', [(0, 1), (1, 0)])]
    all_to_all x3 -> x2, waiting for transfers between devices: 8.52 us -> 6.62 us  [the longest x1 6.61 us: shards(): lax.all_to_all(split_heads(key_set, value_set), XY, 0, 0)]
    pallas_call x3 -> x2, Pallas kernels: 5.43 us -> 3.95 us  [split_heads(): pl.pallas_call(kernel, out_shape=jax.ShapeDtypeStruct((HEADS, 3 * len(arr...]
    unnamed x14 -> x12, local copies, waits for them, and re-layouts: 2.6 us -> 2.6 us
  transfers between devices with their start and end apart: 21 -> 20, of which waited for: 5 -> 5; matrix products, arithmetic and copies ran while one was open for 4% -> 2% of each run, Pallas kernels for 20% -> 19%
where the time goes in v4:
time: 122 us
  starting transfers between devices  46.9 us (38%)
  Pallas kernels  33.2 us (27%)
  waiting for transfers between devices  23.3 us (19%)
  blocking collectives  14 us (11%)
  local copies, waits for them, and re-layouts  3.53 us (3%)
    pallas_call x2, Pallas kernels, attend(): pl.pallas_call(kernel, out_shape=(part, part), in_specs=[SMEM] + [ANY] *...  21.9 us
    ppermute x14, starting transfers between devices, hop(): lax.ppermute(block, Z, [(i, (i + direction) % NZ) for i in range(NZ)])  20.9 us
    ppermute x4, starting transfers between devices, swap_cores(): return lax.ppermute(block, 'c', [(0, 1), (1, 0)])  14.6 us
    all_to_all x1, blocking collectives, shards(): done = lax.all_to_all(done.reshape(HEADS, 3, SLICE, HD), XY, 0, 0)  14 us
    ppermute x14, waiting for transfers between devices, hop(): lax.ppermute(block, Z, [(i, (i + direction) % NZ) for i in range(NZ)])  13.7 us
    all_to_all x1, starting transfers between devices, shards(): lax.all_to_all(split_heads(key_set, value_set), XY, 0, 0)  7.58 us
    all_to_all x1, waiting for transfers between devices, shards(): lax.all_to_all(split_heads(key_set, value_set), XY, 0, 0)  6.61 us
    pallas_call x1, Pallas kernels, finish(): pl.pallas_call(kernel, out_shape=jax.ShapeDtypeStruct((8, 2, 3, SLICE, HD...  5.56 us
  transfers between devices with their start and end apart: 20, of which 5 were waited for; matrix products, arithmetic and copies ran while one was open for 2% of the time, Pallas kernels for 19%

profile of v4, /device:TPU:1, one launch (start us, length us, event | category | flops | bytes accessed | tf_op | source)
XLA Modules:
  0.0 122.2 jit_solution(314595292978832004)
XLA Ops:
  0.0 2.1 %shard_map.91 = bf16[16,6,32,128]{3,2,1,0:T(8,128)(2,1)} custom-call(bf16[3,32,2048]{2,1,0:T(8,128)(2,1)} %refs_0_.2, bf16[3,32,2048]{2,1,0:T(8,128)(2,1)} %refs_1_.1), custom_call_target="tpu_custom_call" | custom-call | tf_op jit(solution)/shard_map/pallas_call | solution.py:45
  2.1 7.6 %all-to-all-start = ((bf16[16,6,32,128]{3,2,1,0:T(8,128)(2,1)}), bf16[16,6,32,128]{3,2,1,0:T(8,128)(2,1)S(1)}, u32[]{:S(2)}, u32[]{:S(2)}) async-start(bf16[16,6,32,128]{3,2,1,0:T(8,128)(2,1)} %shard_map.91), calls=%async_computation | async-start | bytes 1572864 | tf_op jit(solution)/shard_map/all_to_all | solution.py:336
  9.8 0.6 copy-done.4
  10.5 0.6 copy-done.1
  11.1 0.1 reshape.338
  11.4 0.6 copy-done.3
  12.3 0.2 convert_reduce_fusion.1
  12.4 0.6 copy-done.2
  13.6 0.2 convert_reduce_fusion
  14.0 0.2 convert_reduce_fusion.2
  14.4 1.8 %shard_map.92 = bf16[16,3,32,128]{3,2,1,0:T(8,128)(2,1)} custom-call(bf16[3,32,2048]{2,1,0:T(8,128)(2,1)} %refs_0_.3), custom_call_target="tpu_custom_call" | custom-call | tf_op jit(solution)/shard_map/pallas_call | solution.py:45
  16.3 6.6 %all-to-all-done = bf16[16,6,32,128]{3,2,1,0:T(8,128)(2,1)S(1)} async-done(((bf16[16,6,32,128]{3,2,1,0:T(8,128)(2,1)}), bf16[16,6,32,128]{3,2,1,0:T(8,128)(2,1)S(1)}, u32[]{:S(2)}, u32[]{:S(2)}) %all-to-all-start) | async-done | bytes 786464 | tf_op jit(solution)/shard_map/all_to_all | solution.py:336
  23.0 5.7 %collective-permute-start.6 = (bf16[4,2,6,32,128]{4,3,2,1,0:T(8,128)(2,1)S(1)}, bf16[4,2,6,32,128]{4,3,2,1,0:T(8,128)(2,1)S(1)}, u32[]{:S(2)}, u32[]{:S(2)}) collective-permute-start(bf16[4,2,6,32,128]{4,3,2,1,0:T(8,128)(2,1)S(1)} %get-tuple-element.43.refs_5_), channel_id=1, source_target_pairs={{0,193},{1,0},{64,1},{65,64},{128,65},{129,128},{192,129},{193,192... | collective-permute-start | bytes 1179656 | tf_op jit(solution)/shard_map/ppermute | solution.py:328
  28.6 2.7 %collective-permute-start.5 = (bf16[4,2,6,32,128]{4,3,2,1,0:T(8,128)(2,1)S(1)}, bf16[4,2,6,32,128]{4,3,2,1,0:T(8,128)(2,1)S(1)}, u32[]{:S(2)}, u32[]{:S(2)}) collective-permute-start(bf16[4,2,6,32,128]{4,3,2,1,0:T(8,128)(2,1)S(1)} %get-tuple-element.44.refs_4_), channel_id=1, source_target_pairs={{0,193},{1,0},{64,1},{65,64},{128,65},{129,128},{192,129},{193,192... | collective-permute-start | bytes 1179656 | tf_op jit(solution)/shard_map/ppermute | solution.py:328
  31.3 3.8 %all-to-all-start.1 = ((bf16[16,3,32,128]{3,2,1,0:T(8,128)(2,1)}), bf16[16,3,32,128]{3,2,1,0:T(8,128)(2,1)S(1)}, u32[]{:S(2)}, u32[]{:S(2)}) async-start(bf16[16,3,32,128]{3,2,1,0:T(8,128)(2,1)} %shard_map.92), calls=%async_computation.1 | async-start | bytes 786432 | tf_op jit(solution)/shard_map/all_to_all | solution.py:339
  35.2 3.0 %collective-permute-start.8 = (bf16[4,2,6,32,128]{4,3,2,1,0:T(8,128)(2,1)S(1)}, bf16[4,2,6,32,128]{4,3,2,1,0:T(8,128)(2,1)S(1)}, u32[]{:S(2)}, u32[]{:S(2)}) collective-permute-start(bf16[4,2,6,32,128]{4,3,2,1,0:T(8,128)(2,1)S(1)} %collective-permute-done.6.refs_7_), channel_id=1, source_target_pairs={{0,193},{1,0},{64,1},{65,64},{128,65},{129,128},{192,129},{193,192... | collective-permute-start | bytes 1179656 | tf_op jit(solution)/shard_map/ppermute | solution.py:328
  38.2 8.1 %collective-permute-done.3.refs_3_ = bf16[4,2,6,32,128]{4,3,2,1,0:T(8,128)(2,1)S(1)} collective-permute-done((bf16[4,2,6,32,128]{4,3,2,1,0:T(8,128)(2,1)S(1)}, bf16[4,2,6,32,128]{4,3,2,1,0:T(8,128)(2,1)S(1)}, u32[]{:S(2)}, u32[]{:S(2)}) %collective-permute-start.3) | collective-permute-done | bytes 393248 | tf_op jit(solution)/shard_map/ppermute | solution.py:328
  46.3 2.7 %collective-permute-start.7 = (bf16[4,2,6,32,128]{4,3,2,1,0:T(8,128)(2,1)S(1)}, bf16[4,2,6,32,128]{4,3,2,1,0:T(8,128)(2,1)}, u32[]{:S(2)}, u32[]{:S(2)}) collective-permute-start(bf16[4,2,6,32,128]{4,3,2,1,0:T(8,128)(2,1)S(1)} %collective-permute-done.5.refs_6_), channel_id=1, source_target_pairs={{0,193},{1,0},{64,1},{65,64},{128,65},{129,128},{192,129},{193,192... | collective-permute-start | bytes 1179656 | tf_op jit(solution)/shard_map/ppermute | solution.py:328
  49.0 7.1 %collective-permute-start = (bf16[8,2,3,32,128]{4,3,2,1,0:T(8,128)(2,1)S(1)}, bf16[8,2,3,32,128]{4,3,2,1,0:T(8,128)(2,1)S(1)}, u32[]{:S(2)}, u32[]{:S(2)}) collective-permute-start(bf16[8,2,3,32,128]{4,3,2,1,0:T(8,128)(2,1)S(1)} %bitcast.4), channel_id=1, source_target_pairs={{0,8},{8,0},{1,9},{9,1},{2,10},{10,2},{3,11},{11,3},{4,12},{12,4},... | collective-permute-start | bytes 1179656 | tf_op jit(solution)/shard_map/ppermute | solution.py:332
  56.1 1.5 %collective-permute-start.9 = (bf16[4,2,6,32,128]{4,3,2,1,0:T(8,128)(2,1)}, bf16[4,2,6,32,128]{4,3,2,1,0:T(8,128)(2,1)S(1)}, u32[]{:S(2)}, u32[]{:S(2)}) collective-permute-start(bf16[4,2,6,32,128]{4,3,2,1,0:T(8,128)(2,1)} %collective-permute-done.2.refs_0_), channel_id=1, source_target_pairs={{0,1},{1,64},{64,65},{65,128},{128,129},{129,192},{192,193},{193,0... | collective-permute-start | bytes 1179656 | tf_op jit(solution)/shard_map/ppermute | solution.py:328
  57.6 5.6 %collective-permute-done.4.refs_1_ = bf16[4,2,6,32,128]{4,3,2,1,0:T(8,128)(2,1)S(1)} collective-permute-done((bf16[4,2,6,32,128]{4,3,2,1,0:T(8,128)(2,1)S(1)}, bf16[4,2,6,32,128]{4,3,2,1,0:T(8,128)(2,1)S(1)}, u32[]{:S(2)}, u32[]{:S(2)}) %collective-permute-start.4) | collective-permute-done | bytes 393248 | tf_op jit(solution)/shard_map/ppermute | solution.py:328
  63.2 2.7 %collective-permute-start.12 = (bf16[4,2,6,32,128]{4,3,2,1,0:T(8,128)(2,1)}, bf16[4,2,6,32,128]{4,3,2,1,0:T(8,128)(2,1)S(1)}, u32[]{:S(2)}, u32[]{:S(2)}) collective-permute-start(bf16[4,2,6,32,128]{4,3,2,1,0:T(8,128)(2,1)} %collective-permute-done.7.refs_8_), channel_id=1, source_target_pairs={{0,193},{1,0},{64,1},{65,64},{128,65},{129,128},{192,129},{193,192... | collective-permute-start | bytes 1179656 | tf_op jit(solution)/shard_map/ppermute | solution.py:328
  65.8 12.6 %shard_map.93 = (f32[8,2,4,32,128]{4,3,2,1,0:T(8,128)S(1)}, f32[8,2,4,32,128]{4,3,2,1,0:T(8,128)S(1)}) custom-call(s32[231]{0:T(256)S(1)} %concatenate.3.sc, bf16[8,2,3,32,128]{4,3,2,1,0:T(8,128)(2,1)S(1)} %bitcast.5, bf16[8,2,3,32,128]{4,3,2,1,0:T(8,128)(2,1)S(1)} %collective-permute-done.q_other, ...), custom_call_target="tpu_custom_call" | custom-call | flops 1677721600 | bytes 8388608 | tf_op jit(solution)/shard_map/pallas_call | solution.py:260
  78.6 2.7 %collective-permute-start.14 = (bf16[4,2,6,32,128]{4,3,2,1,0:T(8,128)(2,1)S(1)}, bf16[4,2,6,32,128]{4,3,2,1,0:T(8,128)(2,1)S(1)}, u32[]{:S(2)}, u32[]{:S(2)}) collective-permute-start(bf16[4,2,6,32,128]{4,3,2,1,0:T(8,128)(2,1)S(1)} %collective-permute-done.10.refs_3_), channel_id=1, source_target_pairs={{0,193},{1,0},{64,1},{65,64},{128,65},{129,128},{192,129},{193,192... | collective-permute-start | bytes 1179656 | tf_op jit(solution)/shard_map/ppermute | solution.py:328
  81.2 9.3 %shard_map.94 = (f32[8,2,4,32,128]{4,3,2,1,0:T(8,128)S(1)}, f32[8,2,4,32,128]{4,3,2,1,0:T(8,128)S(1)}) custom-call(s32[231]{0:T(256)S(1)} %concatenate.3.sc, bf16[8,2,3,32,128]{4,3,2,1,0:T(8,128)(2,1)S(1)} %bitcast.6, bf16[8,2,3,32,128]{4,3,2,1,0:T(8,128)(2,1)S(1)} %collective-permute-done.q_other, ...), custom_call_target="tpu_custom_call" | custom-call | flops 671088640 | bytes 8388608 | tf_op jit(solution)/shard_map/pallas_call | solution.py:260
  90.5 6.9 %collective-permute-start.17 = (f32[8,2,4,32,128]{4,3,2,1,0:T(8,128)S(1)}, f32[8,2,4,32,128]{4,3,2,1,0:T(8,128)S(1)}, u32[]{:S(2)}, u32[]{:S(2)}) collective-permute-start(f32[8,2,4,32,128]{4,3,2,1,0:T(8,128)S(1)} %get-tuple-element.34), channel_id=1, source_target_pairs={{0,8},{8,0},{1,9},{9,1},{2,10},{10,2},{3,11},{11,3},{4,12},{12,4},... | collective-permute-start | bytes 3145736 | tf_op jit(solution)/shard_map/ppermute | solution.py:332
  97.6 0.4 collective-permute-start.16
  98.0 2.3 %collective-permute-done.15.refs_2_ = bf16[4,2,6,32,128]{4,3,2,1,0:T(8,128)(2,1)S(1)} collective-permute-done((bf16[4,2,6,32,128]{4,3,2,1,0:T(8,128)(2,1)S(1)}, bf16[4,2,6,32,128]{4,3,2,1,0:T(8,128)(2,1)S(1)}, u32[]{:S(2)}, u32[]{:S(2)}) %collective-permute-start.15) | collective-permute-done | bytes 393248 | tf_op jit(solution)/shard_map/ppermute | solution.py:332
  100.3 0.6 collective-permute-done.16.refs_3_
  100.9 5.6 %shard_map.95 = bf16[8,2,3,32,128]{4,3,2,1,0:T(8,128)(2,1)S(1)} custom-call(s32[231]{0:T(256)S(1)} %concatenate.3.sc, bf16[8,2,3,32,128]{4,3,2,1,0:T(8,128)(2,1)S(1)} %bitcast.7, bf16[4,2,6,32,128]{4,3,2,1,0:T(8,128)(2,1)S(1)} %collective-permute-done.13.refs_0_, bf16[4,2,6,32,128]{4,3,2,1,0:T(8,128)(2,1)S(1)} %collective-permute-done.14.refs_1_, ...), custom_call_target="tpu_custom_call" | custom-call | flops 335544320 | bytes 8388608 | tf_op jit(solution)/shard_map/pallas_call | solution.py:298
  106.4 14.0 %all_to_all.15.ref = bf16[16,3,32,128]{3,2,1,0:T(8,128)(2,1)} all-to-all(bf16[16,3,32,128]{3,2,1,0:T(8,128)(2,1)S(1)} %bitcast.8), channel_id=1, replica_groups=mesh['zh'=4,'y'=4,'c'=2,'xh'=2,'xl'=2,'zl'=2] {'y','xh','xl'}, dimensions={0} | all-to-all | bytes 786432 | tf_op jit(solution)/shard_map/all_to_all | solution.py:351
  120.4 1.8 %shard_map.96 = bf16[3,32,2048]{2,1,0:T(8,128)(2,1)} custom-call(bf16[16,3,32,128]{3,2,1,0:T(8,128)(2,1)} %all_to_all.15.ref), custom_call_target="tpu_custom_call" | custom-call | tf_op jit(solution)/shard_map/pallas_call | solution.py:58
  (57 shorter events, 1.6 us)
Async XLA Ops:
  2.1 20.8 %all-to-all-start = ((bf16[16,6,32,128]{3,2,1,0:T(8,128)(2,1)}), bf16[16,6,32,128]{3,2,1,0:T(8,128)(2,1)S(1)}, u32[]{:S(2)}, u32[]{:S(2)}) async-start(bf16[16,6,32,128]{3,2,1,0:T(8,128)(2,1)} %shard_map.91), calls=%async_computation | async-start | bytes 1572864 | tf_op jit(solution)/shard_map/all_to_all | solution.py:336
  9.7 0.7 copy-start.4
  9.7 0.7 copy-start.5
  10.4 0.7 copy-start.1
  11.4 0.7 copy-start.3
  12.0 1.5 %copy-start = (s32[8192]{0:T(1024)S(1)}, s32[8192]{0:T(1024)}, u32[]{:S(2)}) copy-start(s32[8192]{0:T(1024)} %param.13) | copy-start | bytes 98308
  12.4 0.7 copy-start.2
  23.0 12.2 %collective-permute-start.6 = (bf16[4,2,6,32,128]{4,3,2,1,0:T(8,128)(2,1)S(1)}, bf16[4,2,6,32,128]{4,3,2,1,0:T(8,128)(2,1)S(1)}, u32[]{:S(2)}, u32[]{:S(2)}) collective-permute-start(bf16[4,2,6,32,128]{4,3,2,1,0:T(8,128)(2,1)S(1)} %get-tuple-element.43.refs_5_), channel_id=1, source_target_pairs={{0,193},{1,0},{64,1},{65,64},{128,65},{129,128},{192,129},{193,192... | collective-permute-start | bytes 1179656 | tf_op jit(solution)/shard_map/ppermute | solution.py:328
  28.6 9.5 %collective-permute-start.1 = (bf16[4,2,6,32,128]{4,3,2,1,0:T(8,128)(2,1)S(1)}, bf16[4,2,6,32,128]{4,3,2,1,0:T(8,128)(2,1)S(1)}, u32[]{:S(2)}, u32[]{:S(2)}) collective-permute-start(bf16[4,2,6,32,128]{4,3,2,1,0:T(8,128)(2,1)S(1)} %get-tuple-element.44.refs_4_), channel_id=1, source_target_pairs={{0,1},{1,64},{64,65},{65,128},{128,129},{129,192},{192,193},{193,0... | collective-permute-start | bytes 1179656 | tf_op jit(solution)/shard_map/ppermute | solution.py:328
  28.6 17.7 %collective-permute-start.3 = (bf16[4,2,6,32,128]{4,3,2,1,0:T(8,128)(2,1)S(1)}, bf16[4,2,6,32,128]{4,3,2,1,0:T(8,128)(2,1)S(1)}, u32[]{:S(2)}, u32[]{:S(2)}) collective-permute-start(bf16[4,2,6,32,128]{4,3,2,1,0:T(8,128)(2,1)S(1)} %get-tuple-element.43.refs_5_), channel_id=1, source_target_pairs={{0,1},{1,64},{64,65},{65,128},{128,129},{129,192},{192,193},{193,0... | collective-permute-start | bytes 1179656 | tf_op jit(solution)/shard_map/ppermute | solution.py:328
  28.6 17.7 %collective-permute-start.5 = (bf16[4,2,6,32,128]{4,3,2,1,0:T(8,128)(2,1)S(1)}, bf16[4,2,6,32,128]{4,3,2,1,0:T(8,128)(2,1)S(1)}, u32[]{:S(2)}, u32[]{:S(2)}) collective-permute-start(bf16[4,2,6,32,128]{4,3,2,1,0:T(8,128)(2,1)S(1)} %get-tuple-element.44.refs_4_), channel_id=1, source_target_pairs={{0,193},{1,0},{64,1},{65,64},{128,65},{129,128},{192,129},{193,192... | collective-permute-start | bytes 1179656 | tf_op jit(solution)/shard_map/ppermute | solution.py:328
  31.3 17.7 %all-to-all-start.1 = ((bf16[16,3,32,128]{3,2,1,0:T(8,128)(2,1)}), bf16[16,3,32,128]{3,2,1,0:T(8,128)(2,1)S(1)}, u32[]{:S(2)}, u32[]{:S(2)}) async-start(bf16[16,3,32,128]{3,2,1,0:T(8,128)(2,1)} %shard_map.92), calls=%async_computation.1 | async-start | bytes 786432 | tf_op jit(solution)/shard_map/all_to_all | solution.py:339
  35.2 21.0 %collective-permute-start.8 = (bf16[4,2,6,32,128]{4,3,2,1,0:T(8,128)(2,1)S(1)}, bf16[4,2,6,32,128]{4,3,2,1,0:T(8,128)(2,1)S(1)}, u32[]{:S(2)}, u32[]{:S(2)}) collective-permute-start(bf16[4,2,6,32,128]{4,3,2,1,0:T(8,128)(2,1)S(1)} %collective-permute-done.6.refs_7_), channel_id=1, source_target_pairs={{0,193},{1,0},{64,1},{65,64},{128,65},{129,128},{192,129},{193,192... | collective-permute-start | bytes 1179656 | tf_op jit(solution)/shard_map/ppermute | solution.py:328
  38.2 18.0 %collective-permute-start.2 = (bf16[4,2,6,32,128]{4,3,2,1,0:T(8,128)(2,1)S(1)}, bf16[4,2,6,32,128]{4,3,2,1,0:T(8,128)(2,1)}, u32[]{:S(2)}, u32[]{:S(2)}) collective-permute-start(bf16[4,2,6,32,128]{4,3,2,1,0:T(8,128)(2,1)S(1)} %collective-permute-done.1.refs_2_), channel_id=1, source_target_pairs={{0,1},{1,64},{64,65},{65,128},{128,129},{129,192},{192,193},{193,0... | collective-permute-start | bytes 1179656 | tf_op jit(solution)/shard_map/ppermute | solution.py:328
  46.3 16.9 %collective-permute-start.4 = (bf16[4,2,6,32,128]{4,3,2,1,0:T(8,128)(2,1)S(1)}, bf16[4,2,6,32,128]{4,3,2,1,0:T(8,128)(2,1)S(1)}, u32[]{:S(2)}, u32[]{:S(2)}) collective-permute-start(bf16[4,2,6,32,128]{4,3,2,1,0:T(8,128)(2,1)S(1)} %collective-permute-done.3.refs_3_), channel_id=1, source_target_pairs={{0,1},{1,64},{64,65},{65,128},{128,129},{129,192},{192,193},{193,0... | collective-permute-start | bytes 1179656 | tf_op jit(solution)/shard_map/ppermute | solution.py:328
  46.3 16.9 %collective-permute-start.7 = (bf16[4,2,6,32,128]{4,3,2,1,0:T(8,128)(2,1)S(1)}, bf16[4,2,6,32,128]{4,3,2,1,0:T(8,128)(2,1)}, u32[]{:S(2)}, u32[]{:S(2)}) collective-permute-start(bf16[4,2,6,32,128]{4,3,2,1,0:T(8,128)(2,1)S(1)} %collective-permute-done.5.refs_6_), channel_id=1, source_target_pairs={{0,193},{1,0},{64,1},{65,64},{128,65},{129,128},{192,129},{193,192... | collective-permute-start | bytes 1179656 | tf_op jit(solution)/shard_map/ppermute | solution.py:328
  49.0 16.9 %collective-permute-start = (bf16[8,2,3,32,128]{4,3,2,1,0:T(8,128)(2,1)S(1)}, bf16[8,2,3,32,128]{4,3,2,1,0:T(8,128)(2,1)S(1)}, u32[]{:S(2)}, u32[]{:S(2)}) collective-permute-start(bf16[8,2,3,32,128]{4,3,2,1,0:T(8,128)(2,1)S(1)} %bitcast.4), channel_id=1, source_target_pairs={{0,8},{8,0},{1,9},{9,1},{2,10},{10,2},{3,11},{11,3},{4,12},{12,4},... | collective-permute-start | bytes 1179656 | tf_op jit(solution)/shard_map/ppermute | solution.py:332
  56.1 22.3 %collective-permute-start.10 = (bf16[4,2,6,32,128]{4,3,2,1,0:T(8,128)(2,1)S(1)}, bf16[4,2,6,32,128]{4,3,2,1,0:T(8,128)(2,1)S(1)}, u32[]{:S(2)}, u32[]{:S(2)}) collective-permute-start(bf16[4,2,6,32,128]{4,3,2,1,0:T(8,128)(2,1)S(1)} %collective-permute-done.8.refs_9_), channel_id=1, source_target_pairs={{0,193},{1,0},{64,1},{65,64},{128,65},{129,128},{192,129},{193,192... | collective-permute-start | bytes 1179656 | tf_op jit(solution)/shard_map/ppermute | solution.py:328
  56.1 22.4 %collective-permute-start.9 = (bf16[4,2,6,32,128]{4,3,2,1,0:T(8,128)(2,1)}, bf16[4,2,6,32,128]{4,3,2,1,0:T(8,128)(2,1)S(1)}, u32[]{:S(2)}, u32[]{:S(2)}) collective-permute-start(bf16[4,2,6,32,128]{4,3,2,1,0:T(8,128)(2,1)} %collective-permute-done.2.refs_0_), channel_id=1, source_target_pairs={{0,1},{1,64},{64,65},{65,128},{128,129},{129,192},{192,193},{193,0... | collective-permute-start | bytes 1179656 | tf_op jit(solution)/shard_map/ppermute | solution.py:328
  63.2 18.1 %collective-permute-start.11 = (bf16[4,2,6,32,128]{4,3,2,1,0:T(8,128)(2,1)S(1)}, bf16[4,2,6,32,128]{4,3,2,1,0:T(8,128)(2,1)S(1)}, u32[]{:S(2)}, u32[]{:S(2)}) collective-permute-start(bf16[4,2,6,32,128]{4,3,2,1,0:T(8,128)(2,1)S(1)} %collective-permute-done.4.refs_1_), channel_id=1, source_target_pairs={{0,1},{1,64},{64,65},{65,128},{128,129},{129,192},{192,193},{193,0... | collective-permute-start | bytes 1179656 | tf_op jit(solution)/shard_map/ppermute | solution.py:328
  63.2 18.1 %collective-permute-start.12 = (bf16[4,2,6,32,128]{4,3,2,1,0:T(8,128)(2,1)}, bf16[4,2,6,32,128]{4,3,2,1,0:T(8,128)(2,1)S(1)}, u32[]{:S(2)}, u32[]{:S(2)}) collective-permute-start(bf16[4,2,6,32,128]{4,3,2,1,0:T(8,128)(2,1)} %collective-permute-done.7.refs_8_), channel_id=1, source_target_pairs={{0,193},{1,0},{64,1},{65,64},{128,65},{129,128},{192,129},{193,192... | collective-permute-start | bytes 1179656 | tf_op jit(solution)/shard_map/ppermute | solution.py:328
  78.5 12.0 %collective-permute-start.13 = (bf16[4,2,6,32,128]{4,3,2,1,0:T(8,128)(2,1)S(1)}, bf16[4,2,6,32,128]{4,3,2,1,0:T(8,128)(2,1)S(1)}, u32[]{:S(2)}, u32[]{:S(2)}) collective-permute-start(bf16[4,2,6,32,128]{4,3,2,1,0:T(8,128)(2,1)S(1)} %collective-permute-done.9.refs_0_), channel_id=1, source_target_pairs={{0,1},{1,64},{64,65},{65,128},{128,129},{129,192},{192,193},{193,0... | collective-permute-start | bytes 1179656 | tf_op jit(solution)/shard_map/ppermute | solution.py:328
  78.6 11.9 %collective-permute-start.14 = (bf16[4,2,6,32,128]{4,3,2,1,0:T(8,128)(2,1)S(1)}, bf16[4,2,6,32,128]{4,3,2,1,0:T(8,128)(2,1)S(1)}, u32[]{:S(2)}, u32[]{:S(2)}) collective-permute-start(bf16[4,2,6,32,128]{4,3,2,1,0:T(8,128)(2,1)S(1)} %collective-permute-done.10.refs_3_), channel_id=1, source_target_pairs={{0,193},{1,0},{64,1},{65,64},{128,65},{129,128},{192,129},{193,192... | collective-permute-start | bytes 1179656 | tf_op jit(solution)/shard_map/ppermute | solution.py:328
  90.5 10.3 %collective-permute-start.17 = (f32[8,2,4,32,128]{4,3,2,1,0:T(8,128)S(1)}, f32[8,2,4,32,128]{4,3,2,1,0:T(8,128)S(1)}, u32[]{:S(2)}, u32[]{:S(2)}) collective-permute-start(f32[8,2,4,32,128]{4,3,2,1,0:T(8,128)S(1)} %get-tuple-element.34), channel_id=1, source_target_pairs={{0,8},{8,0},{1,9},{9,1},{2,10},{10,2},{3,11},{11,3},{4,12},{12,4},... | collective-permute-start | bytes 3145736 | tf_op jit(solution)/shard_map/ppermute | solution.py:332
  97.5 2.8 %collective-permute-start.15 = (bf16[4,2,6,32,128]{4,3,2,1,0:T(8,128)(2,1)S(1)}, bf16[4,2,6,32,128]{4,3,2,1,0:T(8,128)(2,1)S(1)}, u32[]{:S(2)}, u32[]{:S(2)}) collective-permute-start(bf16[4,2,6,32,128]{4,3,2,1,0:T(8,128)(2,1)S(1)} %collective-permute-done.13.refs_0_), channel_id=1, source_target_pairs={{0,8},{8,0},{1,9},{9,1},{2,10},{10,2},{3,11},{11,3},{4,12},{12,4},... | collective-permute-start | bytes 1179656 | tf_op jit(solution)/shard_map/ppermute | solution.py:332
  97.6 3.3 %collective-permute-start.16 = (bf16[4,2,6,32,128]{4,3,2,1,0:T(8,128)(2,1)S(1)}, bf16[4,2,6,32,128]{4,3,2,1,0:T(8,128)(2,1)S(1)}, u32[]{:S(2)}, u32[]{:S(2)}) collective-permute-start(bf16[4,2,6,32,128]{4,3,2,1,0:T(8,128)(2,1)S(1)} %collective-permute-done.14.refs_1_), channel_id=1, source_target_pairs={{0,8},{8,0},{1,9},{9,1},{2,10},{10,2},{3,11},{11,3},{4,12},{12,4},... | collective-permute-start | bytes 1179656 | tf_op jit(solution)/shard_map/ppermute | solution.py:332

commit v5 on v4

--- a/solution.py
+++ b/solution.py
@@ -1,3 +1,5 @@
+import functools
+
 import jax
 import jax.numpy as jnp
 from jax import lax
@@ -25,14 +27,14 @@
 ANY = pl.BlockSpec(memory_space=pl.ANY)
 NT = (((1,), (1,)), ((), ()))
 
-NEAR = (-2, -1, 0, 1, 2)
-NEXT = (-3, 3)
-FAR = (4,)
-FIRST = (0, 40, 56, 72, 88)
+SETS = ((-1, 0, 1), (-2, 2), (-3, 3), (4,))
+LAST = 3
+ALL, OWN = 4, 5
+FIRST = (0, 24, 40, 56, 72, 88)
 N_SLOTS = 96
 QB, KB = 4, 8
 QT, KT = QB * HALF, KB * HALF
-INDEX, BASE, LOW, HIGH, STARTS = 0, 96, 192, 210, 228
+INDEX, BASE, LOW, HIGH, STARTS = 0, 96, 192, 216, 240
 
 
 def split_heads(*arrays):
@@ -66,10 +68,9 @@
 def scalars(order, documents, zh, zl, c):
     i32 = jnp.int32
     z = zh * 2 + zl
-    rows = [(o, 0, 0) for o in NEAR]
-    rows += [(o, 0, 1) for o in NEXT]
-    rows += [(o, other, 2) for other in range(2) for o in FAR]
-    rows += [(0, 0, 3), (0, 1, 3), (0, 0, 4)]
+    rows = [(o, 0, i) for i in range(LAST) for o in SETS[i]]
+    rows += [(o, other, LAST) for other in range(2) for o in SETS[LAST]]
+    rows += [(0, 0, ALL), (0, 1, ALL), (0, 0, OWN)]
     offsets, cores, sets = (jnp.array(v, i32) for v in zip(*rows, strict=True))
     begins = jnp.array([FIRST[r[2]] // 8 for r in rows], i32)
     planes = lax.rem(z + offsets + NZ, NZ)
@@ -87,11 +88,11 @@
     base_of = low_bits // 2 * BLOCK + low_bits % 2 * SLICE
     base = jnp.sum(jnp.where(hits, base_of[None, :], 0), axis=1)
     starts = jnp.sum((documents[None, :] < jnp.arange(1, 4, dtype=i32)[:, None]).astype(i32), axis=1)
-    first = base[FIRST[3] :: QB]
-    last = base[FIRST[3] + QB - 1 :: QB] + BLOCK - SLICE
+    first = base[FIRST[ALL] :: QB]
+    last = base[FIRST[ALL] + QB - 1 :: QB] + BLOCK - SLICE
     begin = jnp.max(jnp.where(starts[None, :] <= first[:, None], starts[None, :], 0), axis=1)
     set_of = code // 4096
-    member = set_of[None, None, :] == jnp.arange(3, dtype=i32)[:, None, None]
+    member = set_of[None, None, :] == jnp.arange(len(SETS), dtype=i32)[:, None, None]
     before = base_of[None, None, :] + BLOCK - SLICE <= begin[None, :, None]
     upto = base_of[None, None, :] < last[None, :, None]
     low = jnp.sum((member & before).astype(i32), axis=2) // KB
@@ -107,7 +108,7 @@
 
 
 def within(position):
-    return lax.rem(position, HALF) // SLICE * HALF + lax.rem(position, SLICE)
+    return (position & SLICE) * 2 + (position & (SLICE - 1))
 
 
 def gathered(sc, ref, at, count, t):
@@ -117,7 +118,7 @@
 def query_tile(sc, q, first, tile):
     at = first + tile * QB
     q0, q1, q2 = (gathered(sc, q, INDEX + at, QB, t) for t in range(3))
-    row = lax.broadcasted_iota(jnp.int32, (QT, 1), 0)
+    row = lax.broadcasted_iota(jnp.int32, (QT, HD), 0)
     qpos = lookup(sc, BASE + at, QB, row, HALF) + within(row)
     start = jnp.zeros_like(qpos)
     for d in range(3):
@@ -125,37 +126,46 @@
     return q0, jnp.concatenate([q1, q0], 1), jnp.concatenate([q2, q0], 1), qpos, start
 
 
-def see(sc, kv, first, queries, state, low, high):
+def see(sc, kv, first, queries, state, low, high, room):
     q0, q10, q20, qpos, start = queries
     col = lax.broadcasted_iota(jnp.int32, (1, KT), 1)
     ones = jnp.ones((KT, HD), jnp.bfloat16)
 
-    def step(kt, state):
-        top, acc, acc_w = state
+    top_ref, acc_ref, acc_w_ref = room
+    top_ref[...], acc_ref[...], acc_w_ref[...] = state
+
+    def step(kt, _):
+        top = top_ref[...]
         at = first + kt * KB
         k0, k1, k2, v0, v1, v2 = (gathered(sc, kv, INDEX + at, KB, t) for t in range(6))
         kpos = lookup(sc, BASE + at, KB, col, HALF) + within(col)
         s = lax.dot_general(q0, k0, NT, preferred_element_type=jnp.float32)
         d1 = lax.dot_general(q10, jnp.concatenate([k0, k1], 1), NT, preferred_element_type=jnp.float32)
         d2 = lax.dot_general(q20, jnp.concatenate([k0, k2], 1), NT, preferred_element_type=jnp.float32)
-        s = jnp.where((kpos <= qpos) & (kpos >= start), s, HIDDEN)
-        peak = jnp.maximum(jnp.maximum(s[:, :HD], s[:, HD : 2 * HD]), jnp.maximum(s[:, 2 * HD : 3 * HD], s[:, 3 * HD :]))
+        parts = []
+        for i in range(KT // HD):
+            lanes = slice(i * HD, i * HD + HD)
+            visible = (kpos[:, lanes] <= qpos) & (kpos[:, lanes] >= start)
+            parts.append(jnp.where(visible, s[:, lanes], HIDDEN))
+        peak = functools.reduce(jnp.maximum, parts)
         new = jnp.maximum(top, jnp.max(peak, axis=1, keepdims=True))
         shrink = jnp.exp2((top - new) * EXPONENT)
-        shift = jnp.where(new < 0.5 * HIDDEN, 0.0, new)[:, :1]
-        e = jnp.exp2((s - shift) * EXPONENT)
+        shift = jnp.where(new < 0.5 * HIDDEN, 0.0, new)
+        e = jnp.concatenate([jnp.exp2((part - shift) * EXPONENT) for part in parts], 1)
         w = jnp.concatenate([(e * d1).astype(jnp.bfloat16), (e * d2).astype(jnp.bfloat16)], 0)
         shrink4 = jnp.concatenate([shrink] * 4, 1)
         shrink2 = shrink4[:, : 2 * HD]
-        acc = acc * shrink4 + jnp.dot(
+        top_ref[...] = new
+        acc_ref[...] = acc_ref[...] * shrink4 + jnp.dot(
             e.astype(jnp.bfloat16), jnp.concatenate([v0, v1, v2, ones], 1), preferred_element_type=jnp.float32
         )
-        acc_w = acc_w * jnp.concatenate([shrink2, shrink2], 0) + jnp.dot(
+        acc_w_ref[...] = acc_w_ref[...] * jnp.concatenate([shrink2, shrink2], 0) + jnp.dot(
             w, jnp.concatenate([v0, ones], 1), preferred_element_type=jnp.float32
         )
-        return new, acc, acc_w
-
-    return lax.fori_loop(low, high, step, state)
+        return 0
+
+    lax.fori_loop(low, high, step, 0)
+    return top_ref[...], acc_ref[...], acc_w_ref[...]
 
 
 def fresh():
@@ -200,6 +210,13 @@
     return unpack_state([gathered(sc, ref, at, QB, t) for t in range(4)])
 
 
+ROOM = (
+    pltpu.VMEM((QT, HD), jnp.float32),
+    pltpu.VMEM((QT, 4 * HD), jnp.float32),
+    pltpu.VMEM((2 * QT, 2 * HD), jnp.float32),
+)
+
+
 def copy_in(pairs, sem):
     copies = [pltpu.make_async_copy(src, dst, sem) for src, dst in pairs]
     for copy in copies:
@@ -231,18 +248,18 @@
     def kernel(sc, q_own, q_other, *refs):
         kv_refs, refs = refs[:n], refs[n:]
         held_refs, refs = refs[: len(held)], refs[len(held) :]
-        out_refs, (kv, q, st, sem) = refs[:2], refs[2:]
+        out_refs, (kv, q, st, sem, *room) = refs[:2], refs[2:]
         before = [(ref, st.at[8 * i : 8 * i + 8]) for i, ref in enumerate(held_refs)]
         copy_in([(q_own, q.at[0:8]), (q_other, q.at[8:16]), *before, *plane_copies(kv_refs, kv)], sem)
 
         def tile(qt, _):
-            at = INDEX + FIRST[3] + qt * QB
+            at = INDEX + FIRST[ALL] + qt * QB
             low, high = sc[LOW + key_set * 6 + qt], sc[HIGH + key_set * 6 + qt]
 
             def work():
-                info = query_tile(sc, q, FIRST[3], qt)
+                info = query_tile(sc, q, FIRST[ALL], qt)
                 state = gather_state(sc, st, at) if held else fresh()
-                parts = pack_state(see(sc, kv, FIRST[key_set], info, state, low, high))
+                parts = pack_state(see(sc, kv, FIRST[key_set], info, state, low, high, room))
                 for i in range(QB):
                     for t in range(4):
                         st[sc[at + i], :, t] = parts[t][i * HALF : i * HALF + HALF].reshape(2, SLICE, HD)
@@ -267,6 +284,7 @@
             pltpu.VMEM((16, 2, 3, SLICE, HD), jnp.bfloat16),
             kernel_state(16),
             pltpu.SemaphoreType.DMA,
+            *ROOM,
         ],
         compiler_params=pltpu.CompilerParams(vmem_limit_bytes=GRANT),
         cost_estimate=estimate(1024, n // 2 * 512),
@@ -278,15 +296,15 @@
 
     def kernel(sc, q_ref, *refs):
         kv_refs, held_refs = refs[:n], refs[n : n + 2]
-        out, kv, q, one, two, sem = refs[n + 2 :]
+        out, kv, q, one, two, sem, *room = refs[n + 2 :]
         copy_in([(q_ref, q), (held_refs[0], one), (held_refs[1], two), *plane_copies(kv_refs, kv)], sem)
 
         def tile(qt, _):
-            at = INDEX + FIRST[4] + qt * QB
-            info = query_tile(sc, q, FIRST[4], qt)
+            at = INDEX + FIRST[OWN] + qt * QB
+            info = query_tile(sc, q, FIRST[OWN], qt)
             state = join_states(gather_state(sc, one, at), gather_state(sc, two, at))
-            low, high = sc[LOW + 2 * 6 + 4 + qt], sc[HIGH + 2 * 6 + 4 + qt]
-            parts = results(see(sc, kv, FIRST[2], info, state, low, high))
+            low, high = sc[LOW + LAST * 6 + 4 + qt], sc[HIGH + LAST * 6 + 4 + qt]
+            parts = results(see(sc, kv, FIRST[LAST], info, state, low, high, room))
             for i in range(QB):
                 for t, part in enumerate(parts):
                     block = part[i * HALF : i * HALF + HALF].reshape(2, SLICE, HD)
@@ -306,6 +324,7 @@
             kernel_state(8),
             kernel_state(8),
             pltpu.SemaphoreType.DMA,
+            *ROOM,
         ],
         compiler_params=pltpu.CompilerParams(vmem_limit_bytes=GRANT),
         cost_estimate=estimate(512, n // 2 * 512),
@@ -338,14 +357,24 @@
     kv, q, sc = lax.optimization_barrier((kv, split_heads(query_set), sc))
     q = lax.all_to_all(q, XY, 0, 0).reshape(8, 2, 3, SLICE, HD)
     planes = {0: [kv[:4], kv[4:]]}
-    for step in range(1, 4):
+
+    def advance(step):
         planes[-step] = [hop(p, 1) for p in planes[1 - step]]
         planes[step] = [hop(p, -1) for p in planes[step - 1]]
+
+    def attend_set(i, held=()):
+        return attend(sc, queries, [p for o in SETS[i] for p in planes[o]], i, held)
+
+    advance(1)
+    advance(2)
     queries = (q, swap_cores(q))
-    state = attend(sc, queries, [p for o in NEAR for p in planes[o]], 0)
+    state = attend_set(0)
+    state, planes[-2][1], planes[2][0] = lax.optimization_barrier((state, planes[-2][1], planes[2][0]))
+    advance(3)
+    state = attend_set(1, state)
     state, planes[-3][0], planes[3][1] = lax.optimization_barrier((state, planes[-3][0], planes[3][1]))
     far = [hop(planes[-3][0], 1), hop(planes[3][1], -1)]
-    own, other = attend(sc, queries, [p for o in NEXT for p in planes[o]], 1, state)
+    own, other = attend_set(2, state)
     own, other, far = lax.optimization_barrier((own, other, far))
     done = finish(sc, q, [*far, *map(swap_cores, far)], (own, swap_cores(other)))
     done = lax.all_to_all(done.reshape(HEADS, 3, SLICE, HD), XY, 0, 0)

time: 122 us -> 118 us (0.967)
  starting transfers between devices: 46.9 us -> 43.9 us
  waiting for transfers between devices: 23.3 us -> 21.4 us
    ppermute x4, starting transfers between devices: 14.6 us -> 9.28 us  [swap_cores(): return lax.ppermute(block, 'c', [(0, 1), (1, 0)])]
    ppermute x14, waiting for transfers between devices: 13.7 us -> 9.59 us  [hop(): lax.ppermute(block, Z, [(i, (i + direction) % NZ) for i in range(NZ)])]
    all_to_all x1, waiting for transfers between devices: 0.01 us -> 2.61 us  [shards(): q = lax.all_to_all(q, XY, 0, 0).reshape(8, 2, 3, SLICE, HD)]
    ppermute x14, starting transfers between devices: 20.9 us -> 23.2 us  [hop(): lax.ppermute(block, Z, [(i, (i + direction) % NZ) for i in range(NZ)])]
    pallas_call x2 -> x3, Pallas kernels: 21.9 us -> 22.5 us  [attend(): pl.pallas_call(kernel, out_shape=(part, part), in_specs=[SMEM] + [ANY] *...]
  transfers between devices with their start and end apart: 20 -> 20, of which waited for: 5 -> 8; matrix products, arithmetic and copies ran while one was open for 2% -> 2% of each run, Pallas kernels for 19% -> 21%
where the time goes in v5:
time: 118 us; the launch traced here: 117 us
  starting transfers between devices  43.9 us (37%)
  Pallas kernels  33.7 us (29%)
  waiting for transfers between devices  21.4 us (18%)
  blocking collectives  12.8 us (11%)
  local copies, waits for them, and re-layouts  3.73 us (3%)
  other arithmetic  1.23 us (1%)
    ppermute x14, starting transfers between devices, hop(): lax.ppermute(block, Z, [(i, (i + direction) % NZ) for i in range(NZ)])  23.2 us
    pallas_call x3, Pallas kernels, attend(): pl.pallas_call(kernel, out_shape=(part, part), in_specs=[SMEM] + [ANY] *...  22.5 us
    all_to_all x1, blocking collectives, shards(): done = lax.all_to_all(done.reshape(HEADS, 3, SLICE, HD), XY, 0, 0)  12.8 us
    ppermute x14, waiting for transfers between devices, hop(): lax.ppermute(block, Z, [(i, (i + direction) % NZ) for i in range(NZ)])  9.59 us
    ppermute x4, starting transfers between devices, swap_cores(): return lax.ppermute(block, 'c', [(0, 1), (1, 0)])  9.28 us
    all_to_all x1, starting transfers between devices, shards(): lax.all_to_all(split_heads(key_set, value_set), XY, 0, 0)  7.58 us
    all_to_all x1, waiting for transfers between devices, shards(): lax.all_to_all(split_heads(key_set, value_set), XY, 0, 0)  6.32 us
    pallas_call x1, Pallas kernels, finish(): pl.pallas_call(kernel, out_shape=jax.ShapeDtypeStruct((8, 2, 3, SLICE, HD...  5.44 us
  transfers between devices with their start and end apart: 20, of which 8 were waited for; matrix products, arithmetic and copies ran while one was open for 2% of the time, Pallas kernels for 21%

profile of v5, /device:TPU:1, one launch (start us, length us, event | category | flops | bytes accessed | tf_op | source)
XLA Modules:
  0.0 117.1 jit_solution(1644579480821944778)
XLA Ops:
  0.0 2.1 %shard_map.91 = bf16[16,6,32,128]{3,2,1,0:T(8,128)(2,1)} custom-call(bf16[3,32,2048]{2,1,0:T(8,128)(2,1)} %refs_0_.2, bf16[3,32,2048]{2,1,0:T(8,128)(2,1)} %refs_1_.1), custom_call_target="tpu_custom_call" | custom-call | tf_op jit(solution)/shard_map/pallas_call | solution.py:47
  2.2 7.6 %all-to-all-start = ((bf16[16,6,32,128]{3,2,1,0:T(8,128)(2,1)}), bf16[16,6,32,128]{3,2,1,0:T(8,128)(2,1)S(1)}, u32[]{:S(2)}, u32[]{:S(2)}) async-start(bf16[16,6,32,128]{3,2,1,0:T(8,128)(2,1)} %shard_map.91), calls=%async_computation | async-start | bytes 1572864 | tf_op jit(solution)/shard_map/all_to_all | solution.py:355
  9.8 0.6 copy-done.4
  10.5 0.6 copy-done.1
  11.4 0.6 copy-done.3
  12.5 0.6 copy-done.2
  14.7 1.8 %shard_map.92 = bf16[16,3,32,128]{3,2,1,0:T(8,128)(2,1)} custom-call(bf16[3,32,2048]{2,1,0:T(8,128)(2,1)} %refs_0_.3), custom_call_target="tpu_custom_call" | custom-call | tf_op jit(solution)/shard_map/pallas_call | solution.py:47
  16.6 6.3 %all-to-all-done = bf16[16,6,32,128]{3,2,1,0:T(8,128)(2,1)S(1)} async-done(((bf16[16,6,32,128]{3,2,1,0:T(8,128)(2,1)}), bf16[16,6,32,128]{3,2,1,0:T(8,128)(2,1)S(1)}, u32[]{:S(2)}, u32[]{:S(2)}) %all-to-all-start) | async-done | bytes 786464 | tf_op jit(solution)/shard_map/all_to_all | solution.py:355
  23.0 5.7 %collective-permute-start.5 = (bf16[4,2,6,32,128]{4,3,2,1,0:T(8,128)(2,1)S(1)}, bf16[4,2,6,32,128]{4,3,2,1,0:T(8,128)(2,1)S(1)}, u32[]{:S(2)}, u32[]{:S(2)}) collective-permute-start(bf16[4,2,6,32,128]{4,3,2,1,0:T(8,128)(2,1)S(1)} %get-tuple-element.55.refs_3_), channel_id=1, source_target_pairs={{0,193},{1,0},{64,1},{65,64},{128,65},{129,128},{192,129},{193,192... | collective-permute-start | bytes 1179656 | tf_op jit(solution)/shard_map/ppermute | solution.py:347
  28.6 3.8 %all-to-all-start.1 = ((bf16[16,3,32,128]{3,2,1,0:T(8,128)(2,1)}), bf16[16,3,32,128]{3,2,1,0:T(8,128)(2,1)S(1)}, u32[]{:S(2)}, u32[]{:S(2)}) async-start(bf16[16,3,32,128]{3,2,1,0:T(8,128)(2,1)} %shard_map.92), calls=%async_computation.1 | async-start | bytes 786432 | tf_op jit(solution)/shard_map/all_to_all | solution.py:358
  32.5 2.7 %collective-permute-start.4 = (bf16[4,2,6,32,128]{4,3,2,1,0:T(8,128)(2,1)S(1)}, bf16[4,2,6,32,128]{4,3,2,1,0:T(8,128)(2,1)S(1)}, u32[]{:S(2)}, u32[]{:S(2)}) collective-permute-start(bf16[4,2,6,32,128]{4,3,2,1,0:T(8,128)(2,1)S(1)} %get-tuple-element.56.refs_2_), channel_id=1, source_target_pairs={{0,193},{1,0},{64,1},{65,64},{128,65},{129,128},{192,129},{193,192... | collective-permute-start | bytes 1179656 | tf_op jit(solution)/shard_map/ppermute | solution.py:347
  35.3 2.9 %collective-permute-start.8 = (bf16[4,2,6,32,128]{4,3,2,1,0:T(8,128)(2,1)S(1)}, bf16[4,2,6,32,128]{4,3,2,1,0:T(8,128)(2,1)S(1)}, u32[]{:S(2)}, u32[]{:S(2)}) collective-permute-start(bf16[4,2,6,32,128]{4,3,2,1,0:T(8,128)(2,1)S(1)} %collective-permute-done.5.refs_5_), channel_id=1, source_target_pairs={{0,193},{1,0},{64,1},{65,64},{128,65},{129,128},{192,129},{193,192... | collective-permute-start | bytes 1179656 | tf_op jit(solution)/shard_map/ppermute | solution.py:347
  38.2 2.6 %all-to-all-done.1 = bf16[16,3,32,128]{3,2,1,0:T(8,128)(2,1)S(1)} async-done(((bf16[16,3,32,128]{3,2,1,0:T(8,128)(2,1)}), bf16[16,3,32,128]{3,2,1,0:T(8,128)(2,1)S(1)}, u32[]{:S(2)}, u32[]{:S(2)}) %all-to-all-start.1) | async-done | bytes 393248 | tf_op jit(solution)/shard_map/all_to_all | solution.py:358
  40.8 3.7 %collective-permute-start = (bf16[8,2,3,32,128]{4,3,2,1,0:T(8,128)(2,1)S(1)}, bf16[8,2,3,32,128]{4,3,2,1,0:T(8,128)(2,1)S(1)}, u32[]{:S(2)}, u32[]{:S(2)}) collective-permute-start(bf16[8,2,3,32,128]{4,3,2,1,0:T(8,128)(2,1)S(1)} %bitcast.4), channel_id=1, source_target_pairs={{0,8},{8,0},{1,9},{9,1},{2,10},{10,2},{3,11},{11,3},{4,12},{12,4},... | collective-permute-start | bytes 1179656 | tf_op jit(solution)/shard_map/ppermute | solution.py:351
  44.5 1.9 %collective-permute-done.3.refs_1_ = bf16[4,2,6,32,128]{4,3,2,1,0:T(8,128)(2,1)S(1)} collective-permute-done((bf16[4,2,6,32,128]{4,3,2,1,0:T(8,128)(2,1)S(1)}, bf16[4,2,6,32,128]{4,3,2,1,0:T(8,128)(2,1)S(1)}, u32[]{:S(2)}, u32[]{:S(2)}) %collective-permute-start.3) | collective-permute-done | bytes 393248 | tf_op jit(solution)/shard_map/ppermute | solution.py:347
  46.3 2.7 %collective-permute-start.7 = (bf16[4,2,6,32,128]{4,3,2,1,0:T(8,128)(2,1)S(1)}, bf16[4,2,6,32,128]{4,3,2,1,0:T(8,128)(2,1)S(1)}, u32[]{:S(2)}, u32[]{:S(2)}) collective-permute-start(bf16[4,2,6,32,128]{4,3,2,1,0:T(8,128)(2,1)S(1)} %collective-permute-done.4.refs_4_), channel_id=1, source_target_pairs={{0,193},{1,0},{64,1},{65,64},{128,65},{129,128},{192,129},{193,192... | collective-permute-start | bytes 1179656 | tf_op jit(solution)/shard_map/ppermute | solution.py:347
  49.0 3.7 %collective-permute-done.8.refs_3_ = bf16[4,2,6,32,128]{4,3,2,1,0:T(8,128)(2,1)S(1)} collective-permute-done((bf16[4,2,6,32,128]{4,3,2,1,0:T(8,128)(2,1)S(1)}, bf16[4,2,6,32,128]{4,3,2,1,0:T(8,128)(2,1)S(1)}, u32[]{:S(2)}, u32[]{:S(2)}) %collective-permute-start.8) | collective-permute-done | bytes 393248 | tf_op jit(solution)/shard_map/ppermute | solution.py:347
  52.7 3.4 %collective-permute-start.10 = (bf16[4,2,6,32,128]{4,3,2,1,0:T(8,128)(2,1)S(1)}, bf16[4,2,6,32,128]{4,3,2,1,0:T(8,128)(2,1)S(1)}, u32[]{:S(2)}, u32[]{:S(2)}) collective-permute-start(bf16[4,2,6,32,128]{4,3,2,1,0:T(8,128)(2,1)S(1)} %collective-permute-done.8.refs_3_), channel_id=1, source_target_pairs={{0,193},{1,0},{64,1},{65,64},{128,65},{129,128},{192,129},{193,192... | collective-permute-start | bytes 1179656 | tf_op jit(solution)/shard_map/ppermute | solution.py:347
  56.1 8.8 %shard_map.93 = (f32[8,2,4,32,128]{4,3,2,1,0:T(8,128)S(1)}, f32[8,2,4,32,128]{4,3,2,1,0:T(8,128)S(1)}) custom-call(s32[243]{0:T(256)S(1)} %concatenate.3.sc, bf16[8,2,3,32,128]{4,3,2,1,0:T(8,128)(2,1)S(1)} %bitcast.5, bf16[8,2,3,32,128]{4,3,2,1,0:T(8,128)(2,1)S(1)} %collective-permute-done.q_other, ...), custom_call_target="tpu_custom_call" | custom-call | flops 1006632960 | bytes 8388608 | tf_op jit(solution)/shard_map/pallas_call | solution.py:277
  65.0 2.9 %collective-permute-start.12 = (bf16[4,2,6,32,128]{4,3,2,1,0:T(8,128)(2,1)S(1)}, bf16[4,2,6,32,128]{4,3,2,1,0:T(8,128)(2,1)S(1)}, u32[]{:S(2)}, u32[]{:S(2)}) collective-permute-start(bf16[4,2,6,32,128]{4,3,2,1,0:T(8,128)(2,1)S(1)} %collective-permute-done.7.refs_2_), channel_id=1, source_target_pairs={{0,193},{1,0},{64,1},{65,64},{128,65},{129,128},{192,129},{193,192... | collective-permute-start | bytes 1179656 | tf_op jit(solution)/shard_map/ppermute | solution.py:347
  68.0 6.8 %shard_map.94 = (f32[8,2,4,32,128]{4,3,2,1,0:T(8,128)S(1)}, f32[8,2,4,32,128]{4,3,2,1,0:T(8,128)S(1)}) custom-call(s32[243]{0:T(256)S(1)} %concatenate.3.sc, bf16[8,2,3,32,128]{4,3,2,1,0:T(8,128)(2,1)S(1)} %bitcast.6, bf16[8,2,3,32,128]{4,3,2,1,0:T(8,128)(2,1)S(1)} %collective-permute-done.q_other, ...), custom_call_target="tpu_custom_call" | custom-call | flops 671088640 | bytes 8388608 | tf_op jit(solution)/shard_map/pallas_call | solution.py:277
  74.9 2.7 %collective-permute-start.14 = (bf16[4,2,6,32,128]{4,3,2,1,0:T(8,128)(2,1)S(1)}, bf16[4,2,6,32,128]{4,3,2,1,0:T(8,128)(2,1)S(1)}, u32[]{:S(2)}, u32[]{:S(2)}) collective-permute-start(bf16[4,2,6,32,128]{4,3,2,1,0:T(8,128)(2,1)S(1)} %collective-permute-done.10.refs_3_), channel_id=1, source_target_pairs={{0,193},{1,0},{64,1},{65,64},{128,65},{129,128},{192,129},{193,192... | collective-permute-start | bytes 1179656 | tf_op jit(solution)/shard_map/ppermute | solution.py:347
  77.6 2.4 %collective-permute-done.11.refs_1_ = bf16[4,2,6,32,128]{4,3,2,1,0:T(8,128)(2,1)S(1)} collective-permute-done((bf16[4,2,6,32,128]{4,3,2,1,0:T(8,128)(2,1)S(1)}, bf16[4,2,6,32,128]{4,3,2,1,0:T(8,128)(2,1)S(1)}, u32[]{:S(2)}, u32[]{:S(2)}) %collective-permute-start.11) | collective-permute-done | bytes 393248 | tf_op jit(solution)/shard_map/ppermute | solution.py:347
  80.0 6.9 %shard_map.95 = (f32[8,2,4,32,128]{4,3,2,1,0:T(8,128)S(1)}, f32[8,2,4,32,128]{4,3,2,1,0:T(8,128)S(1)}) custom-call(s32[243]{0:T(256)S(1)} %concatenate.3.sc, bf16[8,2,3,32,128]{4,3,2,1,0:T(8,128)(2,1)S(1)} %bitcast.7, bf16[8,2,3,32,128]{4,3,2,1,0:T(8,128)(2,1)S(1)} %collective-permute-done.q_other, ...), custom_call_target="tpu_custom_call" | custom-call | flops 671088640 | bytes 8388608 | tf_op jit(solution)/shard_map/pallas_call | solution.py:277
  86.9 1.6 %collective-permute-done.13.refs_0_ = bf16[4,2,6,32,128]{4,3,2,1,0:T(8,128)(2,1)S(1)} collective-permute-done((bf16[4,2,6,32,128]{4,3,2,1,0:T(8,128)(2,1)S(1)}, bf16[4,2,6,32,128]{4,3,2,1,0:T(8,128)(2,1)S(1)}, u32[]{:S(2)}, u32[]{:S(2)}) %collective-permute-start.13) | collective-permute-done | bytes 393248 | tf_op jit(solution)/shard_map/ppermute | solution.py:347
  88.5 5.1 %collective-permute-start.17 = (f32[8,2,4,32,128]{4,3,2,1,0:T(8,128)S(1)}, f32[8,2,4,32,128]{4,3,2,1,0:T(8,128)S(1)}, u32[]{:S(2)}, u32[]{:S(2)}) collective-permute-start(f32[8,2,4,32,128]{4,3,2,1,0:T(8,128)S(1)} %get-tuple-element.46), channel_id=1, source_target_pairs={{0,8},{8,0},{1,9},{9,1},{2,10},{10,2},{3,11},{11,3},{4,12},{12,4},... | collective-permute-start | bytes 3145736 | tf_op jit(solution)/shard_map/ppermute | solution.py:351
  93.7 0.4 collective-permute-start.16
  94.1 2.3 %collective-permute-done.15.refs_2_ = bf16[4,2,6,32,128]{4,3,2,1,0:T(8,128)(2,1)S(1)} collective-permute-done((bf16[4,2,6,32,128]{4,3,2,1,0:T(8,128)(2,1)S(1)}, bf16[4,2,6,32,128]{4,3,2,1,0:T(8,128)(2,1)S(1)}, u32[]{:S(2)}, u32[]{:S(2)}) %collective-permute-start.15) | collective-permute-done | bytes 393248 | tf_op jit(solution)/shard_map/ppermute | solution.py:351
  96.4 0.6 collective-permute-done.16.refs_3_
  97.0 5.4 %shard_map.96 = bf16[8,2,3,32,128]{4,3,2,1,0:T(8,128)(2,1)S(1)} custom-call(s32[243]{0:T(256)S(1)} %concatenate.3.sc, bf16[8,2,3,32,128]{4,3,2,1,0:T(8,128)(2,1)S(1)} %bitcast.8, bf16[4,2,6,32,128]{4,3,2,1,0:T(8,128)(2,1)S(1)} %collective-permute-done.13.refs_0_, bf16[4,2,6,32,128]{4,3,2,1,0:T(8,128)(2,1)S(1)} %collective-permute-done.14.refs_1_, ...), custom_call_target="tpu_custom_call" | custom-call | flops 335544320 | bytes 8388608 | tf_op jit(solution)/shard_map/pallas_call | solution.py:316
  102.4 12.8 %all_to_all.15.ref = bf16[16,3,32,128]{3,2,1,0:T(8,128)(2,1)} all-to-all(bf16[16,3,32,128]{3,2,1,0:T(8,128)(2,1)S(1)} %bitcast.9), channel_id=1, replica_groups=mesh['zh'=4,'y'=4,'c'=2,'xh'=2,'xl'=2,'zl'=2] {'y','xh','xl'}, dimensions={0} | all-to-all | bytes 786432 | tf_op jit(solution)/shard_map/all_to_all | solution.py:380
  115.2 1.8 %shard_map.97 = bf16[3,32,2048]{2,1,0:T(8,128)(2,1)} custom-call(bf16[16,3,32,128]{3,2,1,0:T(8,128)(2,1)} %all_to_all.15.ref), custom_call_target="tpu_custom_call" | custom-call | tf_op jit(solution)/shard_map/pallas_call | solution.py:60
  (60 shorter events, 2.8 us)
Async XLA Ops:
  2.2 20.8 %all-to-all-start = ((bf16[16,6,32,128]{3,2,1,0:T(8,128)(2,1)}), bf16[16,6,32,128]{3,2,1,0:T(8,128)(2,1)S(1)}, u32[]{:S(2)}, u32[]{:S(2)}) async-start(bf16[16,6,32,128]{3,2,1,0:T(8,128)(2,1)} %shard_map.91), calls=%async_computation | async-start | bytes 1572864 | tf_op jit(solution)/shard_map/all_to_all | solution.py:355
  9.7 0.7 copy-start.4
  9.8 0.7 copy-start.5
  10.4 0.7 copy-start.1
  11.4 0.7 copy-start.3
  12.1 1.5 %copy-start = (s32[8192]{0:T(1024)S(1)}, s32[8192]{0:T(1024)}, u32[]{:S(2)}) copy-start(s32[8192]{0:T(1024)} %param.13) | copy-start | bytes 98308
  12.4 0.7 copy-start.2
  23.0 12.3 %collective-permute-start.5 = (bf16[4,2,6,32,128]{4,3,2,1,0:T(8,128)(2,1)S(1)}, bf16[4,2,6,32,128]{4,3,2,1,0:T(8,128)(2,1)S(1)}, u32[]{:S(2)}, u32[]{:S(2)}) collective-permute-start(bf16[4,2,6,32,128]{4,3,2,1,0:T(8,128)(2,1)S(1)} %get-tuple-element.55.refs_3_), channel_id=1, source_target_pairs={{0,193},{1,0},{64,1},{65,64},{128,65},{129,128},{192,129},{193,192... | collective-permute-start | bytes 1179656 | tf_op jit(solution)/shard_map/ppermute | solution.py:347
  28.6 9.5 %collective-permute-start.1 = (bf16[4,2,6,32,128]{4,3,2,1,0:T(8,128)(2,1)S(1)}, bf16[4,2,6,32,128]{4,3,2,1,0:T(8,128)(2,1)S(1)}, u32[]{:S(2)}, u32[]{:S(2)}) collective-permute-start(bf16[4,2,6,32,128]{4,3,2,1,0:T(8,128)(2,1)S(1)} %get-tuple-element.56.refs_2_), channel_id=1, source_target_pairs={{0,1},{1,64},{64,65},{65,128},{128,129},{129,192},{192,193},{193,0... | collective-permute-start | bytes 1179656 | tf_op jit(solution)/shard_map/ppermute | solution.py:347
  28.6 12.2 %all-to-all-start.1 = ((bf16[16,3,32,128]{3,2,1,0:T(8,128)(2,1)}), bf16[16,3,32,128]{3,2,1,0:T(8,128)(2,1)S(1)}, u32[]{:S(2)}, u32[]{:S(2)}) async-start(bf16[16,3,32,128]{3,2,1,0:T(8,128)(2,1)} %shard_map.92), calls=%async_computation.1 | async-start | bytes 786432 | tf_op jit(solution)/shard_map/all_to_all | solution.py:358
  32.5 13.9 %collective-permute-start.3 = (bf16[4,2,6,32,128]{4,3,2,1,0:T(8,128)(2,1)S(1)}, bf16[4,2,6,32,128]{4,3,2,1,0:T(8,128)(2,1)S(1)}, u32[]{:S(2)}, u32[]{:S(2)}) collective-permute-start(bf16[4,2,6,32,128]{4,3,2,1,0:T(8,128)(2,1)S(1)} %get-tuple-element.55.refs_3_), channel_id=1, source_target_pairs={{0,1},{1,64},{64,65},{65,128},{128,129},{129,192},{192,193},{193,0... | collective-permute-start | bytes 1179656 | tf_op jit(solution)/shard_map/ppermute | solution.py:347
  32.5 13.8 %collective-permute-start.4 = (bf16[4,2,6,32,128]{4,3,2,1,0:T(8,128)(2,1)S(1)}, bf16[4,2,6,32,128]{4,3,2,1,0:T(8,128)(2,1)S(1)}, u32[]{:S(2)}, u32[]{:S(2)}) collective-permute-start(bf16[4,2,6,32,128]{4,3,2,1,0:T(8,128)(2,1)S(1)} %get-tuple-element.56.refs_2_), channel_id=1, source_target_pairs={{0,193},{1,0},{64,1},{65,64},{128,65},{129,128},{192,129},{193,192... | collective-permute-start | bytes 1179656 | tf_op jit(solution)/shard_map/ppermute | solution.py:347
  35.3 17.4 %collective-permute-start.8 = (bf16[4,2,6,32,128]{4,3,2,1,0:T(8,128)(2,1)S(1)}, bf16[4,2,6,32,128]{4,3,2,1,0:T(8,128)(2,1)S(1)}, u32[]{:S(2)}, u32[]{:S(2)}) collective-permute-start(bf16[4,2,6,32,128]{4,3,2,1,0:T(8,128)(2,1)S(1)} %collective-permute-done.5.refs_5_), channel_id=1, source_target_pairs={{0,193},{1,0},{64,1},{65,64},{128,65},{129,128},{192,129},{193,192... | collective-permute-start | bytes 1179656 | tf_op jit(solution)/shard_map/ppermute | solution.py:347
  38.2 17.9 %collective-permute-start.2 = (bf16[4,2,6,32,128]{4,3,2,1,0:T(8,128)(2,1)S(1)}, bf16[4,2,6,32,128]{4,3,2,1,0:T(8,128)(2,1)S(1)}, u32[]{:S(2)}, u32[]{:S(2)}) collective-permute-start(bf16[4,2,6,32,128]{4,3,2,1,0:T(8,128)(2,1)S(1)} %collective-permute-done.1.refs_0_), channel_id=1, source_target_pairs={{0,1},{1,64},{64,65},{65,128},{128,129},{129,192},{192,193},{193,0... | collective-permute-start | bytes 1179656 | tf_op jit(solution)/shard_map/ppermute | solution.py:347
  40.8 15.3 %collective-permute-start = (bf16[8,2,3,32,128]{4,3,2,1,0:T(8,128)(2,1)S(1)}, bf16[8,2,3,32,128]{4,3,2,1,0:T(8,128)(2,1)S(1)}, u32[]{:S(2)}, u32[]{:S(2)}) collective-permute-start(bf16[8,2,3,32,128]{4,3,2,1,0:T(8,128)(2,1)S(1)} %bitcast.4), channel_id=1, source_target_pairs={{0,8},{8,0},{1,9},{9,1},{2,10},{10,2},{3,11},{11,3},{4,12},{12,4},... | collective-permute-start | bytes 1179656 | tf_op jit(solution)/shard_map/ppermute | solution.py:351
  46.3 18.6 %collective-permute-start.6 = (bf16[4,2,6,32,128]{4,3,2,1,0:T(8,128)(2,1)S(1)}, bf16[4,2,6,32,128]{4,3,2,1,0:T(8,128)(2,1)S(1)}, u32[]{:S(2)}, u32[]{:S(2)}) collective-permute-start(bf16[4,2,6,32,128]{4,3,2,1,0:T(8,128)(2,1)S(1)} %collective-permute-done.3.refs_1_), channel_id=1, source_target_pairs={{0,1},{1,64},{64,65},{65,128},{128,129},{129,192},{192,193},{193,0... | collective-permute-start | bytes 1179656 | tf_op jit(solution)/shard_map/ppermute | solution.py:347
  46.3 18.6 %collective-permute-start.7 = (bf16[4,2,6,32,128]{4,3,2,1,0:T(8,128)(2,1)S(1)}, bf16[4,2,6,32,128]{4,3,2,1,0:T(8,128)(2,1)S(1)}, u32[]{:S(2)}, u32[]{:S(2)}) collective-permute-start(bf16[4,2,6,32,128]{4,3,2,1,0:T(8,128)(2,1)S(1)} %collective-permute-done.4.refs_4_), channel_id=1, source_target_pairs={{0,193},{1,0},{64,1},{65,64},{128,65},{129,128},{192,129},{193,192... | collective-permute-start | bytes 1179656 | tf_op jit(solution)/shard_map/ppermute | solution.py:347
  52.7 22.1 %collective-permute-start.10 = (bf16[4,2,6,32,128]{4,3,2,1,0:T(8,128)(2,1)S(1)}, bf16[4,2,6,32,128]{4,3,2,1,0:T(8,128)(2,1)S(1)}, u32[]{:S(2)}, u32[]{:S(2)}) collective-permute-start(bf16[4,2,6,32,128]{4,3,2,1,0:T(8,128)(2,1)S(1)} %collective-permute-done.8.refs_3_), channel_id=1, source_target_pairs={{0,193},{1,0},{64,1},{65,64},{128,65},{129,128},{192,129},{193,192... | collective-permute-start | bytes 1179656 | tf_op jit(solution)/shard_map/ppermute | solution.py:347
  56.1 18.7 %collective-permute-start.9 = (bf16[4,2,6,32,128]{4,3,2,1,0:T(8,128)(2,1)S(1)}, bf16[4,2,6,32,128]{4,3,2,1,0:T(8,128)(2,1)S(1)}, u32[]{:S(2)}, u32[]{:S(2)}) collective-permute-start(bf16[4,2,6,32,128]{4,3,2,1,0:T(8,128)(2,1)S(1)} %collective-permute-done.2.refs_0_), channel_id=1, source_target_pairs={{0,1},{1,64},{64,65},{65,128},{128,129},{129,192},{192,193},{193,0... | collective-permute-start | bytes 1179656 | tf_op jit(solution)/shard_map/ppermute | solution.py:347
  64.9 15.1 %collective-permute-start.11 = (bf16[4,2,6,32,128]{4,3,2,1,0:T(8,128)(2,1)S(1)}, bf16[4,2,6,32,128]{4,3,2,1,0:T(8,128)(2,1)S(1)}, u32[]{:S(2)}, u32[]{:S(2)}) collective-permute-start(bf16[4,2,6,32,128]{4,3,2,1,0:T(8,128)(2,1)S(1)} %collective-permute-done.6.refs_1_), channel_id=1, source_target_pairs={{0,1},{1,64},{64,65},{65,128},{128,129},{129,192},{192,193},{193,0... | collective-permute-start | bytes 1179656 | tf_op jit(solution)/shard_map/ppermute | solution.py:347
  65.0 15.0 %collective-permute-start.12 = (bf16[4,2,6,32,128]{4,3,2,1,0:T(8,128)(2,1)S(1)}, bf16[4,2,6,32,128]{4,3,2,1,0:T(8,128)(2,1)S(1)}, u32[]{:S(2)}, u32[]{:S(2)}) collective-permute-start(bf16[4,2,6,32,128]{4,3,2,1,0:T(8,128)(2,1)S(1)} %collective-permute-done.7.refs_2_), channel_id=1, source_target_pairs={{0,193},{1,0},{64,1},{65,64},{128,65},{129,128},{192,129},{193,192... | collective-permute-start | bytes 1179656 | tf_op jit(solution)/shard_map/ppermute | solution.py:347
  74.8 13.6 %collective-permute-start.13 = (bf16[4,2,6,32,128]{4,3,2,1,0:T(8,128)(2,1)S(1)}, bf16[4,2,6,32,128]{4,3,2,1,0:T(8,128)(2,1)S(1)}, u32[]{:S(2)}, u32[]{:S(2)}) collective-permute-start(bf16[4,2,6,32,128]{4,3,2,1,0:T(8,128)(2,1)S(1)} %collective-permute-done.9.refs_0_), channel_id=1, source_target_pairs={{0,1},{1,64},{64,65},{65,128},{128,129},{129,192},{192,193},{193,0... | collective-permute-start | bytes 1179656 | tf_op jit(solution)/shard_map/ppermute | solution.py:347
  74.9 13.5 %collective-permute-start.14 = (bf16[4,2,6,32,128]{4,3,2,1,0:T(8,128)(2,1)S(1)}, bf16[4,2,6,32,128]{4,3,2,1,0:T(8,128)(2,1)S(1)}, u32[]{:S(2)}, u32[]{:S(2)}) collective-permute-start(bf16[4,2,6,32,128]{4,3,2,1,0:T(8,128)(2,1)S(1)} %collective-permute-done.10.refs_3_), channel_id=1, source_target_pairs={{0,193},{1,0},{64,1},{65,64},{128,65},{129,128},{192,129},{193,192... | collective-permute-start | bytes 1179656 | tf_op jit(solution)/shard_map/ppermute | solution.py:347
  88.5 8.5 %collective-permute-start.17 = (f32[8,2,4,32,128]{4,3,2,1,0:T(8,128)S(1)}, f32[8,2,4,32,128]{4,3,2,1,0:T(8,128)S(1)}, u32[]{:S(2)}, u32[]{:S(2)}) collective-permute-start(f32[8,2,4,32,128]{4,3,2,1,0:T(8,128)S(1)} %get-tuple-element.46), channel_id=1, source_target_pairs={{0,8},{8,0},{1,9},{9,1},{2,10},{10,2},{3,11},{11,3},{4,12},{12,4},... | collective-permute-start | bytes 3145736 | tf_op jit(solution)/shard_map/ppermute | solution.py:351
  93.6 2.8 %collective-permute-start.15 = (bf16[4,2,6,32,128]{4,3,2,1,0:T(8,128)(2,1)S(1)}, bf16[4,2,6,32,128]{4,3,2,1,0:T(8,128)(2,1)S(1)}, u32[]{:S(2)}, u32[]{:S(2)}) collective-permute-start(bf16[4,2,6,32,128]{4,3,2,1,0:T(8,128)(2,1)S(1)} %collective-permute-done.13.refs_0_), channel_id=1, source_target_pairs={{0,8},{8,0},{1,9},{9,1},{2,10},{10,2},{3,11},{11,3},{4,12},{12,4},... | collective-permute-start | bytes 1179656 | tf_op jit(solution)/shard_map/ppermute | solution.py:351
  93.7 3.3 %collective-permute-start.16 = (bf16[4,2,6,32,128]{4,3,2,1,0:T(8,128)(2,1)S(1)}, bf16[4,2,6,32,128]{4,3,2,1,0:T(8,128)(2,1)S(1)}, u32[]{:S(2)}, u32[]{:S(2)}) collective-permute-start(bf16[4,2,6,32,128]{4,3,2,1,0:T(8,128)(2,1)S(1)} %collective-permute-done.14.refs_1_), channel_id=1, source_target_pairs={{0,8},{8,0},{1,9},{9,1},{2,10},{10,2},{3,11},{11,3},{4,12},{12,4},... | collective-permute-start | bytes 1179656 | tf_op jit(solution)/shard_map/ppermute | solution.py:351

commit v6 on v5

--- a/solution.py
+++ b/solution.py
@@ -354,8 +354,7 @@
 def shards(query_set, key_set, value_set, block_order, documents):
     kv = lax.all_to_all(split_heads(key_set, value_set), XY, 0, 0).reshape(8, 2, 6, SLICE, HD)
     sc = scalars(block_order, documents, *(lax.axis_index(a) for a in ("zh", "zl", "c")))
-    kv, q, sc = lax.optimization_barrier((kv, split_heads(query_set), sc))
-    q = lax.all_to_all(q, XY, 0, 0).reshape(8, 2, 3, SLICE, HD)
+    kv, packed, sc = lax.optimization_barrier((kv, split_heads(query_set), sc))
     planes = {0: [kv[:4], kv[4:]]}
 
     def advance(step):
@@ -366,6 +365,8 @@
         return attend(sc, queries, [p for o in SETS[i] for p in planes[o]], i, held)
 
     advance(1)
+    packed, planes[-1][1] = lax.optimization_barrier((packed, planes[-1][1]))
+    q = lax.all_to_all(packed, XY, 0, 0).reshape(8, 2, 3, SLICE, HD)
     advance(2)
     queries = (q, swap_cores(q))
     state = attend_set(0)

time: 118 us -> 126 us (1.068)
  waiting for transfers between devices: 21.4 us -> 26.9 us
  blocking collectives: 12.8 us -> 17.9 us
  starting transfers between devices: 43.9 us -> 42.4 us
    ppermute x14, starting transfers between devices: 23.2 us -> 17.3 us  [hop(): lax.ppermute(block, Z, [(i, (i + direction) % NZ) for i in range(NZ)])]
    all_to_all x1, blocking collectives: 12.8 us -> 17.9 us  [shards(): done = lax.all_to_all(done.reshape(HEADS, 3, SLICE, HD), XY, 0, 0)]
    ppermute x14, waiting for transfers between devices: 9.59 us -> 12.7 us  [hop(): lax.ppermute(block, Z, [(i, (i + direction) % NZ) for i in range(NZ)])]
    ppermute x4, starting transfers between devices: 9.28 us -> 12.4 us  [swap_cores(): return lax.ppermute(block, 'c', [(0, 1), (1, 0)])]
    all_to_all x1, waiting for transfers between devices: 2.61 us -> 4.95 us  [shards(): q = lax.all_to_all(packed, XY, 0, 0).reshape(8, 2, 3, SLICE, HD)]
    all_to_all x1, starting transfers between devices: 3.81 us -> 5.11 us  [shards(): q = lax.all_to_all(packed, XY, 0, 0).reshape(8, 2, 3, SLICE, HD)]
  transfers between devices with their start and end apart: 20 -> 20, of which waited for: 8 -> 8; matrix products, arithmetic and copies ran while one was open for 2% -> 2% of each run, Pallas kernels for 21% -> 19%
where the time goes in v6:
time: 126 us; the launch traced here: 125 us
  starting transfers between devices  42.4 us (34%)
  Pallas kernels  33 us (26%)
  waiting for transfers between devices  26.9 us (21%)
  blocking collectives  17.9 us (14%)
  local copies, waits for them, and re-layouts  3.73 us (3%)
    pallas_call x3, Pallas kernels, attend(): pl.pallas_call(kernel, out_shape=(part, part), in_specs=[SMEM] + [ANY] *...  22.5 us
    all_to_all x1, blocking collectives, shards(): done = lax.all_to_all(done.reshape(HEADS, 3, SLICE, HD), XY, 0, 0)  17.9 us
    ppermute x14, starting transfers between devices, hop(): lax.ppermute(block, Z, [(i, (i + direction) % NZ) for i in range(NZ)])  17.3 us
    ppermute x14, waiting for transfers between devices, hop(): lax.ppermute(block, Z, [(i, (i + direction) % NZ) for i in range(NZ)])  12.7 us
    ppermute x4, starting transfers between devices, swap_cores(): return lax.ppermute(block, 'c', [(0, 1), (1, 0)])  12.4 us
    all_to_all x1, starting transfers between devices, shards(): lax.all_to_all(split_heads(key_set, value_set), XY, 0, 0)  7.58 us
    all_to_all x1, waiting for transfers between devices, shards(): lax.all_to_all(split_heads(key_set, value_set), XY, 0, 0)  6.32 us
    all_to_all x1, starting transfers between devices, shards(): q = lax.all_to_all(packed, XY, 0, 0).reshape(8, 2, 3, SLICE, HD)  5.11 us
  transfers between devices with their start and end apart: 20, of which 8 were waited for; matrix products, arithmetic and copies ran while one was open for 2% of the time, Pallas kernels for 19%

profile of v6, /device:TPU:1, one launch (start us, length us, event | category | flops | bytes accessed | tf_op | source)
XLA Modules:
  0.0 125.4 jit_solution(7826451048242582259)
XLA Ops:
  0.0 2.1 %shard_map.91 = bf16[16,6,32,128]{3,2,1,0:T(8,128)(2,1)} custom-call(bf16[3,32,2048]{2,1,0:T(8,128)(2,1)} %refs_0_.2, bf16[3,32,2048]{2,1,0:T(8,128)(2,1)} %refs_1_.1), custom_call_target="tpu_custom_call" | custom-call | tf_op jit(solution)/shard_map/pallas_call | solution.py:47
  2.2 7.6 %all-to-all-start = ((bf16[16,6,32,128]{3,2,1,0:T(8,128)(2,1)}), bf16[16,6,32,128]{3,2,1,0:T(8,128)(2,1)S(1)}, u32[]{:S(2)}, u32[]{:S(2)}) async-start(bf16[16,6,32,128]{3,2,1,0:T(8,128)(2,1)} %shard_map.91), calls=%async_computation | async-start | bytes 1572864 | tf_op jit(solution)/shard_map/all_to_all | solution.py:355
  9.8 0.6 copy-done.4
  10.5 0.6 copy-done.1
  11.4 0.6 copy-done.3
  12.5 0.6 copy-done.2
  14.7 1.8 %shard_map.92 = bf16[16,3,32,128]{3,2,1,0:T(8,128)(2,1)} custom-call(bf16[3,32,2048]{2,1,0:T(8,128)(2,1)} %refs_0_.3), custom_call_target="tpu_custom_call" | custom-call | tf_op jit(solution)/shard_map/pallas_call | solution.py:47
  16.6 6.3 %all-to-all-done = bf16[16,6,32,128]{3,2,1,0:T(8,128)(2,1)S(1)} async-done(((bf16[16,6,32,128]{3,2,1,0:T(8,128)(2,1)}), bf16[16,6,32,128]{3,2,1,0:T(8,128)(2,1)S(1)}, u32[]{:S(2)}, u32[]{:S(2)}) %all-to-all-start) | async-done | bytes 786464 | tf_op jit(solution)/shard_map/all_to_all | solution.py:355
  23.0 1.7 %collective-permute-start = (bf16[4,2,6,32,128]{4,3,2,1,0:T(8,128)(2,1)S(1)}, bf16[4,2,6,32,128]{4,3,2,1,0:T(8,128)(2,1)S(1)}, u32[]{:S(2)}, u32[]{:S(2)}) collective-permute-start(bf16[4,2,6,32,128]{4,3,2,1,0:T(8,128)(2,1)S(1)} %get-tuple-element.60.refs_3_), channel_id=1, source_target_pairs={{0,1},{1,64},{64,65},{65,128},{128,129},{129,192},{192,193},{193,0... | collective-permute-start | bytes 1179656 | tf_op jit(solution)/shard_map/ppermute | solution.py:347
  24.7 4.0 %collective-permute-start.5 = (bf16[4,2,6,32,128]{4,3,2,1,0:T(8,128)(2,1)S(1)}, bf16[4,2,6,32,128]{4,3,2,1,0:T(8,128)(2,1)S(1)}, u32[]{:S(2)}, u32[]{:S(2)}) collective-permute-start(bf16[4,2,6,32,128]{4,3,2,1,0:T(8,128)(2,1)S(1)} %get-tuple-element.60.refs_3_), channel_id=1, source_target_pairs={{0,193},{1,0},{64,1},{65,64},{128,65},{129,128},{192,129},{193,192... | collective-permute-start | bytes 1179656 | tf_op jit(solution)/shard_map/ppermute | solution.py:347
  28.7 7.1 %collective-permute-done.refs_1_ = bf16[4,2,6,32,128]{4,3,2,1,0:T(8,128)(2,1)S(1)} collective-permute-done((bf16[4,2,6,32,128]{4,3,2,1,0:T(8,128)(2,1)S(1)}, bf16[4,2,6,32,128]{4,3,2,1,0:T(8,128)(2,1)S(1)}, u32[]{:S(2)}, u32[]{:S(2)}) %collective-permute-start) | collective-permute-done | bytes 393248 | tf_op jit(solution)/shard_map/ppermute | solution.py:347
  35.8 5.1 %all-to-all-start.1 = ((bf16[16,3,32,128]{3,2,1,0:T(8,128)(2,1)}), bf16[16,3,32,128]{3,2,1,0:T(8,128)(2,1)S(1)}, u32[]{:S(2)}, u32[]{:S(2)}) async-start(bf16[16,3,32,128]{3,2,1,0:T(8,128)(2,1)} %shard_map.92), calls=%async_computation.1 | async-start | bytes 786432 | tf_op jit(solution)/shard_map/all_to_all | solution.py:369
  40.9 1.2 collective-permute-start.4
  42.1 0.7 collective-permute-start.8
  42.9 1.4 %collective-permute-done.2.refs_0_ = bf16[4,2,6,32,128]{4,3,2,1,0:T(8,128)(2,1)S(1)} collective-permute-done((bf16[4,2,6,32,128]{4,3,2,1,0:T(8,128)(2,1)S(1)}, bf16[4,2,6,32,128]{4,3,2,1,0:T(8,128)(2,1)S(1)}, u32[]{:S(2)}, u32[]{:S(2)}) %collective-permute-start.2) | collective-permute-done | bytes 393248 | tf_op jit(solution)/shard_map/ppermute | solution.py:347
  44.2 5.0 %all-to-all-done.1 = bf16[16,3,32,128]{3,2,1,0:T(8,128)(2,1)S(1)} async-done(((bf16[16,3,32,128]{3,2,1,0:T(8,128)(2,1)}), bf16[16,3,32,128]{3,2,1,0:T(8,128)(2,1)S(1)}, u32[]{:S(2)}, u32[]{:S(2)}) %all-to-all-start.1) | async-done | bytes 393248 | tf_op jit(solution)/shard_map/all_to_all | solution.py:369
  49.2 5.0 %collective-permute-start.1 = (bf16[8,2,3,32,128]{4,3,2,1,0:T(8,128)(2,1)S(1)}, bf16[8,2,3,32,128]{4,3,2,1,0:T(8,128)(2,1)S(1)}, u32[]{:S(2)}, u32[]{:S(2)}) collective-permute-start(bf16[8,2,3,32,128]{4,3,2,1,0:T(8,128)(2,1)S(1)} %bitcast.4), channel_id=1, source_target_pairs={{0,8},{8,0},{1,9},{9,1},{2,10},{10,2},{3,11},{11,3},{4,12},{12,4},... | collective-permute-start | bytes 1179656 | tf_op jit(solution)/shard_map/ppermute | solution.py:351
  54.2 2.7 %collective-permute-start.7 = (bf16[4,2,6,32,128]{4,3,2,1,0:T(8,128)(2,1)S(1)}, bf16[4,2,6,32,128]{4,3,2,1,0:T(8,128)(2,1)S(1)}, u32[]{:S(2)}, u32[]{:S(2)}) collective-permute-start(bf16[4,2,6,32,128]{4,3,2,1,0:T(8,128)(2,1)S(1)} %collective-permute-done.4.refs_4_), channel_id=1, source_target_pairs={{0,193},{1,0},{64,1},{65,64},{128,65},{129,128},{192,129},{193,192... | collective-permute-start | bytes 1179656 | tf_op jit(solution)/shard_map/ppermute | solution.py:347
  56.8 1.1 collective-permute-start.10
  58.3 8.8 %shard_map.93 = (f32[8,2,4,32,128]{4,3,2,1,0:T(8,128)S(1)}, f32[8,2,4,32,128]{4,3,2,1,0:T(8,128)S(1)}) custom-call(s32[243]{0:T(256)S(1)} %concatenate.3.sc, bf16[8,2,3,32,128]{4,3,2,1,0:T(8,128)(2,1)S(1)} %bitcast.5, bf16[8,2,3,32,128]{4,3,2,1,0:T(8,128)(2,1)S(1)} %collective-permute-done.1.q_other, ...), custom_call_target="tpu_custom_call" | custom-call | flops 1006632960 | bytes 8388608 | tf_op jit(solution)/shard_map/pallas_call | solution.py:277
  67.2 2.7 %collective-permute-start.12 = (bf16[4,2,6,32,128]{4,3,2,1,0:T(8,128)(2,1)S(1)}, bf16[4,2,6,32,128]{4,3,2,1,0:T(8,128)(2,1)S(1)}, u32[]{:S(2)}, u32[]{:S(2)}) collective-permute-start(bf16[4,2,6,32,128]{4,3,2,1,0:T(8,128)(2,1)S(1)} %collective-permute-done.7.refs_2_), channel_id=1, source_target_pairs={{0,193},{1,0},{64,1},{65,64},{128,65},{129,128},{192,129},{193,192... | collective-permute-start | bytes 1179656 | tf_op jit(solution)/shard_map/ppermute | solution.py:347
  69.9 6.8 %shard_map.94 = (f32[8,2,4,32,128]{4,3,2,1,0:T(8,128)S(1)}, f32[8,2,4,32,128]{4,3,2,1,0:T(8,128)S(1)}) custom-call(s32[243]{0:T(256)S(1)} %concatenate.3.sc, bf16[8,2,3,32,128]{4,3,2,1,0:T(8,128)(2,1)S(1)} %bitcast.6, bf16[8,2,3,32,128]{4,3,2,1,0:T(8,128)(2,1)S(1)} %collective-permute-done.1.q_other, ...), custom_call_target="tpu_custom_call" | custom-call | flops 671088640 | bytes 8388608 | tf_op jit(solution)/shard_map/pallas_call | solution.py:277
  76.8 2.7 %collective-permute-start.14 = (bf16[4,2,6,32,128]{4,3,2,1,0:T(8,128)(2,1)S(1)}, bf16[4,2,6,32,128]{4,3,2,1,0:T(8,128)(2,1)S(1)}, u32[]{:S(2)}, u32[]{:S(2)}) collective-permute-start(bf16[4,2,6,32,128]{4,3,2,1,0:T(8,128)(2,1)S(1)} %collective-permute-done.10.refs_3_), channel_id=1, source_target_pairs={{0,193},{1,0},{64,1},{65,64},{128,65},{129,128},{192,129},{193,192... | collective-permute-start | bytes 1179656 | tf_op jit(solution)/shard_map/ppermute | solution.py:347
  79.5 2.9 %collective-permute-done.12.refs_2_ = bf16[4,2,6,32,128]{4,3,2,1,0:T(8,128)(2,1)S(1)} collective-permute-done((bf16[4,2,6,32,128]{4,3,2,1,0:T(8,128)(2,1)S(1)}, bf16[4,2,6,32,128]{4,3,2,1,0:T(8,128)(2,1)S(1)}, u32[]{:S(2)}, u32[]{:S(2)}) %collective-permute-start.12) | collective-permute-done | bytes 393248 | tf_op jit(solution)/shard_map/ppermute | solution.py:347
  82.4 6.8 %shard_map.95 = (f32[8,2,4,32,128]{4,3,2,1,0:T(8,128)S(1)}, f32[8,2,4,32,128]{4,3,2,1,0:T(8,128)S(1)}) custom-call(s32[243]{0:T(256)S(1)} %concatenate.3.sc, bf16[8,2,3,32,128]{4,3,2,1,0:T(8,128)(2,1)S(1)} %bitcast.7, bf16[8,2,3,32,128]{4,3,2,1,0:T(8,128)(2,1)S(1)} %collective-permute-done.1.q_other, ...), custom_call_target="tpu_custom_call" | custom-call | flops 671088640 | bytes 8388608 | tf_op jit(solution)/shard_map/pallas_call | solution.py:277
  89.2 1.4 %collective-permute-done.14.refs_1_ = bf16[4,2,6,32,128]{4,3,2,1,0:T(8,128)(2,1)S(1)} collective-permute-done((bf16[4,2,6,32,128]{4,3,2,1,0:T(8,128)(2,1)S(1)}, bf16[4,2,6,32,128]{4,3,2,1,0:T(8,128)(2,1)S(1)}, u32[]{:S(2)}, u32[]{:S(2)}) %collective-permute-start.14) | collective-permute-done | bytes 393248 | tf_op jit(solution)/shard_map/ppermute | solution.py:347
  90.6 6.9 %collective-permute-start.17 = (f32[8,2,4,32,128]{4,3,2,1,0:T(8,128)S(1)}, f32[8,2,4,32,128]{4,3,2,1,0:T(8,128)S(1)}, u32[]{:S(2)}, u32[]{:S(2)}) collective-permute-start(f32[8,2,4,32,128]{4,3,2,1,0:T(8,128)S(1)} %get-tuple-element.50), channel_id=1, source_target_pairs={{0,8},{8,0},{1,9},{9,1},{2,10},{10,2},{3,11},{11,3},{4,12},{12,4},... | collective-permute-start | bytes 3145736 | tf_op jit(solution)/shard_map/ppermute | solution.py:351
  98.0 2.3 %collective-permute-done.15.refs_2_ = bf16[4,2,6,32,128]{4,3,2,1,0:T(8,128)(2,1)S(1)} collective-permute-done((bf16[4,2,6,32,128]{4,3,2,1,0:T(8,128)(2,1)S(1)}, bf16[4,2,6,32,128]{4,3,2,1,0:T(8,128)(2,1)S(1)}, u32[]{:S(2)}, u32[]{:S(2)}) %collective-permute-start.15) | collective-permute-done | bytes 393248 | tf_op jit(solution)/shard_map/ppermute | solution.py:351
  100.4 0.6 collective-permute-done.16.refs_3_
  100.9 4.7 %shard_map.96 = bf16[8,2,3,32,128]{4,3,2,1,0:T(8,128)(2,1)S(1)} custom-call(s32[243]{0:T(256)S(1)} %concatenate.3.sc, bf16[8,2,3,32,128]{4,3,2,1,0:T(8,128)(2,1)S(1)} %bitcast.8, bf16[4,2,6,32,128]{4,3,2,1,0:T(8,128)(2,1)S(1)} %collective-permute-done.13.refs_0_, bf16[4,2,6,32,128]{4,3,2,1,0:T(8,128)(2,1)S(1)} %collective-permute-done.14.refs_1_, ...), custom_call_target="tpu_custom_call" | custom-call | flops 335544320 | bytes 8388608 | tf_op jit(solution)/shard_map/pallas_call | solution.py:316
  105.7 17.9 %all_to_all.15.ref = bf16[16,3,32,128]{3,2,1,0:T(8,128)(2,1)} all-to-all(bf16[16,3,32,128]{3,2,1,0:T(8,128)(2,1)S(1)} %bitcast.9), channel_id=1, replica_groups=mesh['zh'=4,'y'=4,'c'=2,'xh'=2,'xl'=2,'zl'=2] {'y','xh','xl'}, dimensions={0} | all-to-all | bytes 786432 | tf_op jit(solution)/shard_map/all_to_all | solution.py:381
  123.5 1.8 %shard_map.97 = bf16[3,32,2048]{2,1,0:T(8,128)(2,1)} custom-call(bf16[16,3,32,128]{3,2,1,0:T(8,128)(2,1)} %all_to_all.15.ref), custom_call_target="tpu_custom_call" | custom-call | tf_op jit(solution)/shard_map/pallas_call | solution.py:60
  (60 shorter events, 3.5 us)
Async XLA Ops:
  2.2 20.8 %all-to-all-start = ((bf16[16,6,32,128]{3,2,1,0:T(8,128)(2,1)}), bf16[16,6,32,128]{3,2,1,0:T(8,128)(2,1)S(1)}, u32[]{:S(2)}, u32[]{:S(2)}) async-start(bf16[16,6,32,128]{3,2,1,0:T(8,128)(2,1)} %shard_map.91), calls=%async_computation | async-start | bytes 1572864 | tf_op jit(solution)/shard_map/all_to_all | solution.py:355
  9.7 0.7 copy-start.4
  9.8 0.7 copy-start.5
  10.4 0.7 copy-start.1
  11.4 0.7 copy-start.3
  12.1 1.5 %copy-start = (s32[8192]{0:T(1024)S(1)}, s32[8192]{0:T(1024)}, u32[]{:S(2)}) copy-start(s32[8192]{0:T(1024)} %param.13) | copy-start | bytes 98308
  12.4 0.7 copy-start.2
  23.0 12.8 %collective-permute-start = (bf16[4,2,6,32,128]{4,3,2,1,0:T(8,128)(2,1)S(1)}, bf16[4,2,6,32,128]{4,3,2,1,0:T(8,128)(2,1)S(1)}, u32[]{:S(2)}, u32[]{:S(2)}) collective-permute-start(bf16[4,2,6,32,128]{4,3,2,1,0:T(8,128)(2,1)S(1)} %get-tuple-element.60.refs_3_), channel_id=1, source_target_pairs={{0,1},{1,64},{64,65},{65,128},{128,129},{129,192},{192,193},{193,0... | collective-permute-start | bytes 1179656 | tf_op jit(solution)/shard_map/ppermute | solution.py:347
  24.7 17.4 %collective-permute-start.5 = (bf16[4,2,6,32,128]{4,3,2,1,0:T(8,128)(2,1)S(1)}, bf16[4,2,6,32,128]{4,3,2,1,0:T(8,128)(2,1)S(1)}, u32[]{:S(2)}, u32[]{:S(2)}) collective-permute-start(bf16[4,2,6,32,128]{4,3,2,1,0:T(8,128)(2,1)S(1)} %get-tuple-element.60.refs_3_), channel_id=1, source_target_pairs={{0,193},{1,0},{64,1},{65,64},{128,65},{129,128},{192,129},{193,192... | collective-permute-start | bytes 1179656 | tf_op jit(solution)/shard_map/ppermute | solution.py:347
  28.7 15.5 %collective-permute-start.2 = (bf16[4,2,6,32,128]{4,3,2,1,0:T(8,128)(2,1)S(1)}, bf16[4,2,6,32,128]{4,3,2,1,0:T(8,128)(2,1)S(1)}, u32[]{:S(2)}, u32[]{:S(2)}) collective-permute-start(bf16[4,2,6,32,128]{4,3,2,1,0:T(8,128)(2,1)S(1)} %get-tuple-element.59.refs_2_), channel_id=1, source_target_pairs={{0,1},{1,64},{64,65},{65,128},{128,129},{129,192},{192,193},{193,0... | collective-permute-start | bytes 1179656 | tf_op jit(solution)/shard_map/ppermute | solution.py:347
  35.8 13.4 %all-to-all-start.1 = ((bf16[16,3,32,128]{3,2,1,0:T(8,128)(2,1)}), bf16[16,3,32,128]{3,2,1,0:T(8,128)(2,1)S(1)}, u32[]{:S(2)}, u32[]{:S(2)}) async-start(bf16[16,3,32,128]{3,2,1,0:T(8,128)(2,1)} %shard_map.92), calls=%async_computation.1 | async-start | bytes 786432 | tf_op jit(solution)/shard_map/all_to_all | solution.py:369
  40.9 13.2 %collective-permute-start.4 = (bf16[4,2,6,32,128]{4,3,2,1,0:T(8,128)(2,1)S(1)}, bf16[4,2,6,32,128]{4,3,2,1,0:T(8,128)(2,1)S(1)}, u32[]{:S(2)}, u32[]{:S(2)}) collective-permute-start(bf16[4,2,6,32,128]{4,3,2,1,0:T(8,128)(2,1)S(1)} %get-tuple-element.59.refs_2_), channel_id=1, source_target_pairs={{0,193},{1,0},{64,1},{65,64},{128,65},{129,128},{192,129},{193,192... | collective-permute-start | bytes 1179656 | tf_op jit(solution)/shard_map/ppermute | solution.py:347
  42.1 14.7 %collective-permute-start.8 = (bf16[4,2,6,32,128]{4,3,2,1,0:T(8,128)(2,1)S(1)}, bf16[4,2,6,32,128]{4,3,2,1,0:T(8,128)(2,1)S(1)}, u32[]{:S(2)}, u32[]{:S(2)}) collective-permute-start(bf16[4,2,6,32,128]{4,3,2,1,0:T(8,128)(2,1)S(1)} %collective-permute-done.5.refs_5_), channel_id=1, source_target_pairs={{0,193},{1,0},{64,1},{65,64},{128,65},{129,128},{192,129},{193,192... | collective-permute-start | bytes 1179656 | tf_op jit(solution)/shard_map/ppermute | solution.py:347
  44.2 13.7 %collective-permute-start.3 = (bf16[4,2,6,32,128]{4,3,2,1,0:T(8,128)(2,1)S(1)}, bf16[4,2,6,32,128]{4,3,2,1,0:T(8,128)(2,1)S(1)}, u32[]{:S(2)}, u32[]{:S(2)}) collective-permute-start(bf16[4,2,6,32,128]{4,3,2,1,0:T(8,128)(2,1)S(1)} %collective-permute-done.2.refs_0_), channel_id=1, source_target_pairs={{0,1},{1,64},{64,65},{65,128},{128,129},{129,192},{192,193},{193,0... | collective-permute-start | bytes 1179656 | tf_op jit(solution)/shard_map/ppermute | solution.py:347
  49.2 9.1 %collective-permute-start.1 = (bf16[8,2,3,32,128]{4,3,2,1,0:T(8,128)(2,1)S(1)}, bf16[8,2,3,32,128]{4,3,2,1,0:T(8,128)(2,1)S(1)}, u32[]{:S(2)}, u32[]{:S(2)}) collective-permute-start(bf16[8,2,3,32,128]{4,3,2,1,0:T(8,128)(2,1)S(1)} %bitcast.4), channel_id=1, source_target_pairs={{0,8},{8,0},{1,9},{9,1},{2,10},{10,2},{3,11},{11,3},{4,12},{12,4},... | collective-permute-start | bytes 1179656 | tf_op jit(solution)/shard_map/ppermute | solution.py:351
  54.1 12.9 %collective-permute-start.6 = (bf16[4,2,6,32,128]{4,3,2,1,0:T(8,128)(2,1)S(1)}, bf16[4,2,6,32,128]{4,3,2,1,0:T(8,128)(2,1)S(1)}, u32[]{:S(2)}, u32[]{:S(2)}) collective-permute-start(bf16[4,2,6,32,128]{4,3,2,1,0:T(8,128)(2,1)S(1)} %collective-permute-done.refs_1_), channel_id=1, source_target_pairs={{0,1},{1,64},{64,65},{65,128},{128,129},{129,192},{192,193},{193,0... | collective-permute-start | bytes 1179656 | tf_op jit(solution)/shard_map/ppermute | solution.py:347
  54.2 12.9 %collective-permute-start.7 = (bf16[4,2,6,32,128]{4,3,2,1,0:T(8,128)(2,1)S(1)}, bf16[4,2,6,32,128]{4,3,2,1,0:T(8,128)(2,1)S(1)}, u32[]{:S(2)}, u32[]{:S(2)}) collective-permute-start(bf16[4,2,6,32,128]{4,3,2,1,0:T(8,128)(2,1)S(1)} %collective-permute-done.4.refs_4_), channel_id=1, source_target_pairs={{0,193},{1,0},{64,1},{65,64},{128,65},{129,128},{192,129},{193,192... | collective-permute-start | bytes 1179656 | tf_op jit(solution)/shard_map/ppermute | solution.py:347
  56.8 19.9 %collective-permute-start.10 = (bf16[4,2,6,32,128]{4,3,2,1,0:T(8,128)(2,1)S(1)}, bf16[4,2,6,32,128]{4,3,2,1,0:T(8,128)(2,1)S(1)}, u32[]{:S(2)}, u32[]{:S(2)}) collective-permute-start(bf16[4,2,6,32,128]{4,3,2,1,0:T(8,128)(2,1)S(1)} %collective-permute-done.8.refs_3_), channel_id=1, source_target_pairs={{0,193},{1,0},{64,1},{65,64},{128,65},{129,128},{192,129},{193,192... | collective-permute-start | bytes 1179656 | tf_op jit(solution)/shard_map/ppermute | solution.py:347
  57.9 18.8 %collective-permute-start.9 = (bf16[4,2,6,32,128]{4,3,2,1,0:T(8,128)(2,1)S(1)}, bf16[4,2,6,32,128]{4,3,2,1,0:T(8,128)(2,1)S(1)}, u32[]{:S(2)}, u32[]{:S(2)}) collective-permute-start(bf16[4,2,6,32,128]{4,3,2,1,0:T(8,128)(2,1)S(1)} %collective-permute-done.3.refs_0_), channel_id=1, source_target_pairs={{0,1},{1,64},{64,65},{65,128},{128,129},{129,192},{192,193},{193,0... | collective-permute-start | bytes 1179656 | tf_op jit(solution)/shard_map/ppermute | solution.py:347
  67.1 12.4 %collective-permute-start.11 = (bf16[4,2,6,32,128]{4,3,2,1,0:T(8,128)(2,1)S(1)}, bf16[4,2,6,32,128]{4,3,2,1,0:T(8,128)(2,1)S(1)}, u32[]{:S(2)}, u32[]{:S(2)}) collective-permute-start(bf16[4,2,6,32,128]{4,3,2,1,0:T(8,128)(2,1)S(1)} %collective-permute-done.6.refs_1_), channel_id=1, source_target_pairs={{0,1},{1,64},{64,65},{65,128},{128,129},{129,192},{192,193},{193,0... | collective-permute-start | bytes 1179656 | tf_op jit(solution)/shard_map/ppermute | solution.py:347
  67.2 15.2 %collective-permute-start.12 = (bf16[4,2,6,32,128]{4,3,2,1,0:T(8,128)(2,1)S(1)}, bf16[4,2,6,32,128]{4,3,2,1,0:T(8,128)(2,1)S(1)}, u32[]{:S(2)}, u32[]{:S(2)}) collective-permute-start(bf16[4,2,6,32,128]{4,3,2,1,0:T(8,128)(2,1)S(1)} %collective-permute-done.7.refs_2_), channel_id=1, source_target_pairs={{0,193},{1,0},{64,1},{65,64},{128,65},{129,128},{192,129},{193,192... | collective-permute-start | bytes 1179656 | tf_op jit(solution)/shard_map/ppermute | solution.py:347
  76.7 12.5 %collective-permute-start.13 = (bf16[4,2,6,32,128]{4,3,2,1,0:T(8,128)(2,1)S(1)}, bf16[4,2,6,32,128]{4,3,2,1,0:T(8,128)(2,1)S(1)}, u32[]{:S(2)}, u32[]{:S(2)}) collective-permute-start(bf16[4,2,6,32,128]{4,3,2,1,0:T(8,128)(2,1)S(1)} %collective-permute-done.9.refs_0_), channel_id=1, source_target_pairs={{0,1},{1,64},{64,65},{65,128},{128,129},{129,192},{192,193},{193,0... | collective-permute-start | bytes 1179656 | tf_op jit(solution)/shard_map/ppermute | solution.py:347
  76.8 13.8 %collective-permute-start.14 = (bf16[4,2,6,32,128]{4,3,2,1,0:T(8,128)(2,1)S(1)}, bf16[4,2,6,32,128]{4,3,2,1,0:T(8,128)(2,1)S(1)}, u32[]{:S(2)}, u32[]{:S(2)}) collective-permute-start(bf16[4,2,6,32,128]{4,3,2,1,0:T(8,128)(2,1)S(1)} %collective-permute-done.10.refs_3_), channel_id=1, source_target_pairs={{0,193},{1,0},{64,1},{65,64},{128,65},{129,128},{192,129},{193,192... | collective-permute-start | bytes 1179656 | tf_op jit(solution)/shard_map/ppermute | solution.py:347
  90.6 10.3 %collective-permute-start.17 = (f32[8,2,4,32,128]{4,3,2,1,0:T(8,128)S(1)}, f32[8,2,4,32,128]{4,3,2,1,0:T(8,128)S(1)}, u32[]{:S(2)}, u32[]{:S(2)}) collective-permute-start(f32[8,2,4,32,128]{4,3,2,1,0:T(8,128)S(1)} %get-tuple-element.50), channel_id=1, source_target_pairs={{0,8},{8,0},{1,9},{9,1},{2,10},{10,2},{3,11},{11,3},{4,12},{12,4},... | collective-permute-start | bytes 3145736 | tf_op jit(solution)/shard_map/ppermute | solution.py:351
  97.5 2.8 %collective-permute-start.15 = (bf16[4,2,6,32,128]{4,3,2,1,0:T(8,128)(2,1)S(1)}, bf16[4,2,6,32,128]{4,3,2,1,0:T(8,128)(2,1)S(1)}, u32[]{:S(2)}, u32[]{:S(2)}) collective-permute-start(bf16[4,2,6,32,128]{4,3,2,1,0:T(8,128)(2,1)S(1)} %collective-permute-done.13.refs_0_), channel_id=1, source_target_pairs={{0,8},{8,0},{1,9},{9,1},{2,10},{10,2},{3,11},{11,3},{4,12},{12,4},... | collective-permute-start | bytes 1179656 | tf_op jit(solution)/shard_map/ppermute | solution.py:351
  97.6 3.3 %collective-permute-start.16 = (bf16[4,2,6,32,128]{4,3,2,1,0:T(8,128)(2,1)S(1)}, bf16[4,2,6,32,128]{4,3,2,1,0:T(8,128)(2,1)S(1)}, u32[]{:S(2)}, u32[]{:S(2)}) collective-permute-start(bf16[4,2,6,32,128]{4,3,2,1,0:T(8,128)(2,1)S(1)} %collective-permute-done.14.refs_1_), channel_id=1, source_target_pairs={{0,8},{8,0},{1,9},{9,1},{2,10},{10,2},{3,11},{11,3},{4,12},{12,4},... | collective-permute-start | bytes 1179656 | tf_op jit(solution)/shard_map/ppermute | solution.py:351
